TPU v7x, 512 devices: a whole 4x4x16 slice. The times are simulated.
512 devices in a mesh: kv: 32 (over z, core), tp: 16 (over y, x).
Axes of the slice: x: 4, y: 4, z: 16, core: 2. Of those that a mesh axis runs over, the one named last changes fastest.
Arguments:
- queries: bfloat16 [4, 8192], replicated, may hold values from -7 to 7
- res_cache: bfloat16 [16384, 2, 8, 512], P(('kv', 'tp')), may hold values from -12.5 to 12.5
- res_count: int32 [512, 4], P(('kv', 'tp')), may hold values from 1 to 16, 32 in all within a row
- move_cache: bfloat16 [16384, 2, 8, 512], P(('kv', 'tp')), may hold values from -12.5 to 12.5
- move_request: int32 [16384], P(('kv', 'tp')), may hold values from 0 to 3
- move_owner: int32 [16384, 1], P(('kv', 'tp')), may hold values from 0 to 31; in each aligned block of 32 rows (0 to 31, 32 to 63, ...) at most 2 rows name the same one
- out_weight: bfloat16 [8192, 16384], P('kv', 'tp'), may hold values from -0.0625 to 0.0625
Outputs:
- mixed: bfloat16 [4, 16384], P(None, 'tp')
- landed_pages: bfloat16 [32768, 2, 8, 512], P(('kv', 'tp'))
- landed_request: int32 [32768], P(('kv', 'tp'))
Inputs may be any that keep to these rules, and one draw needn't show every extreme that they name: `res_count`: each row sums to 32: every resident slot is used, slots filled in request order, every request on every block. `move_owner`: at most 2 of the 32 outgoing pages of one device name one owner.
All inputs are finite; a program needn't handle non-finite values.
Results may differ from a plain program's by a relative error of at most 0.01.
Values may be sent and summed in bfloat16 or wider, within the bound.
No kernel may reach another device: no remote copies, remote signals or barrier semaphores. Data moves between devices by JAX's collectives and lax.ppermute only.
A program may use at most 192 MiB of HBM per device.

v0:
```python
import math

import jax
import jax.numpy as jnp
from jax import lax
from jax.sharding import PartitionSpec as P

HQ = 64
KVH = 4
HD = 128
GROUP = 16
B = 4
PAGE = 8
CAP = 2


NEG = -1e30


def combined_all(part, axis, combine):
    gathered = jax.tree.map(lambda a: lax.all_gather(a, axis), part)

    def take(source):
        return jax.tree.map(lambda a: lax.dynamic_index_in_dim(a, source, 0, False), gathered)

    return lax.fori_loop(
        1, lax.axis_size(axis), lambda source, state: combine(state, take(source)), take(0)
    )


def attend(query_heads, pages, page_request, score_scale):
    page_count = pages.shape[0]
    key_rows = pages[:, 0].reshape(page_count * PAGE, KVH, HD)
    value_rows = pages[:, 1].reshape(page_count * PAGE, KVH, HD)
    token_request = jnp.repeat(page_request, PAGE)
    wanted = (token_request[None, :] == jnp.arange(B, dtype=jnp.int32)[:, None])[:, None, None, :]
    scores = (
        jnp.einsum("bgih,tgh->bgit", query_heads, key_rows, preferred_element_type=jnp.float32)
        * score_scale
    )
    scores = jnp.where(wanted, scores, NEG)
    peak_score = jnp.maximum(jnp.max(scores, axis=-1), NEG)
    weights = jnp.where(wanted, jnp.exp(scores - peak_score[..., None]), 0.0).astype(jnp.bfloat16)
    weight_sum = jnp.sum(weights, axis=-1, dtype=jnp.float32)
    summed = jnp.einsum("bgit,tgh->bgih", weights, value_rows, preferred_element_type=jnp.float32)
    return (peak_score, weight_sum, summed)


def combine(left_part, right_part):
    peak_score = jnp.maximum(left_part[0], right_part[0])
    left_factor = jnp.exp(left_part[0] - peak_score)
    right_factor = jnp.exp(right_part[0] - peak_score)
    weight_sum = left_part[1] * left_factor + right_part[1] * right_factor
    summed = left_part[2] * left_factor[..., None] + right_part[2] * right_factor[..., None]
    return (peak_score, weight_sum, summed)


def local(queries, res_cache, res_count, move_cache, move_request, move_owner, out_weight):
    kv_size = lax.axis_size("kv")
    heads_own = HQ // kv_size
    score_scale = 1.0 / math.sqrt(HD)
    query_heads = queries.reshape(B, KVH, GROUP, HD)
    slot_ends = jnp.cumsum(res_count[0])
    slot_index = jnp.arange(res_cache.shape[0], dtype=jnp.int32)
    slot_request = jnp.sum((slot_index[:, None] >= slot_ends[None, :]).astype(jnp.int32), axis=1)
    owners = move_owner[:, 0]
    places = (owners[:, None] == jnp.arange(kv_size, dtype=jnp.int32)[None, :]).astype(jnp.int32)
    page_rank = jnp.sum(jnp.cumsum(places, axis=0) * places, axis=1) - 1
    slot_target = owners * CAP + page_rank
    outgoing = (
        jnp.zeros((kv_size * CAP,) + move_cache.shape[1:], jnp.bfloat16)
        .at[slot_target]
        .set(move_cache)
    )
    outgoing_ids = jnp.full((kv_size * CAP,), -1, jnp.int32).at[slot_target].set(move_request)
    landed = lax.all_to_all(outgoing, "kv", split_axis=0, concat_axis=0, tiled=True)
    landed_ids = lax.all_to_all(outgoing_ids, "kv", split_axis=0, concat_axis=0, tiled=True)
    running = attend(query_heads, res_cache, slot_request, score_scale)
    running = combine(running, attend(query_heads, landed, landed_ids, score_scale))
    peak_score = running[0].reshape(B, HQ)
    weight_sum = running[1].reshape(B, HQ)
    summed = running[2].reshape(B, HQ, HD)
    peak_score = peak_score.reshape(B, kv_size, heads_own)
    weight_sum = weight_sum.reshape(B, kv_size, heads_own)
    summed = summed.reshape(B, kv_size, heads_own, HD)
    peak_score, weight_sum, summed = (
        lax.all_to_all(peak_score, "kv", split_axis=1, concat_axis=1, tiled=True),
        lax.all_to_all(weight_sum, "kv", split_axis=1, concat_axis=1, tiled=True),
        lax.all_to_all(summed, "kv", split_axis=1, concat_axis=1, tiled=True),
    )
    column_peak = jnp.max(peak_score, axis=1)
    factor = jnp.exp(peak_score - column_peak[:, None, :])
    column_part = (
        column_peak,
        jnp.sum(weight_sum * factor, axis=1),
        jnp.sum(summed * factor[..., None], axis=1),
    )
    column_peak, weight_sum, summed = combined_all(column_part, "tp", combine)
    attended = (summed / weight_sum[..., None]).reshape(B, heads_own * HD).astype(jnp.bfloat16)
    partial_out = jnp.dot(attended, out_weight, preferred_element_type=jnp.float32)
    mixed = lax.psum(partial_out, "kv").astype(jnp.bfloat16)
    return (mixed, landed, landed_ids)


def solution(mesh):
    placed = (
        P(),
        P(("kv", "tp"), None, None, None),
        P(("kv", "tp"), None),
        P(("kv", "tp"), None, None, None),
        P(("kv", "tp")),
        P(("kv", "tp"), None),
        P("kv", "tp"),
    )
    return jax.shard_map(
        local,
        mesh=mesh,
        in_specs=placed,
        out_specs=(P(None, "tp"), P(("kv", "tp"), None, None, None), P(("kv", "tp"))),
        check_vma=False,
    )
```

profile of v0, /device:TPU:1, one launch (start us, length us, event | category | flops | bytes accessed | tf_op | source)
XLA Modules:
  0.0 294.8 jit_solution(53899632717009818)
XLA Ops:
  0.7 0.7 copy-done.6
  1.5 0.2 select_reduce_fusion
  1.7 0.8 scatter_custom_fusion
  2.5 0.7 all_to_all.20
  3.2 16.7 %all-to-all-start = ((s32[32,2,1]{1,2,0:T(1,128)}), s32[32,2,1]{1,2,0:T(1,128)S(1)}, u32[]{:S(2)}, u32[]{:S(2)}) async-start(s32[32,2,1]{1,2,0:T(1,128)} %bitcast.11), calls=%async_computation | async-start | bytes 32768 | tf_op jit(solution)/shard_map/all_to_all | solution.py:77
  20.0 1.1 broadcast_in_dim.76
  21.1 4.4 %scatter_fusion = bf16[64,2,8,512]{3,2,1,0:T(8,128)(2,1)} fusion(bf16[64,2,8,512]{3,2,1,0:T(8,128)(2,1)} %broadcast_in_dim.76, s32[32]{0:T(128)S(1)} %fusion.23, bf16[32,2,8,512]{3,2,1,0:T(8,128)(2,1)S(1)} %copy-done.1), kind=kCustom, calls=%fused_computation.1 | custom fusion | bytes 1572992 | tf_op jit(solution)/shard_map/scatter | solution.py:73
  25.4 6.3 %all-to-all-done = s32[32,2,1]{1,2,0:T(1,128)S(1)} async-done(((s32[32,2,1]{1,2,0:T(1,128)}), s32[32,2,1]{1,2,0:T(1,128)S(1)}, u32[]{:S(2)}, u32[]{:S(2)}) %all-to-all-start) | async-done | bytes 288 | tf_op jit(solution)/shard_map/all_to_all | solution.py:77
  31.7 6.1 %all-to-all-start.1 = ((bf16[64,2,8,512]{3,2,1,0:T(8,128)(2,1)}), bf16[64,2,8,512]{3,2,1,0:T(8,128)(2,1)S(1)}, u32[]{:S(2)}, u32[]{:S(2)}) async-start(bf16[64,2,8,512]{3,2,1,0:T(8,128)(2,1)} %scatter_fusion), calls=%async_computation.1 | async-start | bytes 2097152 | tf_op jit(solution)/shard_map/all_to_all | solution.py:76
  37.8 0.6 copy-done.7
  38.4 0.2 reduce-window.8
  39.1 0.9 fusion.31
  40.0 0.5 broadcast.101
  40.5 0.7 reduce.3
  41.2 0.1 all_to_all.22
  41.4 0.4 copy-done.5
  41.9 51.6 %all-to-all-done.1 = bf16[64,2,8,512]{3,2,1,0:T(8,128)(2,1)S(1)} async-done(((bf16[64,2,8,512]{3,2,1,0:T(8,128)(2,1)}), bf16[64,2,8,512]{3,2,1,0:T(8,128)(2,1)S(1)}, u32[]{:S(2)}, u32[]{:S(2)}) %all-to-all-start.1) | async-done | bytes 1048608 | tf_op jit(solution)/shard_map/all_to_all | solution.py:76
  93.6 0.1 reshape_squeeze.13
  93.7 0.4 fusion.32
  94.1 0.1 copy.56
  94.2 0.2 convert_reduce_fusion
  94.5 0.1 copy.58
  94.6 0.1 copy.52
  94.7 0.5 copy-done.3
  95.2 0.2 convert_reduce_fusion.1
  95.4 0.1 copy.57
  95.5 0.6 multiply_add_fusion
  96.1 4.0 %all-to-all-start.2 = ((f32[4,32,2]{0,2,1:T(2,128)}), f32[4,32,2]{0,2,1:T(2,128)S(1)}, u32[]{:S(2)}, u32[]{:S(2)}) async-start(f32[4,32,2]{0,2,1:T(2,128)} %bitcast.82), calls=%async_computation.2 | async-start | bytes 65536 | tf_op jit(solution)/shard_map/all_to_all | solution.py:87
  100.1 0.9 fusion.9
  101.0 0.1 reshape_squeeze.15
  101.1 11.3 %all-to-all-done.2 = f32[4,32,2]{0,2,1:T(2,128)S(1)} async-done(((f32[4,32,2]{0,2,1:T(2,128)}), f32[4,32,2]{0,2,1:T(2,128)S(1)}, u32[]{:S(2)}, u32[]{:S(2)}) %all-to-all-start.2) | async-done | bytes 1056 | tf_op jit(solution)/shard_map/all_to_all | solution.py:87
  112.4 4.5 %all-to-all-start.3 = ((f32[4,32,2]{0,2,1:T(2,128)}), f32[4,32,2]{0,2,1:T(2,128)S(1)}, u32[]{:S(2)}, u32[]{:S(2)}) async-start(f32[4,32,2]{0,2,1:T(2,128)} %bitcast.81), calls=%async_computation.3 | async-start | bytes 65536 | tf_op jit(solution)/shard_map/all_to_all | solution.py:88
  116.9 0.3 fusion.8
  117.2 0.7 copy.62
  118.0 11.2 %all-to-all-done.3 = f32[4,32,2]{0,2,1:T(2,128)S(1)} async-done(((f32[4,32,2]{0,2,1:T(2,128)}), f32[4,32,2]{0,2,1:T(2,128)S(1)}, u32[]{:S(2)}, u32[]{:S(2)}) %all-to-all-start.3) | async-done | bytes 1056 | tf_op jit(solution)/shard_map/all_to_all | solution.py:88
  129.2 4.5 %all-to-all-start.4 = ((f32[4,32,2,128]{3,2,0,1:T(2,128)}), f32[4,32,2,128]{3,2,0,1:T(2,128)S(1)}, u32[]{:S(2)}, u32[]{:S(2)}) async-start(f32[4,32,2,128]{3,2,0,1:T(2,128)} %copy.62), calls=%async_computation.4 | async-start | bytes 262144 | tf_op jit(solution)/shard_map/all_to_all | solution.py:89
  133.8 0.3 copy.63
  134.1 19.6 %all-gather.4 = f32[16,4,2]{1,2,0:T(2,128)S(1)} all-gather(f32[1,4,2]{1,2,0:T(2,128)S(1)} %bitcast.101), channel_id=3, replica_groups=mesh['kv'=32,'tp'=16] {'tp'}, dimensions={0}, use_global_device_ids=true | all-gather | bytes 544 | tf_op jit(solution)/shard_map/all_gather | solution.py:21
  153.7 17.1 %all-gather.3 = f32[16,4,2]{1,2,0:T(2,128)S(1)} all-gather(f32[1,4,2]{1,2,0:T(2,128)S(1)} %bitcast.100), channel_id=2, replica_groups=mesh['kv'=32,'tp'=16] {'tp'}, dimensions={0}, use_global_device_ids=true | all-gather | bytes 544 | tf_op jit(solution)/shard_map/all_gather | solution.py:21
  170.8 0.2 multiply_reduce_fusion
  171.0 15.9 %all-gather.2 = f32[64,2,128]{2,1,0:T(2,128)S(1)} all-gather(f32[4,2,128]{2,1,0:T(2,128)S(1)} %multiply_reduce_fusion), channel_id=4, replica_groups=mesh['kv'=32,'tp'=16] {'tp'}, dimensions={0}, use_global_device_ids=true | all-gather | bytes 69632 | tf_op jit(solution)/shard_map/all_gather | solution.py:21
  186.9 4.4 %while.19 = (s32[]{:T(128)}, f32[4,2]{0,1:T(2,128)S(1)}, f32[4,2]{0,1:T(2,128)S(1)}, f32[4,2,128]{2,1,0:T(2,128)S(1)}, f32[16,4,2]{1,2,0:T(2,128)S(1)}, /*index=...) while((s32[]{:T(128)}, f32[4,2]{0,1:T(2,128)S(1)}, ...), condition=%wide.region_14.15_spmd, body=%wide.region_13.14_spmd.sunk | while | flops 3125 | bytes 12887 | solution.py:26
  187.0 0.1 copy.105
  187.1 0.1 copy.106
  187.3 0.1 copy.105
  187.6 0.1 copy.105
  187.9 0.1 copy.105
  188.1 0.1 copy.105
  188.2 0.1 copy.106
  188.4 0.1 copy.105
  188.7 0.1 copy.105
  189.0 0.1 copy.105
  189.3 0.1 copy.105
  189.6 0.1 copy.105
  189.9 0.1 copy.105
  190.0 0.1 copy.106
  190.2 0.1 copy.105
  190.3 0.1 copy.106
  190.5 0.1 copy.105
  190.8 0.1 copy.105
  191.1 0.1 copy.105
  191.6 0.2 fusion.19
  191.7 102.1 %psum.7 = bf16[4,1024]{1,0:T(4,128)(2,1)} all-reduce(f32[4,1024]{1,0:T(4,128)S(1)} %fusion.19), channel_id=1, replica_groups=mesh['kv'=32,'tp'=16] {'kv'}, use_global_device_ids=true, to_apply=%region_15.16 | all-reduce | flops 4096 | bytes 24576 | tf_op jit(solution)/shard_map/psum | solution.py:101
  293.8 1.0 copy.121
  (80 shorter events, 3.8 us)
Async XLA Ops:
  0.6 190.9 %copy-start = (bf16[256,1024]{1,0:T(8,128)(2,1)S(1)}, bf16[256,1024]{1,0:T(8,128)(2,1)}, u32[]{:S(2)}) copy-start(bf16[256,1024]{1,0:T(8,128)(2,1)} %param.15) | copy-start | bytes 1572868
  0.6 0.7 copy-start.6
  3.2 28.5 %all-to-all-start = ((s32[32,2,1]{1,2,0:T(1,128)}), s32[32,2,1]{1,2,0:T(1,128)S(1)}, u32[]{:S(2)}, u32[]{:S(2)}) async-start(s32[32,2,1]{1,2,0:T(1,128)} %bitcast.11), calls=%async_computation | async-start | bytes 32768 | tf_op jit(solution)/shard_map/all_to_all | solution.py:77
  20.0 1.1 copy-start.1
  25.4 12.3 %copy-start.4 = (bf16[4,8192]{1,0:T(4,128)(2,1)S(1)}, bf16[4,8192]{1,0:T(4,128)(2,1)}, u32[]{:S(2)}) copy-start(bf16[4,8192]{1,0:T(4,128)(2,1)} %param.9) | copy-start | bytes 196612
  31.7 7.2 %copy-start.2 = (bf16[32,2,8,512]{3,2,1,0:T(8,128)(2,1)S(1)}, bf16[32,2,8,512]{3,2,1,0:T(8,128)(2,1)}, u32[]{:S(2)}) copy-start(bf16[32,2,8,512]{3,2,1,0:T(8,128)(2,1)} %param.10) | copy-start | bytes 1572868
  31.7 61.8 %all-to-all-start.1 = ((bf16[64,2,8,512]{3,2,1,0:T(8,128)(2,1)}), bf16[64,2,8,512]{3,2,1,0:T(8,128)(2,1)S(1)}, u32[]{:S(2)}, u32[]{:S(2)}) async-start(bf16[64,2,8,512]{3,2,1,0:T(8,128)(2,1)} %scatter_fusion), calls=%async_computation.1 | async-start | bytes 2097152 | tf_op jit(solution)/shard_map/all_to_all | solution.py:76
  37.8 0.7 copy-start.7
  41.3 0.5 copy-start.5
  94.2 1.0 copy-start.3
  96.1 16.3 %all-to-all-start.2 = ((f32[4,32,2]{0,2,1:T(2,128)}), f32[4,32,2]{0,2,1:T(2,128)S(1)}, u32[]{:S(2)}, u32[]{:S(2)}) async-start(f32[4,32,2]{0,2,1:T(2,128)} %bitcast.82), calls=%async_computation.2 | async-start | bytes 65536 | tf_op jit(solution)/shard_map/all_to_all | solution.py:87
  101.0 15.9 %copy-start.8 = (f32[4,4,16,128]{3,2,0,1:T(8,128)S(1)}, f32[4,4,16,128]{3,2,0,1:T(8,128)}, u32[]{:S(2)}) copy-start(f32[4,4,16,128]{3,2,0,1:T(8,128)} %fusion.9) | copy-start | bytes 393220
  112.4 16.8 %all-to-all-start.3 = ((f32[4,32,2]{0,2,1:T(2,128)}), f32[4,32,2]{0,2,1:T(2,128)S(1)}, u32[]{:S(2)}, u32[]{:S(2)}) async-start(f32[4,32,2]{0,2,1:T(2,128)} %bitcast.81), calls=%async_computation.3 | async-start | bytes 65536 | tf_op jit(solution)/shard_map/all_to_all | solution.py:88
  129.2 41.6 %all-to-all-start.4 = ((f32[4,32,2,128]{3,2,0,1:T(2,128)}), f32[4,32,2,128]{3,2,0,1:T(2,128)S(1)}, u32[]{:S(2)}, u32[]{:S(2)}) async-start(f32[4,32,2,128]{3,2,0,1:T(2,128)} %copy.62), calls=%async_computation.4 | async-start | bytes 262144 | tf_op jit(solution)/shard_map/all_to_all | solution.py:89
where the time goes:
time: 297 us; the launch traced here: 295 us
  blocking collectives  155 us (52%)
  waiting for transfers between devices  80.3 us (27%)
  starting transfers between devices  35.9 us (12%)
  local copies, waits for them, and re-layouts  16 us (5%)
  other arithmetic  4.37 us (1%)
    psum x1, blocking collectives, local(): mixed = lax.psum(partial_out, 'kv').astype(jnp.bfloat16)  102 us
    all_gather x3, blocking collectives, combined_all(): gathered = jax.tree.map(lambda a: lax.all_gather(a, axis), part)  52.6 us
    all_to_all x1, waiting for transfers between devices, local(): lax.all_to_all(outgoing, 'kv', split_axis=0, concat_axis=0, tiled=True)  51.6 us
    all_to_all x1, starting transfers between devices, local(): lax.all_to_all(outgoing_ids, 'kv', split_axis=0, concat_axis=0, tiled=True)  16.7 us
    all_to_all x1, waiting for transfers between devices, local(): lax.all_to_all(peak_score, 'kv', split_axis=1, concat_axis=1, tiled=True)  11.3 us
    all_to_all x1, waiting for transfers between devices, local(): lax.all_to_all(weight_sum, 'kv', split_axis=1, concat_axis=1, tiled=True)  11.2 us
    all_to_all x1, waiting for transfers between devices, local(): lax.all_to_all(outgoing_ids, 'kv', split_axis=0, concat_axis=0, tiled=True)  6.26 us
    all_to_all x1, starting transfers between devices, local(): lax.all_to_all(outgoing, 'kv', split_axis=0, concat_axis=0, tiled=True)  6.06 us
  transfers between devices with their start and end apart: 5, of which 4 were waited for; matrix products, arithmetic and copies ran while one was open for 4% of the time, Pallas kernels for 0%

commit v1 on v0

v1 whole, which is shorter than its diff:
```python
import math

import jax
import jax.numpy as jnp
from jax import lax
from jax.experimental import pallas as pl
from jax.experimental.pallas import tpu as pltpu
from jax.sharding import PartitionSpec as P

HQ = 64
KVH = 4
HD = 128
GROUP = 16
B = 4
PAGE = 8
CAP = 2
NEG = -1e30

VMEM = pl.BlockSpec(memory_space=pltpu.VMEM)
SMEM = pl.BlockSpec(memory_space=pltpu.SMEM)
F32 = jnp.float32
BF16 = jnp.bfloat16


def iota(shape, dim):
    return lax.broadcasted_iota(jnp.int32, shape, dim)


def round_up(x):
    return (x + jnp.abs(x) * 2.0**-7).astype(BF16).astype(F32)


def token_rows(ref, part):
    pages = ref[:, part].astype(F32)
    return pages.reshape(pages.shape[0] * PAGE, KVH * HD).astype(BF16)


def attend_kernel(q_ref, res_ref, move_ref, count_ref, request_ref, owner_ref, request_row_ref, out_ref):
    rows = GROUP * B
    n_res, n_move = res_ref.shape[0], move_ref.shape[0]
    page = iota((8, n_res * PAGE), 1) // PAGE
    end = jnp.int32(0)
    res_request = jnp.zeros_like(page)
    for b in range(B - 1):
        end = end + count_ref[0, b]
        res_request = res_request + (page >= end).astype(jnp.int32)
    page = iota((8, n_move * PAGE), 1) // PAGE
    move_request = jnp.zeros_like(page)
    for p in range(n_move):
        move_request = jnp.where(page == p, request_ref[p], move_request)
    token_request = jnp.concatenate([res_request, move_request], axis=1)
    wanted = iota((8, token_request.shape[1]), 0) % B == token_request
    wanted = jnp.concatenate([wanted.astype(F32)] * (rows // 8), axis=0) > 0.5

    keys = jnp.concatenate([token_rows(res_ref, 0), token_rows(move_ref, 0)], axis=0)
    values = jnp.concatenate([token_rows(res_ref, 1), token_rows(move_ref, 1)], axis=0)
    q = q_ref[...].astype(F32)

    owner = owner_ref[...]
    column = jnp.sum(
        jnp.where(iota((n_move, n_move), 0) == iota((n_move, n_move), 1), owner, 0), axis=1, keepdims=True
    )
    before = (column == owner) & (iota((n_move, n_move), 0) < iota((n_move, n_move), 1))
    rank = jnp.sum(before.astype(jnp.int32), axis=0, keepdims=True)
    all_rows = out_ref.shape[0] * 8
    named = iota((all_rows, n_move), 0) // 8 == owner
    marks = request_row_ref[...] + 1
    slot_ids = [
        (jnp.sum(jnp.where(named & (rank == r), marks, 0), axis=1, keepdims=True) - 1).astype(F32)
        for r in range(CAP)
    ]

    lane = iota((rows, HD), 1)
    per = rows // 8
    for g in range(KVH):
        heads = [q[:, (g * GROUP + i) * HD : (g * GROUP + i + 1) * HD] for i in range(GROUP)]
        q_rows = jnp.concatenate(heads, axis=0).astype(BF16)
        scores = lax.dot_general(
            q_rows, keys[:, g * HD : (g + 1) * HD], (((1,), (1,)), ((), ())), preferred_element_type=F32
        ) * (1.0 / math.sqrt(HD))
        scores = jnp.where(wanted, scores, NEG)
        shift = round_up(jnp.max(scores, axis=1, keepdims=True))
        weights = jnp.where(wanted, jnp.exp(scores - shift), 0.0).astype(BF16)
        weight_sum = jnp.sum(weights.astype(F32), axis=1, keepdims=True)
        summed = jnp.dot(weights, values[:, g * HD : (g + 1) * HD], preferred_element_type=F32)
        own = slice(g * rows, (g + 1) * rows)
        extra = jnp.where(lane == 0, shift, jnp.where(lane == 1, weight_sum, 0.0))
        for r in range(CAP):
            extra = jnp.where(lane == 2 + r, slot_ids[r][own], extra)
        both = jnp.concatenate([summed.reshape(per, 8, HD), extra.reshape(per, 8, HD)], axis=1)
        out_ref[g * per : (g + 1) * per] = both.astype(BF16)


def pack_kernel(move_ref, owner_ref, out_ref, used_ref):
    n_move, slots = move_ref.shape[0], out_ref.shape[0]
    out_ref[...] = jnp.zeros(out_ref.shape, out_ref.dtype)
    for o in range(slots // CAP):
        used_ref[o] = 0

    def place(p, carry):
        owner = owner_ref[p]
        rank = used_ref[owner]
        used_ref[owner] = rank + 1
        out_ref[owner * CAP + rank] = move_ref[p]
        return carry

    lax.fori_loop(0, n_move, place, 0)


def combined(parts):
    shifts, sums, values = parts[:, 8:, 0:1], parts[:, 8:, 1:2], parts[:, :8, :]
    shift = jnp.max(shifts, axis=0)
    factor = jnp.exp(shifts - shift[None])
    return shift, jnp.sum(sums * factor, axis=0), jnp.sum(values * factor, axis=0)


def column_kernel(parts_ref, out_ref, ids_ref):
    parts = parts_ref[...].astype(F32)
    shift, weight_sum, values = combined(parts)
    lane = iota((8, HD), 1)
    extra = jnp.where(lane == 0, shift, jnp.where(lane == 1, weight_sum, 0.0))
    out_ref[...] = jnp.concatenate([values, extra], axis=0)
    n = parts.shape[0]
    source, place = iota((n, n * CAP), 0), iota((n, n * CAP), 1)
    ids = parts[:, 8, :]
    ids = jnp.where(place % CAP == 0, ids[:, 2:3], ids[:, 3:4])
    ids_ref[...] = jnp.sum(jnp.where(source == place // CAP, ids, 0.0), axis=0, keepdims=True).astype(jnp.int32)


def project_kernel(parts_ref, weight_ref, out_ref):
    _, weight_sum, values = combined(parts_ref[...])
    attended = (values / weight_sum).astype(BF16)
    total = jnp.zeros((8, weight_ref.shape[1]), F32)
    upper = jnp.dot(attended, weight_ref[:HD], preferred_element_type=F32)
    lower = jnp.dot(attended, weight_ref[HD:], preferred_element_type=F32)
    out_ref[...] = (upper[:B] + lower[B:]).astype(out_ref.dtype)


def add_kernel(parts_ref, out_ref):
    out_ref[...] = jnp.sum(parts_ref[...].astype(F32), axis=0).astype(out_ref.dtype)


def local(queries, res_cache, res_count, move_cache, move_request, move_owner, out_weight):
    kv_size = lax.axis_size("kv")
    owners = move_owner.reshape(-1)
    parts = pl.pallas_call(
        attend_kernel,
        out_shape=jax.ShapeDtypeStruct((kv_size, 16, HD), BF16),
        in_specs=[VMEM, VMEM, VMEM, SMEM, SMEM, VMEM, VMEM],
        out_specs=VMEM,
        name="attend",
    )(queries, res_cache, move_cache, res_count, move_request, owners[None, :], move_request[None, :])
    outgoing = pl.pallas_call(
        pack_kernel,
        out_shape=jax.ShapeDtypeStruct((kv_size * CAP,) + move_cache.shape[1:], BF16),
        in_specs=[VMEM, SMEM],
        out_specs=VMEM,
        scratch_shapes=[pltpu.SMEM((kv_size,), jnp.int32)],
        name="pack",
    )(move_cache, owners)
    parts = lax.all_to_all(parts, "kv", split_axis=0, concat_axis=0, tiled=True)
    landed = lax.all_to_all(outgoing, "kv", split_axis=0, concat_axis=0, tiled=True)
    part, landed_ids = pl.pallas_call(
        column_kernel,
        out_shape=(
            jax.ShapeDtypeStruct((16, HD), F32),
            jax.ShapeDtypeStruct((1, kv_size * CAP), jnp.int32),
        ),
        in_specs=[VMEM],
        out_specs=(VMEM, VMEM),
        name="column",
    )(parts)
    columns = lax.all_gather(part, "tp")
    partial_out = pl.pallas_call(
        project_kernel,
        out_shape=jax.ShapeDtypeStruct((B, out_weight.shape[1]), BF16),
        in_specs=[VMEM, VMEM],
        out_specs=VMEM,
        name="project",
    )(columns, out_weight)
    partials = lax.all_gather(partial_out, "kv")
    mixed = pl.pallas_call(
        add_kernel,
        out_shape=jax.ShapeDtypeStruct((B, out_weight.shape[1]), BF16),
        in_specs=[VMEM],
        out_specs=VMEM,
        name="add",
    )(partials)
    return (mixed, landed, landed_ids.reshape(-1))


def solution(mesh):
    placed = (
        P(),
        P(("kv", "tp"), None, None, None),
        P(("kv", "tp"), None),
        P(("kv", "tp"), None, None, None),
        P(("kv", "tp")),
        P(("kv", "tp"), None),
        P("kv", "tp"),
    )
    return jax.shard_map(
        local,
        mesh=mesh,
        in_specs=placed,
        out_specs=(P(None, "tp"), P(("kv", "tp"), None, None, None), P(("kv", "tp"))),
        check_vma=False,
    )
```

time: 297 us -> 121 us (0.41)
  blocking collectives: 155 us -> 71.9 us
  waiting for transfers between devices: 80.3 us -> 13.5 us
  local copies, waits for them, and re-layouts: 16 us -> 1.61 us
  starting transfers between devices: 35.9 us -> 21.9 us
  Pallas kernels: 0 us -> 10.9 us
  other arithmetic: 4.37 us -> 0 us
    psum x1 -> x0, blocking collectives: 102 us -> none  [local(): mixed = lax.psum(partial_out, 'kv').astype(jnp.bfloat16)]
    all_to_all x1, waiting for transfers between devices: 51.6 us -> 0.01 us  [local(): lax.all_to_all(outgoing, 'kv', split_axis=0, concat_axis=0, tiled=True)]
    all_gather x3 -> x2, blocking collectives: 52.6 us -> 71.9 us  [the longest x1 50.2 us: local(): partials = lax.all_gather(partial_out, 'kv')]
    all_to_all x4 -> x1, waiting for transfers between devices: 28.7 us -> 13.5 us  [local(): parts = lax.all_to_all(parts, 'kv', split_axis=0, concat_axis=0, tiled=True)]
    all_to_all x4 -> x1, starting transfers between devices: 29.8 us -> 16.7 us  [local(): parts = lax.all_to_all(parts, 'kv', split_axis=0, concat_axis=0, tiled=True)]
    pallas_call x0 -> x5, Pallas kernels: none -> 10.9 us  [the longest x1 3.11 us: local(): pl.pallas_call(attend_kernel, out_shape=jax.ShapeDtypeStruct((kv_size, 16...]
    scatter x2 -> x0, local copies, waits for them, and re-layouts: 5.16 us -> none  [the longest x1 4.35 us: local(): outgoing = jnp.zeros((kv_size * CAP,) + move_cache.shape[1:], jnp.bfloat1...]
    exp x31 -> x0, local copies, waits for them, and re-layouts: 3.08 us -> none  [the longest x15 1.4 us: combine(): right_factor = jnp.exp(right_part[0] - peak_score)]
  transfers between devices with their start and end apart: 5 -> 2, of which waited for: 4 -> 1; matrix products, arithmetic and copies ran while one was open for 4% -> 0% of each run, Pallas kernels for 0% -> 6%
where the time goes in v1:
time: 121 us
  blocking collectives  71.9 us (59%)
  starting transfers between devices  21.9 us (18%)
  waiting for transfers between devices  13.5 us (11%)
  Pallas kernels  10.9 us (9%)
  local copies, waits for them, and re-layouts  1.61 us (1%)
    all_gather x1, blocking collectives, local(): partials = lax.all_gather(partial_out, 'kv')  50.2 us
    all_gather x1, blocking collectives, local(): columns = lax.all_gather(part, 'tp')  21.7 us
    all_to_all x1, starting transfers between devices, local(): parts = lax.all_to_all(parts, 'kv', split_axis=0, concat_axis=0, tiled=True)  16.7 us
    all_to_all x1, waiting for transfers between devices, local(): parts = lax.all_to_all(parts, 'kv', split_axis=0, concat_axis=0, tiled=True)  13.5 us
    all_to_all x1, starting transfers between devices, local(): lax.all_to_all(outgoing, 'kv', split_axis=0, concat_axis=0, tiled=True)  5.19 us
    pallas_call x1, Pallas kernels, local(): pl.pallas_call(attend_kernel, out_shape=jax.ShapeDtypeStruct((kv_size, 16...  3.11 us
  transfers between devices with their start and end apart: 2, of which 1 were waited for; matrix products, arithmetic and copies ran while one was open for 0% of the time, Pallas kernels for 6%

profile of v1, /device:TPU:1, one launch (start us, length us, event | category | flops | bytes accessed | tf_op | source)
XLA Modules:
  0.0 120.5 jit_solution(12494654487008086636)
XLA Ops:
  0.6 3.1 %attend.1 = bf16[32,16,128]{2,1,0:T(8,128)(2,1)} custom-call(bf16[4,8192]{1,0:T(4,128)(2,1)} %q_ref.1, bf16[32,2,8,512]{3,2,1,0:T(8,128)(2,1)} %res_ref.1, bf16[32,2,8,512]{3,2,1,0:T(8,128)(2,1)} %move_ref.3, s32[1,4]{1,0:T(1,128)} %count_ref.1, s32[32]{0:T(128)} %request_ref.1, s32[1,32]{1,0:T(1,128)} %bitcast.9, s32[1,32]{1,0:T(1,128)} %bitcast.8), custom_call_target="tpu_custom_call" | custom-call | tf_op jit(solution)/shard_map/attend/pallas_call | solution.py:146
  3.7 16.7 %all-to-all-start = ((bf16[32,16,128]{2,1,0:T(8,128)(2,1)}), bf16[32,16,128]{2,1,0:T(8,128)(2,1)S(1)}, u32[]{:S(2)}, u32[]{:S(2)}) async-start(bf16[32,16,128]{2,1,0:T(8,128)(2,1)} %attend.1), calls=%async_computation | async-start | bytes 262144 | tf_op jit(solution)/shard_map/all_to_all | solution.py:161
  20.5 2.4 %pack.1 = bf16[64,2,8,512]{3,2,1,0:T(8,128)(2,1)} custom-call(bf16[32,2,8,512]{3,2,1,0:T(8,128)(2,1)} %move_ref.3, s32[32]{0:T(128)} %bitcast.10), custom_call_target="tpu_custom_call" | custom-call | tf_op jit(solution)/shard_map/pack/pallas_call | solution.py:153
  22.9 13.5 %all-to-all-done.parts_ref = bf16[32,16,128]{2,1,0:T(8,128)(2,1)S(1)} async-done(((bf16[32,16,128]{2,1,0:T(8,128)(2,1)}), bf16[32,16,128]{2,1,0:T(8,128)(2,1)S(1)}, u32[]{:S(2)}, u32[]{:S(2)}) %all-to-all-start) | async-done | bytes 131104 | tf_op jit(solution)/shard_map/all_to_all | solution.py:161
  36.3 0.0 copy-start
  36.3 0.6 copy-done
  37.0 5.2 %all-to-all-start.1 = ((bf16[64,2,8,512]{3,2,1,0:T(8,128)(2,1)}), bf16[64,2,8,512]{3,2,1,0:T(8,128)(2,1)S(1)}, u32[]{:S(2)}, u32[]{:S(2)}) async-start(bf16[64,2,8,512]{3,2,1,0:T(8,128)(2,1)} %pack.1), calls=%async_computation.1 | async-start | bytes 2097152 | tf_op jit(solution)/shard_map/all_to_all | solution.py:162
  42.2 1.7 %column.1 = (f32[16,128]{1,0:T(8,128)}, s32[1,64]{1,0:T(1,128)}) custom-call(bf16[32,16,128]{2,1,0:T(8,128)(2,1)} %copy-done), custom_call_target="tpu_custom_call" | custom-call | tf_op jit(solution)/shard_map/column/pallas_call | solution.py:163
  43.9 21.7 %all-gather = f32[256,128]{1,0:T(8,128)} all-gather(f32[16,128]{1,0:T(8,128)} %get-tuple-element.5), channel_id=2, replica_groups=mesh['kv'=32,'tp'=16] {'tp'}, dimensions={0}, use_global_device_ids=true | all-gather | bytes 139264 | tf_op jit(solution)/shard_map/all_gather | solution.py:173
  65.6 2.1 %project.1 = bf16[4,1024]{1,0:T(4,128)(2,1)} custom-call(f32[16,16,128]{2,1,0:T(8,128)} %bitcast.6, bf16[256,1024]{1,0:T(8,128)(2,1)} %weight_ref.1), custom_call_target="tpu_custom_call" | custom-call | tf_op jit(solution)/shard_map/project/pallas_call | solution.py:174
  67.6 50.2 %all-gather.2.parts_ref = bf16[32,4,1024]{2,1,0:T(4,128)(2,1)} all-gather(bf16[1,4,1024]{2,1,0:T(4,128)(2,1)} %bitcast.7), channel_id=3, replica_groups=mesh['kv'=32,'tp'=16] {'kv'}, dimensions={0}, use_global_device_ids=true | all-gather | bytes 270336 | tf_op jit(solution)/shard_map/all_gather | solution.py:181
  117.9 1.7 %add.1 = bf16[4,1024]{1,0:T(4,128)(2,1)} custom-call(bf16[32,4,1024]{2,1,0:T(4,128)(2,1)} %all-gather.2.parts_ref), custom_call_target="tpu_custom_call" | custom-call | tf_op jit(solution)/shard_map/add/pallas_call | solution.py:182
  119.5 0.0 all-to-all-done.1
  119.5 1.0 copy.11
Async XLA Ops:
  3.7 32.6 %all-to-all-start = ((bf16[32,16,128]{2,1,0:T(8,128)(2,1)}), bf16[32,16,128]{2,1,0:T(8,128)(2,1)S(1)}, u32[]{:S(2)}, u32[]{:S(2)}) async-start(bf16[32,16,128]{2,1,0:T(8,128)(2,1)} %attend.1), calls=%async_computation | async-start | bytes 262144 | tf_op jit(solution)/shard_map/all_to_all | solution.py:161
  36.3 0.6 copy-start
  37.0 82.6 %all-to-all-start.1 = ((bf16[64,2,8,512]{3,2,1,0:T(8,128)(2,1)}), bf16[64,2,8,512]{3,2,1,0:T(8,128)(2,1)S(1)}, u32[]{:S(2)}, u32[]{:S(2)}) async-start(bf16[64,2,8,512]{3,2,1,0:T(8,128)(2,1)} %pack.1), calls=%async_computation.1 | async-start | bytes 2097152 | tf_op jit(solution)/shard_map/all_to_all | solution.py:162

commit v2 on v1

--- a/solution.py
+++ b/solution.py
@@ -14,6 +14,7 @@
 B = 4
 PAGE = 8
 CAP = 2
+CHIPS = 16
 NEG = -1e30
 
 VMEM = pl.BlockSpec(memory_space=pltpu.VMEM)
@@ -91,20 +92,74 @@
         out_ref[g * per : (g + 1) * per] = both.astype(BF16)
 
 
-def pack_kernel(move_ref, owner_ref, out_ref, used_ref):
-    n_move, slots = move_ref.shape[0], out_ref.shape[0]
-    out_ref[...] = jnp.zeros(out_ref.shape, out_ref.dtype)
-    for o in range(slots // CAP):
+def pack_kernel(move_ref, owner_ref, own_ref, other_ref, used_ref):
+    own_ref[...] = jnp.zeros(own_ref.shape, own_ref.dtype)
+    other_ref[...] = jnp.zeros(other_ref.shape, other_ref.dtype)
+    for o in range(used_ref.shape[0]):
         used_ref[o] = 0
+    me = lax.axis_index("kv")
+    chip, core = me // 2, me % 2
 
     def place(p, carry):
         owner = owner_ref[p]
         rank = used_ref[owner]
         used_ref[owner] = rank + 1
-        out_ref[owner * CAP + rank] = move_ref[p]
+        slot = ((owner // 2 - chip) & (CHIPS - 1)) * CAP + rank
+
+        @pl.when(owner % 2 == core)
+        def _():
+            own_ref[slot] = move_ref[p]
+
+        @pl.when(owner % 2 != core)
+        def _():
+            other_ref[slot] = move_ref[p]
+
         return carry
 
-    lax.fori_loop(0, n_move, place, 0)
+    lax.fori_loop(0, move_ref.shape[0], place, 0)
+
+
+UP = (4, 5, 6, 7)
+DOWN = (12, 11, 10, 9)
+NEAR = (0, 1, 2, 3, 15, 14, 13)
+CHUNK = 2 * CAP
+
+
+def merge_kernel(own_ref, got_ref, up_ref, down_ref, far_ref, near_ref):
+    core = lax.axis_index("kv") % 2
+    for ref, distances in ((up_ref, UP), (down_ref, DOWN), (far_ref, (8,)), (near_ref, NEAR)):
+        for n, distance in enumerate(distances):
+            ref[pl.ds(n * CHUNK + core * CAP, CAP)] = own_ref[distance * CAP : (distance + 1) * CAP]
+            ref[pl.ds(n * CHUNK + (1 - core) * CAP, CAP)] = got_ref[distance * CAP : (distance + 1) * CAP]
+
+
+def forward_kernel(near_ref, up_ref, down_ref, after_ref, *out_refs):
+    del after_ref
+    for n in range(3):
+        own, came = slice((n + 1) * CHUNK, (n + 2) * CHUNK), slice((n + 4) * CHUNK, (n + 5) * CHUNK)
+        out_refs[2 * n][:CHUNK] = near_ref[own]
+        out_refs[2 * n][CHUNK:] = up_ref[own]
+        out_refs[2 * n + 1][:CHUNK] = near_ref[came]
+        out_refs[2 * n + 1][CHUNK:] = down_ref[own]
+
+
+def land_kernel(near_ref, up_ref, down_ref, far_ref, *refs):
+    out_ref = refs[-1]
+    chip = lax.axis_index("kv") // 2
+
+    def put(back, pages):
+        source = (chip + back) & (CHIPS - 1)
+        out_ref[pl.ds(source * CHUNK, CHUNK)] = pages
+
+    put(0, near_ref[:CHUNK])
+    put(-4, up_ref[:CHUNK])
+    put(4, down_ref[:CHUNK])
+    put(8, far_ref[...])
+    for n in range(3):
+        put(-n - 1, refs[2 * n][:CHUNK])
+        put(-n - 5, refs[2 * n][CHUNK:])
+        put(n + 1, refs[2 * n + 1][:CHUNK])
+        put(n + 5, refs[2 * n + 1][CHUNK:])
 
 
 def combined(parts):
@@ -119,7 +174,7 @@
     shift, weight_sum, values = combined(parts)
     lane = iota((8, HD), 1)
     extra = jnp.where(lane == 0, shift, jnp.where(lane == 1, weight_sum, 0.0))
-    out_ref[...] = jnp.concatenate([values, extra], axis=0)
+    out_ref[...] = jnp.broadcast_to(jnp.concatenate([values, extra], axis=0)[None], out_ref.shape)
     n = parts.shape[0]
     source, place = iota((n, n * CAP), 0), iota((n, n * CAP), 1)
     ids = parts[:, 8, :]
@@ -136,12 +191,17 @@
     out_ref[...] = (upper[:B] + lower[B:]).astype(out_ref.dtype)
 
 
+def pair_kernel(parts_ref, out_ref):
+    both = jnp.sum(parts_ref[...].astype(F32), axis=0).astype(out_ref.dtype)
+    out_ref[...] = jnp.broadcast_to(both[None], out_ref.shape)
+
+
 def add_kernel(parts_ref, out_ref):
     out_ref[...] = jnp.sum(parts_ref[...].astype(F32), axis=0).astype(out_ref.dtype)
 
 
 def local(queries, res_cache, res_count, move_cache, move_request, move_owner, out_weight):
-    kv_size = lax.axis_size("kv")
+    kv_size, tp_size = lax.axis_size("kv"), lax.axis_size("tp")
     owners = move_owner.reshape(-1)
     parts = pl.pallas_call(
         attend_kernel,
@@ -150,27 +210,43 @@
         out_specs=VMEM,
         name="attend",
     )(queries, res_cache, move_cache, res_count, move_request, owners[None, :], move_request[None, :])
-    outgoing = pl.pallas_call(
+    page = move_cache.shape[1:]
+
+    def pages(n):
+        return jax.ShapeDtypeStruct((n,) + page, BF16)
+
+    def shift(x, chips):
+        return lax.ppermute(x, "kv", [(i, (i + 2 * chips) % kv_size) for i in range(kv_size)])
+
+    own, other = pl.pallas_call(
         pack_kernel,
-        out_shape=jax.ShapeDtypeStruct((kv_size * CAP,) + move_cache.shape[1:], BF16),
+        out_shape=(pages(CHIPS * CAP), pages(CHIPS * CAP)),
         in_specs=[VMEM, SMEM],
-        out_specs=VMEM,
+        out_specs=(VMEM, VMEM),
         scratch_shapes=[pltpu.SMEM((kv_size,), jnp.int32)],
         name="pack",
     )(move_cache, owners)
+    got = lax.ppermute(other, "kv", [(i, i ^ 1) for i in range(kv_size)])
     parts = lax.all_to_all(parts, "kv", split_axis=0, concat_axis=0, tiled=True)
-    landed = lax.all_to_all(outgoing, "kv", split_axis=0, concat_axis=0, tiled=True)
+    up, down, far, near = pl.pallas_call(
+        merge_kernel,
+        out_shape=(pages(16), pages(16), pages(4), pages(28)),
+        in_specs=[VMEM, VMEM],
+        out_specs=(VMEM, VMEM, VMEM, VMEM),
+        name="merge",
+    )(own, got)
+    up, down, far = shift(up, 4), shift(down, -4), shift(far, 8)
     part, landed_ids = pl.pallas_call(
         column_kernel,
         out_shape=(
-            jax.ShapeDtypeStruct((16, HD), F32),
+            jax.ShapeDtypeStruct((tp_size, 16, HD), F32),
             jax.ShapeDtypeStruct((1, kv_size * CAP), jnp.int32),
         ),
         in_specs=[VMEM],
         out_specs=(VMEM, VMEM),
         name="column",
     )(parts)
-    columns = lax.all_gather(part, "tp")
+    columns = lax.all_to_all(part, "tp", split_axis=0, concat_axis=0, tiled=True)
     partial_out = pl.pallas_call(
         project_kernel,
         out_shape=jax.ShapeDtypeStruct((B, out_weight.shape[1]), BF16),
@@ -178,7 +254,22 @@
         out_specs=VMEM,
         name="project",
     )(columns, out_weight)
-    partials = lax.all_gather(partial_out, "kv")
+    pair = lax.all_gather(partial_out, "kv", axis_index_groups=[[2 * z, 2 * z + 1] for z in range(CHIPS)])
+    chip_out = pl.pallas_call(
+        pair_kernel,
+        out_shape=jax.ShapeDtypeStruct((CHIPS, B, out_weight.shape[1]), BF16),
+        in_specs=[VMEM],
+        out_specs=VMEM,
+        name="pair",
+    )(pair)
+    partials = lax.all_to_all(
+        chip_out,
+        "kv",
+        split_axis=0,
+        concat_axis=0,
+        tiled=True,
+        axis_index_groups=[[2 * z + c for z in range(CHIPS)] for c in range(2)],
+    )
     mixed = pl.pallas_call(
         add_kernel,
         out_shape=jax.ShapeDtypeStruct((B, out_weight.shape[1]), BF16),
@@ -186,6 +277,21 @@
         out_specs=VMEM,
         name="add",
     )(partials)
+    steps = pl.pallas_call(
+        forward_kernel,
+        out_shape=tuple(pages(8) for _ in range(6)),
+        in_specs=[VMEM, VMEM, VMEM, pl.BlockSpec(memory_space=pl.ANY)],
+        out_specs=(VMEM,) * 6,
+        name="forward",
+    )(near, up, down, partial_out)
+    steps = [shift(x, (n // 2 + 1) * (1 - 2 * (n % 2))) for n, x in enumerate(steps)]
+    landed = pl.pallas_call(
+        land_kernel,
+        out_shape=pages(kv_size * CAP),
+        in_specs=[VMEM] * 10,
+        out_specs=VMEM,
+        name="land",
+    )(near, up, down, far, *steps)
     return (mixed, landed, landed_ids.reshape(-1))
 
 

time: 121 us -> 134 us (1.11)
  the two profiles are of different devices: /device:TPU:1 before, /device:TPU:34 now
where the time goes in v2:
time: 134 us; the launch traced here: 133 us
  starting transfers between devices  70.7 us (53%)
  waiting for transfers between devices  35 us (26%)
  Pallas kernels  19.7 us (15%)
  local copies, waits for them, and re-layouts  4.1 us (3%)
  blocking collectives  3.12 us (2%)
    ppermute x9, starting transfers between devices, shift(): lax.ppermute(x, 'kv', [(i, (i + 2 * chips) % kv_size) for i in range(kv_s...  40.8 us
    ppermute x9, waiting for transfers between devices, shift(): lax.ppermute(x, 'kv', [(i, (i + 2 * chips) % kv_size) for i in range(kv_s...  24.2 us
    all_to_all x1, starting transfers between devices, local(): parts = lax.all_to_all(parts, 'kv', split_axis=0, concat_axis=0, tiled=True)  15.4 us
    all_to_all x1, waiting for transfers between devices, local(): parts = lax.all_to_all(parts, 'kv', split_axis=0, concat_axis=0, tiled=True)  10.8 us
    all_to_all x1, starting transfers between devices, local(): lax.all_to_all(part, 'tp', split_axis=0, concat_axis=0, tiled=True)  7.48 us
    all_to_all x1, starting transfers between devices, local(): lax.all_to_all(chip_out, 'kv', split_axis=0, concat_axis=0, tiled=True, a...  5.02 us
    unnamed x28, local copies, waits for them, and re-layouts  4.1 us
    all_gather x1, blocking collectives, local(): lax.all_gather(partial_out, 'kv', axis_index_groups=[[2 * z, 2 * z + 1] f...  3.12 us
  transfers between devices with their start and end apart: 13, of which 5 were waited for; matrix products, arithmetic and copies ran while one was open for 0% of the time, Pallas kernels for 11%

profile of v2, /device:TPU:34, one launch (start us, length us, event | category | flops | bytes accessed | tf_op | source)
XLA Modules:
  0.0 133.4 jit_solution(1628965196754794079)
XLA Ops:
  0.6 3.1 %attend.1 = bf16[32,16,128]{2,1,0:T(8,128)(2,1)} custom-call(bf16[4,8192]{1,0:T(4,128)(2,1)} %q_ref.1, bf16[32,2,8,512]{3,2,1,0:T(8,128)(2,1)} %res_ref.1, bf16[32,2,8,512]{3,2,1,0:T(8,128)(2,1)} %move_ref.3, s32[1,4]{1,0:T(1,128)} %count_ref.1, s32[32]{0:T(128)} %request_ref.1, s32[1,32]{1,0:T(1,128)} %bitcast.7, s32[1,32]{1,0:T(1,128)} %bitcast.6), custom_call_target="tpu_custom_call" | custom-call | tf_op jit(solution)/shard_map/attend/pallas_call | solution.py:206
  3.7 15.4 %all-to-all-start = ((bf16[32,16,128]{2,1,0:T(8,128)(2,1)}), bf16[32,16,128]{2,1,0:T(8,128)(2,1)S(1)}, u32[]{:S(2)}, u32[]{:S(2)}) async-start(bf16[32,16,128]{2,1,0:T(8,128)(2,1)} %attend.1), calls=%async_computation | async-start | bytes 262144 | tf_op jit(solution)/shard_map/all_to_all | solution.py:230
  19.1 2.9 %pack.1 = (bf16[32,2,8,512]{3,2,1,0:T(8,128)(2,1)}, bf16[32,2,8,512]{3,2,1,0:T(8,128)(2,1)}) custom-call(bf16[32,2,8,512]{3,2,1,0:T(8,128)(2,1)} %move_ref.3, s32[32]{0:T(128)} %bitcast.8), custom_call_target="tpu_custom_call" | custom-call | tf_op jit(solution)/shard_map/pack/pallas_call | solution.py:221
  22.0 2.0 %collective-permute-start = (bf16[32,2,8,512]{3,2,1,0:T(8,128)(2,1)}, bf16[32,2,8,512]{3,2,1,0:T(8,128)(2,1)S(1)}, u32[]{:S(2)}, u32[]{:S(2)}) collective-permute-start(bf16[32,2,8,512]{3,2,1,0:T(8,128)(2,1)} %get-tuple-element.19), channel_id=1, source_target_pairs={{0,16},{16,0},{32,48},{48,32},{64,80},{80,64},{96,112},{112,96},{1... | collective-permute-start | bytes 1572872 | tf_op jit(solution)/shard_map/ppermute | solution.py:229
  24.0 10.8 %all-to-all-done.parts_ref = bf16[32,16,128]{2,1,0:T(8,128)(2,1)S(1)} async-done(((bf16[32,16,128]{2,1,0:T(8,128)(2,1)}), bf16[32,16,128]{2,1,0:T(8,128)(2,1)S(1)}, u32[]{:S(2)}, u32[]{:S(2)}) %all-to-all-start) | async-done | bytes 131104 | tf_op jit(solution)/shard_map/all_to_all | solution.py:230
  34.8 0.0 copy-start.4
  34.8 0.6 copy-done.4
  35.5 1.8 %column.1 = (f32[16,16,128]{2,1,0:T(8,128)}, s32[1,64]{1,0:T(1,128)}) custom-call(bf16[32,16,128]{2,1,0:T(8,128)(2,1)} %copy-done.4), custom_call_target="tpu_custom_call" | custom-call | tf_op jit(solution)/shard_map/column/pallas_call | solution.py:239
  37.2 7.5 %all-to-all-start.1 = ((f32[16,16,128]{2,1,0:T(8,128)}), f32[16,16,128]{2,1,0:T(8,128)S(1)}, u32[]{:S(2)}, u32[]{:S(2)}) async-start(f32[16,16,128]{2,1,0:T(8,128)} %get-tuple-element.17), calls=%async_computation.1 | async-start | bytes 262144 | tf_op jit(solution)/shard_map/all_to_all | solution.py:249
  44.7 0.0 collective-permute-done.got_ref
  44.7 0.0 copy-start.2
  44.7 0.8 copy-done.2
  45.5 2.3 %merge.1 = (bf16[16,2,8,512]{3,2,1,0:T(8,128)(2,1)}, bf16[16,2,8,512]{3,2,1,0:T(8,128)(2,1)}, bf16[4,2,8,512]{3,2,1,0:T(8,128)(2,1)}, bf16[28,2,8,512]{3,2,1,0:T(8,128)(2,1)}) custom-call(bf16[32,2,8,512]{3,2,1,0:T(8,128)(2,1)} %get-tuple-element.18.own_ref, bf16[32,2,8,512]{3,2,1,0:T(8,128)(2,1)} %copy-done.2), custom_call_target="tpu_custom_call" | custom-call | tf_op jit(solution)/shard_map/merge/pallas_call | solution.py:231
  47.8 2.6 %collective-permute-start.1 = (bf16[16,2,8,512]{3,2,1,0:T(8,128)(2,1)}, bf16[16,2,8,512]{3,2,1,0:T(8,128)(2,1)S(1)}, u32[]{:S(2)}, u32[]{:S(2)}) collective-permute-start(bf16[16,2,8,512]{3,2,1,0:T(8,128)(2,1)} %get-tuple-element.21), channel_id=1, source_target_pairs={{0,128},{16,144},{32,160},{48,176},{64,192},{80,208},{96,224},{112... | collective-permute-start | bytes 786440 | tf_op jit(solution)/shard_map/ppermute | solution.py:219
  50.4 7.1 %collective-permute-start.2 = (bf16[16,2,8,512]{3,2,1,0:T(8,128)(2,1)}, bf16[16,2,8,512]{3,2,1,0:T(8,128)(2,1)S(1)}, u32[]{:S(2)}, u32[]{:S(2)}) collective-permute-start(bf16[16,2,8,512]{3,2,1,0:T(8,128)(2,1)} %get-tuple-element.22), channel_id=1, source_target_pairs={{0,384},{16,400},{32,416},{48,432},{64,448},{80,464},{96,480},{112... | collective-permute-start | bytes 786440 | tf_op jit(solution)/shard_map/ppermute | solution.py:219
  57.6 0.0 all-to-all-done.1.parts_ref
  57.6 0.0 copy-start.5
  57.6 0.6 copy-done.5
  58.2 2.1 %project.1.after_ref = bf16[4,1024]{1,0:T(4,128)(2,1)} custom-call(f32[16,16,128]{2,1,0:T(8,128)} %copy-done.5, bf16[256,1024]{1,0:T(8,128)(2,1)} %weight_ref.1), custom_call_target="tpu_custom_call" | custom-call | tf_op jit(solution)/shard_map/project/pallas_call | solution.py:250
  60.3 3.1 %all-gather.1.parts_ref = bf16[2,4,1024]{2,1,0:T(4,128)(2,1)} all-gather(bf16[1,4,1024]{2,1,0:T(4,128)(2,1)} %bitcast.5), channel_id=2, replica_groups={{0,16},{32,48},{64,80},{96,112},{128,144},{160,176},{192,208},{224,240}..., dimensions={0}, use_global_device_ids=true | all-gather | bytes 24576 | tf_op jit(solution)/shard_map/all_gather | solution.py:257
  63.4 1.4 %pair.1 = bf16[16,4,1024]{2,1,0:T(4,128)(2,1)} custom-call(bf16[2,4,1024]{2,1,0:T(4,128)(2,1)} %all-gather.1.parts_ref), custom_call_target="tpu_custom_call" | custom-call | tf_op jit(solution)/shard_map/pair/pallas_call | solution.py:258
  64.8 5.0 %all-to-all-start.2 = ((bf16[16,4,1024]{2,1,0:T(4,128)(2,1)}), bf16[16,4,1024]{2,1,0:T(4,128)(2,1)S(1)}, u32[]{:S(2)}, u32[]{:S(2)}) async-start(bf16[16,4,1024]{2,1,0:T(4,128)(2,1)} %pair.1), calls=%async_computation.2 | async-start | bytes 262144 | tf_op jit(solution)/shard_map/all_to_all | solution.py:265
  69.8 4.7 %collective-permute-done.1.up_ref = bf16[16,2,8,512]{3,2,1,0:T(8,128)(2,1)S(1)} collective-permute-done((bf16[16,2,8,512]{3,2,1,0:T(8,128)(2,1)}, bf16[16,2,8,512]{3,2,1,0:T(8,128)(2,1)S(1)}, u32[]{:S(2)}, u32[]{:S(2)}) %collective-permute-start.1) | collective-permute-done | bytes 262176 | tf_op jit(solution)/shard_map/ppermute | solution.py:219
  74.5 0.0 copy-start
  74.5 8.9 %collective-permute-done.2.down_ref = bf16[16,2,8,512]{3,2,1,0:T(8,128)(2,1)S(1)} collective-permute-done((bf16[16,2,8,512]{3,2,1,0:T(8,128)(2,1)}, bf16[16,2,8,512]{3,2,1,0:T(8,128)(2,1)S(1)}, u32[]{:S(2)}, u32[]{:S(2)}) %collective-permute-start.2) | collective-permute-done | bytes 262176 | tf_op jit(solution)/shard_map/ppermute | solution.py:219
  83.4 0.0 copy-start.1
  83.4 0.0 copy-done
  83.4 0.7 copy-done.1
  84.1 0.0 copy-start.13
  84.1 2.1 %forward.1 = (bf16[8,2,8,512]{3,2,1,0:T(8,128)(2,1)}, bf16[8,2,8,512]{3,2,1,0:T(8,128)(2,1)}, bf16[8,2,8,512]{3,2,1,0:T(8,128)(2,1)}, bf16[8,2,8,512]{3,2,1,0:T(...) custom-call(bf16[28,2,8,512]{3,2,1,0:T(8,128)(2,1)} %get-tuple-element.20.near_ref, ...), custom_call_target="tpu_custom_call" | custom-call | tf_op jit(solution)/shard_map/forward/pallas_call | solution.py:280
  86.2 1.9 %collective-permute-start.4 = (bf16[8,2,8,512]{3,2,1,0:T(8,128)(2,1)}, bf16[8,2,8,512]{3,2,1,0:T(8,128)(2,1)S(1)}, u32[]{:S(2)}, u32[]{:S(2)}) collective-permute-start(bf16[8,2,8,512]{3,2,1,0:T(8,128)(2,1)} %get-tuple-element.24), channel_id=1, source_target_pairs={{0,32},{16,48},{32,64},{48,80},{64,96},{80,112},{96,128},{112,144}... | collective-permute-start | bytes 393224 | tf_op jit(solution)/shard_map/ppermute | solution.py:219
  88.1 0.0 copy-done.13
  88.1 4.4 %collective-permute-start.3 = (bf16[4,2,8,512]{3,2,1,0:T(8,128)(2,1)S(1)}, bf16[4,2,8,512]{3,2,1,0:T(8,128)(2,1)S(1)}, u32[]{:S(2)}, u32[]{:S(2)}) collective-permute-start(bf16[4,2,8,512]{3,2,1,0:T(8,128)(2,1)S(1)} %copy-done.13), channel_id=1, source_target_pairs={{0,256},{16,272},{32,288},{48,304},{64,320},{80,336},{96,352},{112... | collective-permute-start | bytes 196616 | tf_op jit(solution)/shard_map/ppermute | solution.py:219
  92.6 6.7 %collective-permute-start.5 = (bf16[8,2,8,512]{3,2,1,0:T(8,128)(2,1)}, bf16[8,2,8,512]{3,2,1,0:T(8,128)(2,1)S(1)}, u32[]{:S(2)}, u32[]{:S(2)}) collective-permute-start(bf16[8,2,8,512]{3,2,1,0:T(8,128)(2,1)} %get-tuple-element.25), channel_id=1, source_target_pairs={{0,480},{16,496},{32,0},{48,16},{64,32},{80,48},{96,64},{112,80},{... | collective-permute-start | bytes 393224 | tf_op jit(solution)/shard_map/ppermute | solution.py:219
  99.3 5.4 %collective-permute-start.6 = (bf16[8,2,8,512]{3,2,1,0:T(8,128)(2,1)}, bf16[8,2,8,512]{3,2,1,0:T(8,128)(2,1)S(1)}, u32[]{:S(2)}, u32[]{:S(2)}) collective-permute-start(bf16[8,2,8,512]{3,2,1,0:T(8,128)(2,1)} %get-tuple-element.26), channel_id=1, source_target_pairs={{0,64},{16,80},{32,96},{48,112},{64,128},{80,144},{96,160},{112,17... | collective-permute-start | bytes 393224 | tf_op jit(solution)/shard_map/ppermute | solution.py:219
  104.8 2.5 %collective-permute-start.7 = (bf16[8,2,8,512]{3,2,1,0:T(8,128)(2,1)}, bf16[8,2,8,512]{3,2,1,0:T(8,128)(2,1)S(1)}, u32[]{:S(2)}, u32[]{:S(2)}) collective-permute-start(bf16[8,2,8,512]{3,2,1,0:T(8,128)(2,1)} %get-tuple-element.27), channel_id=1, source_target_pairs={{0,448},{16,464},{32,480},{48,496},{64,0},{80,16},{96,32},{112,48}... | collective-permute-start | bytes 393224 | tf_op jit(solution)/shard_map/ppermute | solution.py:219
  107.3 0.0 collective-permute-done.3.far_ref
  107.3 0.0 copy-start.12
  107.3 8.1 %collective-permute-start.8 = (bf16[8,2,8,512]{3,2,1,0:T(8,128)(2,1)}, bf16[8,2,8,512]{3,2,1,0:T(8,128)(2,1)S(1)}, u32[]{:S(2)}, u32[]{:S(2)}) collective-permute-start(bf16[8,2,8,512]{3,2,1,0:T(8,128)(2,1)} %get-tuple-element.28), channel_id=1, source_target_pairs={{0,96},{16,112},{32,128},{48,144},{64,160},{80,176},{96,192},{112,... | collective-permute-start | bytes 393224 | tf_op jit(solution)/shard_map/ppermute | solution.py:219
  115.4 0.0 collective-permute-done.4.refs_0_
  115.4 0.0 copy-start.6
  115.4 1.9 %collective-permute-start.9 = (bf16[8,2,8,512]{3,2,1,0:T(8,128)(2,1)}, bf16[8,2,8,512]{3,2,1,0:T(8,128)(2,1)S(1)}, u32[]{:S(2)}, u32[]{:S(2)}) collective-permute-start(bf16[8,2,8,512]{3,2,1,0:T(8,128)(2,1)} %get-tuple-element.29), channel_id=1, source_target_pairs={{0,416},{16,432},{32,448},{48,464},{64,480},{80,496},{96,0},{112,1... | collective-permute-start | bytes 393224 | tf_op jit(solution)/shard_map/ppermute | solution.py:219
  117.4 0.0 collective-permute-done.5.refs_1_
  117.4 0.0 copy-start.7
  117.4 0.0 collective-permute-done.6.refs_2_
  117.4 0.0 copy-start.8
  117.4 0.0 collective-permute-done.7.refs_3_
  117.4 0.0 copy-start.9
  117.4 2.2 %collective-permute-done.8.refs_4_ = bf16[8,2,8,512]{3,2,1,0:T(8,128)(2,1)S(1)} collective-permute-done((bf16[8,2,8,512]{3,2,1,0:T(8,128)(2,1)}, bf16[8,2,8,512]{3,2,1,0:T(8,128)(2,1)S(1)}, u32[]{:S(2)}, u32[]{:S(2)}) %collective-permute-start.8) | collective-permute-done | bytes 131104 | tf_op jit(solution)/shard_map/ppermute | solution.py:219
  119.6 0.0 copy-start.10
  119.6 8.4 %collective-permute-done.9.refs_5_ = bf16[8,2,8,512]{3,2,1,0:T(8,128)(2,1)S(1)} collective-permute-done((bf16[8,2,8,512]{3,2,1,0:T(8,128)(2,1)}, bf16[8,2,8,512]{3,2,1,0:T(8,128)(2,1)S(1)}, u32[]{:S(2)}, u32[]{:S(2)}) %collective-permute-start.9) | collective-permute-done | bytes 131104 | tf_op jit(solution)/shard_map/ppermute | solution.py:219
  128.0 0.0 copy-done.12
  128.0 0.0 copy-done.6
  128.0 0.0 copy-done.7
  128.0 0.0 copy-done.8
  128.0 0.0 copy-done.9
  128.0 0.0 copy-done.10
  128.0 0.0 copy-start.11
  128.0 0.6 copy-done.11
  128.7 2.5 %land.1 = bf16[64,2,8,512]{3,2,1,0:T(8,128)(2,1)} custom-call(bf16[28,2,8,512]{3,2,1,0:T(8,128)(2,1)} %get-tuple-element.20.near_ref, bf16[16,2,8,512]{3,2,1,0:T(8,128)(2,1)} %copy-done, bf16[16,2,8,512]{3,2,1,0:T(8,128)(2,1)} %copy-done.1, bf16[4,2,8,512]{3,2,1,0:T(8,128)(2,1)} %copy-done.12, bf16[8,2,8,512]{3,2,1,0:T(8,128)(2,1)} %copy-done.6, ...), custom_call_target="tpu_custom_call" | custom-call | tf_op jit(solution)/shard_map/land/pallas_call | solution.py:288
  131.2 0.0 all-to-all-done.2.parts_ref
  131.2 0.0 copy-start.3
  131.2 0.6 copy-done.3
  131.8 1.6 %add.1 = bf16[4,1024]{1,0:T(4,128)(2,1)} custom-call(bf16[16,4,1024]{2,1,0:T(4,128)(2,1)} %copy-done.3), custom_call_target="tpu_custom_call" | custom-call | tf_op jit(solution)/shard_map/add/pallas_call | solution.py:273
Async XLA Ops:
  3.7 31.1 %all-to-all-start = ((bf16[32,16,128]{2,1,0:T(8,128)(2,1)}), bf16[32,16,128]{2,1,0:T(8,128)(2,1)S(1)}, u32[]{:S(2)}, u32[]{:S(2)}) async-start(bf16[32,16,128]{2,1,0:T(8,128)(2,1)} %attend.1), calls=%async_computation | async-start | bytes 262144 | tf_op jit(solution)/shard_map/all_to_all | solution.py:230
  22.0 22.7 %collective-permute-start = (bf16[32,2,8,512]{3,2,1,0:T(8,128)(2,1)}, bf16[32,2,8,512]{3,2,1,0:T(8,128)(2,1)S(1)}, u32[]{:S(2)}, u32[]{:S(2)}) collective-permute-start(bf16[32,2,8,512]{3,2,1,0:T(8,128)(2,1)} %get-tuple-element.19), channel_id=1, source_target_pairs={{0,16},{16,0},{32,48},{48,32},{64,80},{80,64},{96,112},{112,96},{1... | collective-permute-start | bytes 1572872 | tf_op jit(solution)/shard_map/ppermute | solution.py:229
  34.8 0.6 copy-start.4
  37.2 20.3 %all-to-all-start.1 = ((f32[16,16,128]{2,1,0:T(8,128)}), f32[16,16,128]{2,1,0:T(8,128)S(1)}, u32[]{:S(2)}, u32[]{:S(2)}) async-start(f32[16,16,128]{2,1,0:T(8,128)} %get-tuple-element.17), calls=%async_computation.1 | async-start | bytes 262144 | tf_op jit(solution)/shard_map/all_to_all | solution.py:249
  44.7 0.8 copy-start.2
  47.8 26.7 %collective-permute-start.1 = (bf16[16,2,8,512]{3,2,1,0:T(8,128)(2,1)}, bf16[16,2,8,512]{3,2,1,0:T(8,128)(2,1)S(1)}, u32[]{:S(2)}, u32[]{:S(2)}) collective-permute-start(bf16[16,2,8,512]{3,2,1,0:T(8,128)(2,1)} %get-tuple-element.21), channel_id=1, source_target_pairs={{0,128},{16,144},{32,160},{48,176},{64,192},{80,208},{96,224},{112... | collective-permute-start | bytes 786440 | tf_op jit(solution)/shard_map/ppermute | solution.py:219
  50.4 33.0 %collective-permute-start.2 = (bf16[16,2,8,512]{3,2,1,0:T(8,128)(2,1)}, bf16[16,2,8,512]{3,2,1,0:T(8,128)(2,1)S(1)}, u32[]{:S(2)}, u32[]{:S(2)}) collective-permute-start(bf16[16,2,8,512]{3,2,1,0:T(8,128)(2,1)} %get-tuple-element.22), channel_id=1, source_target_pairs={{0,384},{16,400},{32,416},{48,432},{64,448},{80,464},{96,480},{112... | collective-permute-start | bytes 786440 | tf_op jit(solution)/shard_map/ppermute | solution.py:219
  57.6 0.7 copy-start.5
  64.8 66.4 %all-to-all-start.2 = ((bf16[16,4,1024]{2,1,0:T(4,128)(2,1)}), bf16[16,4,1024]{2,1,0:T(4,128)(2,1)S(1)}, u32[]{:S(2)}, u32[]{:S(2)}) async-start(bf16[16,4,1024]{2,1,0:T(4,128)(2,1)} %pair.1), calls=%async_computation.2 | async-start | bytes 262144 | tf_op jit(solution)/shard_map/all_to_all | solution.py:265
  74.5 8.9 %copy-start = (bf16[16,2,8,512]{3,2,1,0:T(8,128)(2,1)}, bf16[16,2,8,512]{3,2,1,0:T(8,128)(2,1)S(1)}, u32[]{:S(2)}) copy-start(bf16[16,2,8,512]{3,2,1,0:T(8,128)(2,1)S(1)} %collective-permute-done.1.up_ref) | copy-start | bytes 786436
  83.4 0.7 copy-start.1
  84.1 4.0 %copy-start.13 = (bf16[4,2,8,512]{3,2,1,0:T(8,128)(2,1)S(1)}, bf16[4,2,8,512]{3,2,1,0:T(8,128)(2,1)}, u32[]{:S(2)}) copy-start(bf16[4,2,8,512]{3,2,1,0:T(8,128)(2,1)} %get-tuple-element.23) | copy-start | bytes 196612
  86.2 29.2 %collective-permute-start.4 = (bf16[8,2,8,512]{3,2,1,0:T(8,128)(2,1)}, bf16[8,2,8,512]{3,2,1,0:T(8,128)(2,1)S(1)}, u32[]{:S(2)}, u32[]{:S(2)}) collective-permute-start(bf16[8,2,8,512]{3,2,1,0:T(8,128)(2,1)} %get-tuple-element.24), channel_id=1, source_target_pairs={{0,32},{16,48},{32,64},{48,80},{64,96},{80,112},{96,128},{112,144}... | collective-permute-start | bytes 393224 | tf_op jit(solution)/shard_map/ppermute | solution.py:219
  88.1 19.2 %collective-permute-start.3 = (bf16[4,2,8,512]{3,2,1,0:T(8,128)(2,1)S(1)}, bf16[4,2,8,512]{3,2,1,0:T(8,128)(2,1)S(1)}, u32[]{:S(2)}, u32[]{:S(2)}) collective-permute-start(bf16[4,2,8,512]{3,2,1,0:T(8,128)(2,1)S(1)} %copy-done.13), channel_id=1, source_target_pairs={{0,256},{16,272},{32,288},{48,304},{64,320},{80,336},{96,352},{112... | collective-permute-start | bytes 196616 | tf_op jit(solution)/shard_map/ppermute | solution.py:219
  92.6 24.8 %collective-permute-start.5 = (bf16[8,2,8,512]{3,2,1,0:T(8,128)(2,1)}, bf16[8,2,8,512]{3,2,1,0:T(8,128)(2,1)S(1)}, u32[]{:S(2)}, u32[]{:S(2)}) collective-permute-start(bf16[8,2,8,512]{3,2,1,0:T(8,128)(2,1)} %get-tuple-element.25), channel_id=1, source_target_pairs={{0,480},{16,496},{32,0},{48,16},{64,32},{80,48},{96,64},{112,80},{... | collective-permute-start | bytes 393224 | tf_op jit(solution)/shard_map/ppermute | solution.py:219
  99.3 18.1 %collective-permute-start.6 = (bf16[8,2,8,512]{3,2,1,0:T(8,128)(2,1)}, bf16[8,2,8,512]{3,2,1,0:T(8,128)(2,1)S(1)}, u32[]{:S(2)}, u32[]{:S(2)}) collective-permute-start(bf16[8,2,8,512]{3,2,1,0:T(8,128)(2,1)} %get-tuple-element.26), channel_id=1, source_target_pairs={{0,64},{16,80},{32,96},{48,112},{64,128},{80,144},{96,160},{112,17... | collective-permute-start | bytes 393224 | tf_op jit(solution)/shard_map/ppermute | solution.py:219
  104.8 12.6 %collective-permute-start.7 = (bf16[8,2,8,512]{3,2,1,0:T(8,128)(2,1)}, bf16[8,2,8,512]{3,2,1,0:T(8,128)(2,1)S(1)}, u32[]{:S(2)}, u32[]{:S(2)}) collective-permute-start(bf16[8,2,8,512]{3,2,1,0:T(8,128)(2,1)} %get-tuple-element.27), channel_id=1, source_target_pairs={{0,448},{16,464},{32,480},{48,496},{64,0},{80,16},{96,32},{112,48}... | collective-permute-start | bytes 393224 | tf_op jit(solution)/shard_map/ppermute | solution.py:219
  107.3 20.7 %copy-start.12 = (bf16[4,2,8,512]{3,2,1,0:T(8,128)(2,1)}, bf16[4,2,8,512]{3,2,1,0:T(8,128)(2,1)S(1)}, u32[]{:S(2)}) copy-start(bf16[4,2,8,512]{3,2,1,0:T(8,128)(2,1)S(1)} %collective-permute-done.3.far_ref) | copy-start | bytes 196612
  107.3 12.3 %collective-permute-start.8 = (bf16[8,2,8,512]{3,2,1,0:T(8,128)(2,1)}, bf16[8,2,8,512]{3,2,1,0:T(8,128)(2,1)S(1)}, u32[]{:S(2)}, u32[]{:S(2)}) collective-permute-start(bf16[8,2,8,512]{3,2,1,0:T(8,128)(2,1)} %get-tuple-element.28), channel_id=1, source_target_pairs={{0,96},{16,112},{32,128},{48,144},{64,160},{80,176},{96,192},{112,... | collective-permute-start | bytes 393224 | tf_op jit(solution)/shard_map/ppermute | solution.py:219
  115.4 12.5 %copy-start.6 = (bf16[8,2,8,512]{3,2,1,0:T(8,128)(2,1)}, bf16[8,2,8,512]{3,2,1,0:T(8,128)(2,1)S(1)}, u32[]{:S(2)}) copy-start(bf16[8,2,8,512]{3,2,1,0:T(8,128)(2,1)S(1)} %collective-permute-done.4.refs_0_) | copy-start | bytes 393220
  115.4 12.5 %collective-permute-start.9 = (bf16[8,2,8,512]{3,2,1,0:T(8,128)(2,1)}, bf16[8,2,8,512]{3,2,1,0:T(8,128)(2,1)S(1)}, u32[]{:S(2)}, u32[]{:S(2)}) collective-permute-start(bf16[8,2,8,512]{3,2,1,0:T(8,128)(2,1)} %get-tuple-element.29), channel_id=1, source_target_pairs={{0,416},{16,432},{32,448},{48,464},{64,480},{80,496},{96,0},{112,1... | collective-permute-start | bytes 393224 | tf_op jit(solution)/shard_map/ppermute | solution.py:219
  117.4 10.6 %copy-start.7 = (bf16[8,2,8,512]{3,2,1,0:T(8,128)(2,1)}, bf16[8,2,8,512]{3,2,1,0:T(8,128)(2,1)S(1)}, u32[]{:S(2)}) copy-start(bf16[8,2,8,512]{3,2,1,0:T(8,128)(2,1)S(1)} %collective-permute-done.5.refs_1_) | copy-start | bytes 393220
  117.4 10.6 %copy-start.8 = (bf16[8,2,8,512]{3,2,1,0:T(8,128)(2,1)}, bf16[8,2,8,512]{3,2,1,0:T(8,128)(2,1)S(1)}, u32[]{:S(2)}) copy-start(bf16[8,2,8,512]{3,2,1,0:T(8,128)(2,1)S(1)} %collective-permute-done.6.refs_2_) | copy-start | bytes 393220
  117.4 10.6 %copy-start.9 = (bf16[8,2,8,512]{3,2,1,0:T(8,128)(2,1)}, bf16[8,2,8,512]{3,2,1,0:T(8,128)(2,1)S(1)}, u32[]{:S(2)}) copy-start(bf16[8,2,8,512]{3,2,1,0:T(8,128)(2,1)S(1)} %collective-permute-done.7.refs_3_) | copy-start | bytes 393220
  119.6 8.4 %copy-start.10 = (bf16[8,2,8,512]{3,2,1,0:T(8,128)(2,1)}, bf16[8,2,8,512]{3,2,1,0:T(8,128)(2,1)S(1)}, u32[]{:S(2)}) copy-start(bf16[8,2,8,512]{3,2,1,0:T(8,128)(2,1)S(1)} %collective-permute-done.8.refs_4_) | copy-start | bytes 393220
  128.0 0.7 copy-start.11
  131.2 0.7 copy-start.3

commit v3 on v2

--- a/solution.py
+++ b/solution.py
@@ -18,6 +18,7 @@
 NEG = -1e30
 
 VMEM = pl.BlockSpec(memory_space=pltpu.VMEM)
+ANY = pl.BlockSpec(memory_space=pl.ANY)
 SMEM = pl.BlockSpec(memory_space=pltpu.SMEM)
 F32 = jnp.float32
 BF16 = jnp.bfloat16
@@ -92,6 +93,13 @@
         out_ref[g * per : (g + 1) * per] = both.astype(BF16)
 
 
+CHUNK = 8
+HALF = CHUNK // 2
+FAR = 8
+HOME = 4 * FAR
+GIVEN = 4 * (FAR - 1)
+
+
 def pack_kernel(move_ref, owner_ref, own_ref, other_ref, used_ref):
     own_ref[...] = jnp.zeros(own_ref.shape, own_ref.dtype)
     other_ref[...] = jnp.zeros(other_ref.shape, other_ref.dtype)
@@ -104,13 +112,19 @@
         owner = owner_ref[p]
         rank = used_ref[owner]
         used_ref[owner] = rank + 1
-        slot = ((owner // 2 - chip) & (CHIPS - 1)) * CAP + rank
-
-        @pl.when(owner % 2 == core)
+        up = (owner // 2 - chip) & (CHIPS - 1)
+        lands = owner % 2
+        carrier = jnp.where(up == 0, lands, jnp.where(up == FAR, core, (up > FAR).astype(jnp.int32)))
+        distance = jnp.where(up > FAR, CHIPS - up, up)
+        slot = (distance - 1) * 4 + jnp.where(lands == carrier, 0, CAP) + rank
+        home = jnp.where(carrier == core, HOME, GIVEN) + rank
+        slot = jnp.where(up == 0, home, slot)
+
+        @pl.when(carrier == core)
         def _():
             own_ref[slot] = move_ref[p]
 
-        @pl.when(owner % 2 != core)
+        @pl.when(carrier != core)
         def _():
             other_ref[slot] = move_ref[p]
 
@@ -119,47 +133,60 @@
     lax.fori_loop(0, move_ref.shape[0], place, 0)
 
 
-UP = (4, 5, 6, 7)
-DOWN = (12, 11, 10, 9)
-NEAR = (0, 1, 2, 3, 15, 14, 13)
-CHUNK = 2 * CAP
-
-
-def merge_kernel(own_ref, got_ref, up_ref, down_ref, far_ref, near_ref):
+def merge_kernel(own_ref, got_ref, three_ref, six_ref, near_ref):
     core = lax.axis_index("kv") % 2
-    for ref, distances in ((up_ref, UP), (down_ref, DOWN), (far_ref, (8,)), (near_ref, NEAR)):
+    for ref, distances in ((three_ref, (3, 4, 5)), (six_ref, (6, 7)), (near_ref, (1, 2))):
         for n, distance in enumerate(distances):
-            ref[pl.ds(n * CHUNK + core * CAP, CAP)] = own_ref[distance * CAP : (distance + 1) * CAP]
-            ref[pl.ds(n * CHUNK + (1 - core) * CAP, CAP)] = got_ref[distance * CAP : (distance + 1) * CAP]
-
-
-def forward_kernel(near_ref, up_ref, down_ref, after_ref, *out_refs):
+            for end in range(2):
+                source = slice((distance - 1) * 4 + end * CAP, (distance - 1) * 4 + (end + 1) * CAP)
+                base = n * CHUNK + end * HALF
+                ref[pl.ds(base + core * CAP, CAP)] = own_ref[source]
+                ref[pl.ds(base + (1 - core) * CAP, CAP)] = got_ref[source]
+    six_ref[2 * CHUNK :] = own_ref[(FAR - 1) * 4 : FAR * 4]
+
+
+def forward_kernel(near_ref, three_ref, six_ref, after_ref, one_ref, two_ref):
     del after_ref
-    for n in range(3):
-        own, came = slice((n + 1) * CHUNK, (n + 2) * CHUNK), slice((n + 4) * CHUNK, (n + 5) * CHUNK)
-        out_refs[2 * n][:CHUNK] = near_ref[own]
-        out_refs[2 * n][CHUNK:] = up_ref[own]
-        out_refs[2 * n + 1][:CHUNK] = near_ref[came]
-        out_refs[2 * n + 1][CHUNK:] = down_ref[own]
-
-
-def land_kernel(near_ref, up_ref, down_ref, far_ref, *refs):
-    out_ref = refs[-1]
-    chip = lax.axis_index("kv") // 2
-
-    def put(back, pages):
-        source = (chip + back) & (CHIPS - 1)
-        out_ref[pl.ds(source * CHUNK, CHUNK)] = pages
-
-    put(0, near_ref[:CHUNK])
-    put(-4, up_ref[:CHUNK])
-    put(4, down_ref[:CHUNK])
-    put(8, far_ref[...])
-    for n in range(3):
-        put(-n - 1, refs[2 * n][:CHUNK])
-        put(-n - 5, refs[2 * n][CHUNK:])
-        put(n + 1, refs[2 * n + 1][:CHUNK])
-        put(n + 5, refs[2 * n + 1][CHUNK:])
+    for n, ref in enumerate((one_ref, two_ref)):
+        last = CHUNK if n == 0 else HALF
+        ref[:CHUNK] = near_ref[n * CHUNK : (n + 1) * CHUNK]
+        ref[CHUNK : 2 * CHUNK] = three_ref[(n + 1) * CHUNK : (n + 2) * CHUNK]
+        ref[2 * CHUNK :] = six_ref[(n + 1) * CHUNK : (n + 1) * CHUNK + last]
+
+
+def arrived(three_ref, six_ref, one_ref, two_ref):
+    return (
+        (1, one_ref, 0),
+        (2, two_ref, 0),
+        (3, three_ref, 0),
+        (4, one_ref, CHUNK),
+        (5, two_ref, CHUNK),
+        (6, six_ref, 0),
+        (7, one_ref, 2 * CHUNK),
+    )
+
+
+def give_kernel(three_ref, six_ref, one_ref, two_ref, out_ref):
+    for distance, ref, first in arrived(three_ref, six_ref, one_ref, two_ref):
+        out_ref[(distance - 1) * HALF : distance * HALF] = ref[first + HALF : first + CHUNK]
+    out_ref[GIVEN:] = two_ref[2 * CHUNK + CAP :]
+
+
+def land_kernel(own_ref, got_ref, three_ref, six_ref, one_ref, two_ref, taken_ref, out_ref):
+    me = lax.axis_index("kv")
+    chip, core = me // 2, me % 2
+    way = 1 - 2 * core
+
+    def first_row(up):
+        return ((chip + up) & (CHIPS - 1)) * HALF
+
+    out_ref[pl.ds(first_row(0) + core * CAP, CAP)] = own_ref[HOME:]
+    out_ref[pl.ds(first_row(0) + (1 - core) * CAP, CAP)] = got_ref[GIVEN:]
+    out_ref[pl.ds(first_row(FAR) + core * CAP, CAP)] = two_ref[2 * CHUNK : 2 * CHUNK + CAP]
+    out_ref[pl.ds(first_row(FAR) + (1 - core) * CAP, CAP)] = taken_ref[GIVEN:]
+    for distance, ref, first in arrived(three_ref, six_ref, one_ref, two_ref):
+        out_ref[pl.ds(first_row(-way * distance), HALF)] = ref[first : first + HALF]
+        out_ref[pl.ds(first_row(way * distance), HALF)] = taken_ref[(distance - 1) * HALF : distance * HALF]
 
 
 def combined(parts):
@@ -169,7 +196,8 @@
     return shift, jnp.sum(sums * factor, axis=0), jnp.sum(values * factor, axis=0)
 
 
-def column_kernel(parts_ref, out_ref, ids_ref):
+def column_kernel(parts_ref, after_ref, out_ref, ids_ref):
+    del after_ref
     parts = parts_ref[...].astype(F32)
     shift, weight_sum, values = combined(parts)
     lane = iota((8, HD), 1)
@@ -216,36 +244,40 @@
         return jax.ShapeDtypeStruct((n,) + page, BF16)
 
     def shift(x, chips):
-        return lax.ppermute(x, "kv", [(i, (i + 2 * chips) % kv_size) for i in range(kv_size)])
+        pairs = [(i, (i + 2 * chips * (1 - 2 * (i % 2))) % kv_size) for i in range(kv_size)]
+        return lax.ppermute(x, "kv", pairs)
+
+    def swap(x):
+        return lax.ppermute(x, "kv", [(i, i ^ 1) for i in range(kv_size)])
 
     own, other = pl.pallas_call(
         pack_kernel,
-        out_shape=(pages(CHIPS * CAP), pages(CHIPS * CAP)),
+        out_shape=(pages(HOME + CAP), pages(GIVEN + CAP)),
         in_specs=[VMEM, SMEM],
         out_specs=(VMEM, VMEM),
         scratch_shapes=[pltpu.SMEM((kv_size,), jnp.int32)],
         name="pack",
     )(move_cache, owners)
-    got = lax.ppermute(other, "kv", [(i, i ^ 1) for i in range(kv_size)])
+    got = swap(other)
     parts = lax.all_to_all(parts, "kv", split_axis=0, concat_axis=0, tiled=True)
-    up, down, far, near = pl.pallas_call(
+    three, six, near = pl.pallas_call(
         merge_kernel,
-        out_shape=(pages(16), pages(16), pages(4), pages(28)),
+        out_shape=(pages(3 * CHUNK), pages(2 * CHUNK + HALF), pages(2 * CHUNK)),
         in_specs=[VMEM, VMEM],
-        out_specs=(VMEM, VMEM, VMEM, VMEM),
+        out_specs=(VMEM, VMEM, VMEM),
         name="merge",
     )(own, got)
-    up, down, far = shift(up, 4), shift(down, -4), shift(far, 8)
+    six, three = shift(six, 6), shift(three, 3)
     part, landed_ids = pl.pallas_call(
         column_kernel,
         out_shape=(
             jax.ShapeDtypeStruct((tp_size, 16, HD), F32),
             jax.ShapeDtypeStruct((1, kv_size * CAP), jnp.int32),
         ),
-        in_specs=[VMEM],
+        in_specs=[VMEM, ANY],
         out_specs=(VMEM, VMEM),
         name="column",
-    )(parts)
+    )(parts, near)
     columns = lax.all_to_all(part, "tp", split_axis=0, concat_axis=0, tiled=True)
     partial_out = pl.pallas_call(
         project_kernel,
@@ -277,21 +309,29 @@
         out_specs=VMEM,
         name="add",
     )(partials)
-    steps = pl.pallas_call(
+    one, two = pl.pallas_call(
         forward_kernel,
-        out_shape=tuple(pages(8) for _ in range(6)),
-        in_specs=[VMEM, VMEM, VMEM, pl.BlockSpec(memory_space=pl.ANY)],
-        out_specs=(VMEM,) * 6,
+        out_shape=(pages(3 * CHUNK), pages(2 * CHUNK + HALF)),
+        in_specs=[VMEM, VMEM, VMEM, ANY],
+        out_specs=(VMEM, VMEM),
         name="forward",
-    )(near, up, down, partial_out)
-    steps = [shift(x, (n // 2 + 1) * (1 - 2 * (n % 2))) for n, x in enumerate(steps)]
+    )(near, three, six, chip_out)
+    two, one = shift(two, 2), shift(one, 1)
+    give = pl.pallas_call(
+        give_kernel,
+        out_shape=pages(GIVEN + CAP),
+        in_specs=[VMEM] * 4,
+        out_specs=VMEM,
+        name="give",
+    )(three, six, one, two)
+    taken = swap(give)
     landed = pl.pallas_call(
         land_kernel,
         out_shape=pages(kv_size * CAP),
-        in_specs=[VMEM] * 10,
+        in_specs=[VMEM] * 7,
         out_specs=VMEM,
         name="land",
-    )(near, up, down, far, *steps)
+    )(own, got, three, six, one, two, taken)
     return (mixed, landed, landed_ids.reshape(-1))
 
 

time: 134 us -> 112 us (0.84)
  the two profiles are of different devices: /device:TPU:34 before, /device:TPU:1 now
where the time goes in v3:
time: 112 us; the launch traced here: 110 us
  starting transfers between devices  54.8 us (49%)
  Pallas kernels  22.2 us (20%)
  blocking collectives  19 us (17%)
  waiting for transfers between devices  7.44 us (7%)
  local copies, waits for them, and re-layouts  5.8 us (5%)
    ppermute x4, starting transfers between devices, shift(): return lax.ppermute(x, 'kv', pairs)  20.7 us
    ppermute x2, starting transfers between devices, swap(): return lax.ppermute(x, 'kv', [(i, i ^ 1) for i in range(kv_size)])  14.4 us
    all_to_all x1, blocking collectives, local(): lax.all_to_all(part, 'tp', split_axis=0, concat_axis=0, tiled=True)  13.9 us
    all_to_all x1, starting transfers between devices, local(): parts = lax.all_to_all(parts, 'kv', split_axis=0, concat_axis=0, tiled=True)  9.98 us
    all_to_all x1, starting transfers between devices, local(): lax.all_to_all(chip_out, 'kv', split_axis=0, concat_axis=0, tiled=True, a...  9.76 us
    unnamed x16, local copies, waits for them, and re-layouts  5.8 us
    all_gather x1, blocking collectives, local(): lax.all_gather(partial_out, 'kv', axis_index_groups=[[2 * z, 2 * z + 1] f...  5.09 us
    ppermute x4, waiting for transfers between devices, shift(): return lax.ppermute(x, 'kv', pairs)  4.83 us
  transfers between devices with their start and end apart: 8, of which 2 were waited for; matrix products, arithmetic and copies ran while one was open for 0% of the time, Pallas kernels for 13%

profile of v3, /device:TPU:1, one launch (start us, length us, event | category | flops | bytes accessed | tf_op | source)
XLA Modules:
  0.0 109.9 jit_solution(17826957900129955878)
XLA Ops:
  0.6 3.0 %pack.1 = (bf16[34,2,8,512]{3,2,1,0:T(8,128)(2,1)}, bf16[30,2,8,512]{3,2,1,0:T(8,128)(2,1)}) custom-call(bf16[32,2,8,512]{3,2,1,0:T(8,128)(2,1)} %move_ref.3, s32[32]{0:T(128)} %bitcast.7), custom_call_target="tpu_custom_call" | custom-call | tf_op jit(solution)/shard_map/pack/pallas_call | solution.py:253
  3.7 8.8 %collective-permute-start = (bf16[30,2,8,512]{3,2,1,0:T(8,128)(2,1)}, bf16[30,2,8,512]{3,2,1,0:T(8,128)(2,1)S(1)}, u32[]{:S(2)}, u32[]{:S(2)}) collective-permute-start(bf16[30,2,8,512]{3,2,1,0:T(8,128)(2,1)} %get-tuple-element.13), channel_id=1, source_target_pairs={{0,16},{16,0},{32,48},{48,32},{64,80},{80,64},{96,112},{112,96},{1... | collective-permute-start | bytes 1474568 | tf_op jit(solution)/shard_map/ppermute | solution.py:251
  12.5 3.1 %attend.1 = bf16[32,16,128]{2,1,0:T(8,128)(2,1)} custom-call(bf16[4,8192]{1,0:T(4,128)(2,1)} %q_ref.1, bf16[32,2,8,512]{3,2,1,0:T(8,128)(2,1)} %res_ref.1, bf16[32,2,8,512]{3,2,1,0:T(8,128)(2,1)} %move_ref.3, s32[1,4]{1,0:T(1,128)} %count_ref.1, s32[32]{0:T(128)} %request_ref.1, s32[1,32]{1,0:T(1,128)} %bitcast.8, s32[1,32]{1,0:T(1,128)} %bitcast.6), custom_call_target="tpu_custom_call" | custom-call | tf_op jit(solution)/shard_map/attend/pallas_call | solution.py:234
  15.6 10.0 %all-to-all-start = ((bf16[32,16,128]{2,1,0:T(8,128)(2,1)}), bf16[32,16,128]{2,1,0:T(8,128)(2,1)S(1)}, u32[]{:S(2)}, u32[]{:S(2)}) async-start(bf16[32,16,128]{2,1,0:T(8,128)(2,1)} %attend.1), calls=%async_computation | async-start | bytes 262144 | tf_op jit(solution)/shard_map/all_to_all | solution.py:262
  25.6 0.0 collective-permute-done.got_ref
  25.6 0.0 copy-start.2
  25.6 0.8 copy-done.2
  26.4 2.2 %merge.1 = (bf16[24,2,8,512]{3,2,1,0:T(8,128)(2,1)}, bf16[20,2,8,512]{3,2,1,0:T(8,128)(2,1)}, bf16[16,2,8,512]{3,2,1,0:T(8,128)(2,1)}) custom-call(bf16[34,2,8,512]{3,2,1,0:T(8,128)(2,1)} %get-tuple-element.12.own_ref, bf16[30,2,8,512]{3,2,1,0:T(8,128)(2,1)} %copy-done.2), custom_call_target="tpu_custom_call" | custom-call | tf_op jit(solution)/shard_map/merge/pallas_call | solution.py:263
  28.6 6.3 %collective-permute-start.1 = (bf16[24,2,8,512]{3,2,1,0:T(8,128)(2,1)}, bf16[24,2,8,512]{3,2,1,0:T(8,128)(2,1)S(1)}, u32[]{:S(2)}, u32[]{:S(2)}) collective-permute-start(bf16[24,2,8,512]{3,2,1,0:T(8,128)(2,1)} %get-tuple-element.16), channel_id=1, source_target_pairs={{0,96},{16,432},{32,128},{48,464},{64,160},{80,496},{96,192},{112,... | collective-permute-start | bytes 1179656 | tf_op jit(solution)/shard_map/ppermute | solution.py:248
  34.9 7.8 %collective-permute-start.2 = (bf16[20,2,8,512]{3,2,1,0:T(8,128)(2,1)}, bf16[20,2,8,512]{3,2,1,0:T(8,128)(2,1)S(1)}, u32[]{:S(2)}, u32[]{:S(2)}) collective-permute-start(bf16[20,2,8,512]{3,2,1,0:T(8,128)(2,1)} %get-tuple-element.17), channel_id=1, source_target_pairs={{0,192},{16,336},{32,224},{48,368},{64,256},{80,400},{96,288},{112... | collective-permute-start | bytes 983048 | tf_op jit(solution)/shard_map/ppermute | solution.py:248
  42.8 0.0 all-to-all-done.parts_ref
  42.8 0.0 copy-start.5
  42.8 0.6 copy-done.5
  43.5 1.8 %column.1 = (f32[16,16,128]{2,1,0:T(8,128)}, s32[1,64]{1,0:T(1,128)}) custom-call(bf16[32,16,128]{2,1,0:T(8,128)(2,1)} %copy-done.5, bf16[16,2,8,512]{3,2,1,0:T(8,128)(2,1)} %get-tuple-element.14.after_ref.near_ref), custom_call_target="tpu_custom_call" | custom-call | tf_op jit(solution)/shard_map/column/pallas_call | solution.py:271
  45.2 13.9 %all_to_all.15.parts_ref = f32[16,16,128]{2,1,0:T(8,128)} all-to-all(f32[16,16,128]{2,1,0:T(8,128)} %get-tuple-element.15), channel_id=1, replica_groups=mesh['kv'=32,'tp'=16] {'tp'}, dimensions={0} | all-to-all | bytes 262144 | tf_op jit(solution)/shard_map/all_to_all | solution.py:281
  59.1 2.1 %project.1 = bf16[4,1024]{1,0:T(4,128)(2,1)} custom-call(f32[16,16,128]{2,1,0:T(8,128)} %all_to_all.15.parts_ref, bf16[256,1024]{1,0:T(8,128)(2,1)} %weight_ref.1), custom_call_target="tpu_custom_call" | custom-call | tf_op jit(solution)/shard_map/project/pallas_call | solution.py:282
  61.2 5.1 %all-gather.1.parts_ref = bf16[2,4,1024]{2,1,0:T(4,128)(2,1)} all-gather(bf16[1,4,1024]{2,1,0:T(4,128)(2,1)} %bitcast.5), channel_id=2, replica_groups={{0,16},{32,48},{64,80},{96,112},{128,144},{160,176},{192,208},{224,240}..., dimensions={0}, use_global_device_ids=true | all-gather | bytes 24576 | tf_op jit(solution)/shard_map/all_gather | solution.py:289
  66.3 1.4 %pair.1.after_ref = bf16[16,4,1024]{2,1,0:T(4,128)(2,1)} custom-call(bf16[2,4,1024]{2,1,0:T(4,128)(2,1)} %all-gather.1.parts_ref), custom_call_target="tpu_custom_call" | custom-call | tf_op jit(solution)/shard_map/pair/pallas_call | solution.py:290
  67.7 4.8 %collective-permute-done.2.six_ref = bf16[20,2,8,512]{3,2,1,0:T(8,128)(2,1)S(1)} collective-permute-done((bf16[20,2,8,512]{3,2,1,0:T(8,128)(2,1)}, bf16[20,2,8,512]{3,2,1,0:T(8,128)(2,1)S(1)}, u32[]{:S(2)}, u32[]{:S(2)}) %collective-permute-start.2) | collective-permute-done | bytes 327712 | tf_op jit(solution)/shard_map/ppermute | solution.py:248
  72.5 0.0 copy-start.1
  72.5 0.0 collective-permute-done.1.three_ref
  72.5 0.7 copy-done.1
  73.2 0.0 copy-start
  73.2 0.8 copy-done
  74.0 2.0 %forward.1 = (bf16[24,2,8,512]{3,2,1,0:T(8,128)(2,1)}, bf16[20,2,8,512]{3,2,1,0:T(8,128)(2,1)}) custom-call(bf16[16,2,8,512]{3,2,1,0:T(8,128)(2,1)} %get-tuple-element.14.after_ref.near_ref, bf16[24,2,8,512]{3,2,1,0:T(8,128)(2,1)} %copy-done, bf16[20,2,8,512]{3,2,1,0:T(8,128)(2,1)} %copy-done.1, bf16[16,4,1024]{2,1,0:T(4,128)(2,1)} %pair.1.after_ref), custom_call_target="tpu_custom_call" | custom-call | tf_op jit(solution)/shard_map/forward/pallas_call | solution.py:312
  76.0 1.9 %collective-permute-start.3 = (bf16[24,2,8,512]{3,2,1,0:T(8,128)(2,1)}, bf16[24,2,8,512]{3,2,1,0:T(8,128)(2,1)S(1)}, u32[]{:S(2)}, u32[]{:S(2)}) collective-permute-start(bf16[24,2,8,512]{3,2,1,0:T(8,128)(2,1)} %get-tuple-element.18), channel_id=1, source_target_pairs={{0,32},{16,496},{32,64},{48,16},{64,96},{80,48},{96,128},{112,80},... | collective-permute-start | bytes 1179656 | tf_op jit(solution)/shard_map/ppermute | solution.py:248
  77.9 4.6 %collective-permute-start.4 = (bf16[20,2,8,512]{3,2,1,0:T(8,128)(2,1)}, bf16[20,2,8,512]{3,2,1,0:T(8,128)(2,1)S(1)}, u32[]{:S(2)}, u32[]{:S(2)}) collective-permute-start(bf16[20,2,8,512]{3,2,1,0:T(8,128)(2,1)} %get-tuple-element.19), channel_id=1, source_target_pairs={{0,64},{16,464},{32,96},{48,496},{64,128},{80,16},{96,160},{112,48... | collective-permute-start | bytes 983048 | tf_op jit(solution)/shard_map/ppermute | solution.py:248
  82.5 9.8 %all-to-all-start.2 = ((bf16[16,4,1024]{2,1,0:T(4,128)(2,1)}), bf16[16,4,1024]{2,1,0:T(4,128)(2,1)S(1)}, u32[]{:S(2)}, u32[]{:S(2)}) async-start(bf16[16,4,1024]{2,1,0:T(4,128)(2,1)} %pair.1.after_ref), calls=%async_computation.2 | async-start | bytes 262144 | tf_op jit(solution)/shard_map/all_to_all | solution.py:297
  92.2 0.0 collective-permute-done.4.two_ref
  92.3 0.0 copy-start.4
  92.3 0.0 collective-permute-done.3.one_ref
  92.3 0.7 copy-done.4
  93.0 0.0 copy-start.3
  93.0 0.7 copy-done.3
  93.7 2.1 %give.1 = bf16[30,2,8,512]{3,2,1,0:T(8,128)(2,1)} custom-call(bf16[24,2,8,512]{3,2,1,0:T(8,128)(2,1)} %copy-done, bf16[20,2,8,512]{3,2,1,0:T(8,128)(2,1)} %copy-done.1, bf16[24,2,8,512]{3,2,1,0:T(8,128)(2,1)} %copy-done.3, bf16[20,2,8,512]{3,2,1,0:T(8,128)(2,1)} %copy-done.4), custom_call_target="tpu_custom_call" | custom-call | tf_op jit(solution)/shard_map/give/pallas_call | solution.py:320
  95.9 5.6 %collective-permute-start.5 = (bf16[30,2,8,512]{3,2,1,0:T(8,128)(2,1)}, bf16[30,2,8,512]{3,2,1,0:T(8,128)(2,1)S(1)}, u32[]{:S(2)}, u32[]{:S(2)}) collective-permute-start(bf16[30,2,8,512]{3,2,1,0:T(8,128)(2,1)} %give.1), channel_id=1, source_target_pairs={{0,16},{16,0},{32,48},{48,32},{64,80},{80,64},{96,112},{112,96},{1... | collective-permute-start | bytes 1474568 | tf_op jit(solution)/shard_map/ppermute | solution.py:251
  101.5 2.6 %all-to-all-done.2.parts_ref = bf16[16,4,1024]{2,1,0:T(4,128)(2,1)S(1)} async-done(((bf16[16,4,1024]{2,1,0:T(4,128)(2,1)}), bf16[16,4,1024]{2,1,0:T(4,128)(2,1)S(1)}, u32[]{:S(2)}, u32[]{:S(2)}) %all-to-all-start.2) | async-done | bytes 131104 | tf_op jit(solution)/shard_map/all_to_all | solution.py:297
  104.1 0.0 copy-start.6
  104.1 0.6 copy-done.6
  104.7 1.6 %add.1 = bf16[4,1024]{1,0:T(4,128)(2,1)} custom-call(bf16[16,4,1024]{2,1,0:T(4,128)(2,1)} %copy-done.6), custom_call_target="tpu_custom_call" | custom-call | tf_op jit(solution)/shard_map/add/pallas_call | solution.py:305
  106.3 0.0 collective-permute-done.5.taken_ref
  106.3 0.0 copy-start.7
  106.3 0.8 copy-done.7
  107.1 2.8 %land.1 = bf16[64,2,8,512]{3,2,1,0:T(8,128)(2,1)} custom-call(bf16[34,2,8,512]{3,2,1,0:T(8,128)(2,1)} %get-tuple-element.12.own_ref, bf16[30,2,8,512]{3,2,1,0:T(8,128)(2,1)} %copy-done.2, bf16[24,2,8,512]{3,2,1,0:T(8,128)(2,1)} %copy-done, bf16[20,2,8,512]{3,2,1,0:T(8,128)(2,1)} %copy-done.1, bf16[24,2,8,512]{3,2,1,0:T(8,128)(2,1)} %copy-done.3, ...), custom_call_target="tpu_custom_call" | custom-call | tf_op jit(solution)/shard_map/land/pallas_call | solution.py:328
Async XLA Ops:
  3.7 21.9 %collective-permute-start = (bf16[30,2,8,512]{3,2,1,0:T(8,128)(2,1)}, bf16[30,2,8,512]{3,2,1,0:T(8,128)(2,1)S(1)}, u32[]{:S(2)}, u32[]{:S(2)}) collective-permute-start(bf16[30,2,8,512]{3,2,1,0:T(8,128)(2,1)} %get-tuple-element.13), channel_id=1, source_target_pairs={{0,16},{16,0},{32,48},{48,32},{64,80},{80,64},{96,112},{112,96},{1... | collective-permute-start | bytes 1474568 | tf_op jit(solution)/shard_map/ppermute | solution.py:251
  15.6 27.2 %all-to-all-start = ((bf16[32,16,128]{2,1,0:T(8,128)(2,1)}), bf16[32,16,128]{2,1,0:T(8,128)(2,1)S(1)}, u32[]{:S(2)}, u32[]{:S(2)}) async-start(bf16[32,16,128]{2,1,0:T(8,128)(2,1)} %attend.1), calls=%async_computation | async-start | bytes 262144 | tf_op jit(solution)/shard_map/all_to_all | solution.py:262
  25.6 0.8 copy-start.2
  28.6 43.9 %collective-permute-start.1 = (bf16[24,2,8,512]{3,2,1,0:T(8,128)(2,1)}, bf16[24,2,8,512]{3,2,1,0:T(8,128)(2,1)S(1)}, u32[]{:S(2)}, u32[]{:S(2)}) collective-permute-start(bf16[24,2,8,512]{3,2,1,0:T(8,128)(2,1)} %get-tuple-element.16), channel_id=1, source_target_pairs={{0,96},{16,432},{32,128},{48,464},{64,160},{80,496},{96,192},{112,... | collective-permute-start | bytes 1179656 | tf_op jit(solution)/shard_map/ppermute | solution.py:248
  34.9 37.5 %collective-permute-start.2 = (bf16[20,2,8,512]{3,2,1,0:T(8,128)(2,1)}, bf16[20,2,8,512]{3,2,1,0:T(8,128)(2,1)S(1)}, u32[]{:S(2)}, u32[]{:S(2)}) collective-permute-start(bf16[20,2,8,512]{3,2,1,0:T(8,128)(2,1)} %get-tuple-element.17), channel_id=1, source_target_pairs={{0,192},{16,336},{32,224},{48,368},{64,256},{80,400},{96,288},{112... | collective-permute-start | bytes 983048 | tf_op jit(solution)/shard_map/ppermute | solution.py:248
  42.8 0.6 copy-start.5
  72.5 0.7 copy-start.1
  73.2 0.8 copy-start
  76.0 16.3 %collective-permute-start.3 = (bf16[24,2,8,512]{3,2,1,0:T(8,128)(2,1)}, bf16[24,2,8,512]{3,2,1,0:T(8,128)(2,1)S(1)}, u32[]{:S(2)}, u32[]{:S(2)}) collective-permute-start(bf16[24,2,8,512]{3,2,1,0:T(8,128)(2,1)} %get-tuple-element.18), channel_id=1, source_target_pairs={{0,32},{16,496},{32,64},{48,16},{64,96},{80,48},{96,128},{112,80},... | collective-permute-start | bytes 1179656 | tf_op jit(solution)/shard_map/ppermute | solution.py:248
  77.9 14.3 %collective-permute-start.4 = (bf16[20,2,8,512]{3,2,1,0:T(8,128)(2,1)}, bf16[20,2,8,512]{3,2,1,0:T(8,128)(2,1)S(1)}, u32[]{:S(2)}, u32[]{:S(2)}) collective-permute-start(bf16[20,2,8,512]{3,2,1,0:T(8,128)(2,1)} %get-tuple-element.19), channel_id=1, source_target_pairs={{0,64},{16,464},{32,96},{48,496},{64,128},{80,16},{96,160},{112,48... | collective-permute-start | bytes 983048 | tf_op jit(solution)/shard_map/ppermute | solution.py:248
  82.5 21.6 %all-to-all-start.2 = ((bf16[16,4,1024]{2,1,0:T(4,128)(2,1)}), bf16[16,4,1024]{2,1,0:T(4,128)(2,1)S(1)}, u32[]{:S(2)}, u32[]{:S(2)}) async-start(bf16[16,4,1024]{2,1,0:T(4,128)(2,1)} %pair.1.after_ref), calls=%async_computation.2 | async-start | bytes 262144 | tf_op jit(solution)/shard_map/all_to_all | solution.py:297
  92.3 0.7 copy-start.4
  93.0 0.8 copy-start.3
  95.9 10.4 %collective-permute-start.5 = (bf16[30,2,8,512]{3,2,1,0:T(8,128)(2,1)}, bf16[30,2,8,512]{3,2,1,0:T(8,128)(2,1)S(1)}, u32[]{:S(2)}, u32[]{:S(2)}) collective-permute-start(bf16[30,2,8,512]{3,2,1,0:T(8,128)(2,1)} %give.1), channel_id=1, source_target_pairs={{0,16},{16,0},{32,48},{48,32},{64,80},{80,64},{96,112},{112,96},{1... | collective-permute-start | bytes 1474568 | tf_op jit(solution)/shard_map/ppermute | solution.py:251
  104.1 0.7 copy-start.6
  106.3 0.8 copy-start.7

commit v4 on v1

--- a/solution.py
+++ b/solution.py
@@ -14,9 +14,12 @@
 B = 4
 PAGE = 8
 CAP = 2
+CHIPS = 16
 NEG = -1e30
+SMALL = 8 * 2**20
 
 VMEM = pl.BlockSpec(memory_space=pltpu.VMEM)
+ANY = pl.BlockSpec(memory_space=pl.ANY)
 SMEM = pl.BlockSpec(memory_space=pltpu.SMEM)
 F32 = jnp.float32
 BF16 = jnp.bfloat16
@@ -91,20 +94,121 @@
         out_ref[g * per : (g + 1) * per] = both.astype(BF16)
 
 
-def pack_kernel(move_ref, owner_ref, out_ref, used_ref):
-    n_move, slots = move_ref.shape[0], out_ref.shape[0]
-    out_ref[...] = jnp.zeros(out_ref.shape, out_ref.dtype)
-    for o in range(slots // CAP):
+FAR = 8
+QUAD = 4
+HOME = QUAD * FAR
+GIVEN = QUAD * (FAR - 1)
+
+
+def copy_all(copies, sems):
+    running = [pltpu.make_async_copy(a, b, sems.at[n]) for n, (a, b) in enumerate(copies)]
+    for copy in running:
+        copy.start()
+    for copy in running:
+        copy.wait()
+
+
+def quads(ref, first, count=1):
+    return ref.at[pl.ds(first * QUAD, count * QUAD)]
+
+
+def pack_kernel(move_ref, owner_ref, own_ref, other_ref, used_ref):
+    own_ref[...] = jnp.zeros(own_ref.shape, own_ref.dtype)
+    other_ref[...] = jnp.zeros(other_ref.shape, other_ref.dtype)
+    for o in range(used_ref.shape[0]):
         used_ref[o] = 0
+    me = lax.axis_index("kv")
+    chip, core = me // 2, me % 2
 
     def place(p, carry):
         owner = owner_ref[p]
         rank = used_ref[owner]
         used_ref[owner] = rank + 1
-        out_ref[owner * CAP + rank] = move_ref[p]
+        up = (owner // 2 - chip) & (CHIPS - 1)
+        lands = owner % 2
+        carrier = jnp.where(up == 0, lands, jnp.where(up == FAR, core, (up > FAR).astype(jnp.int32)))
+        distance = jnp.where(up > FAR, CHIPS - up, up)
+        slot = (distance - 1) * 4 + jnp.where(lands == carrier, 0, CAP) + rank
+        home = jnp.where(carrier == core, HOME, GIVEN) + rank
+        slot = jnp.where(up == 0, home, slot)
+
+        @pl.when(carrier == core)
+        def _():
+            own_ref[slot] = move_ref[p]
+
+        @pl.when(carrier != core)
+        def _():
+            other_ref[slot] = move_ref[p]
+
         return carry
 
-    lax.fori_loop(0, n_move, place, 0)
+    lax.fori_loop(0, move_ref.shape[0], place, 0)
+
+
+def merge_kernel(own_ref, got_ref, three_ref, six_ref, sems):
+    copy_all(
+        [
+            (quads(own_ref, 5, 3), quads(six_ref, 0, 3)),
+            (quads(got_ref, 5, 2), quads(six_ref, 3, 2)),
+            (quads(own_ref, 2, 3), quads(three_ref, 0, 3)),
+            (quads(got_ref, 2, 3), quads(three_ref, 3, 3)),
+        ],
+        sems,
+    )
+
+
+def forward_kernel(own_ref, got_ref, three_ref, six_ref, after_ref, one_ref, two_ref, sems):
+    del after_ref
+    copies = []
+    for n, ref in enumerate((one_ref, two_ref)):
+        parts = [(own_ref, n), (got_ref, n), (three_ref, 1 + n), (three_ref, 4 + n), (six_ref, 1 + n)]
+        parts += [(six_ref, 4)] if n == 0 else []
+        copies += [(quads(source, first), quads(ref, to)) for to, (source, first) in enumerate(parts)]
+    copy_all(copies, sems)
+
+
+def arrived(three_ref, six_ref, one_ref, two_ref):
+    return (
+        (1, one_ref, 0, 1),
+        (2, two_ref, 0, 1),
+        (3, three_ref, 0, 3),
+        (4, one_ref, 2, 3),
+        (5, two_ref, 2, 3),
+        (6, six_ref, 0, 3),
+        (7, one_ref, 4, 5),
+    )
+
+
+def give_kernel(three_ref, six_ref, one_ref, two_ref, out_ref, sems):
+    core = lax.axis_index("kv") % 2
+    copies = [(two_ref.at[pl.ds(4 * QUAD + CAP, CAP)], out_ref.at[pl.ds(GIVEN, CAP)])]
+    for distance, ref, same, other in arrived(three_ref, six_ref, one_ref, two_ref):
+        for quad, start in ((same, core), (other, 1 - core)):
+            to = out_ref.at[pl.ds((distance - 1) * QUAD + start * CAP, CAP)]
+            copies.append((ref.at[pl.ds(quad * QUAD + CAP, CAP)], to))
+    copy_all(copies, sems)
+
+
+def land_kernel(own_ref, got_ref, three_ref, six_ref, one_ref, two_ref, taken_ref, out_ref, sems):
+    me = lax.axis_index("kv")
+    chip, core = me // 2, me % 2
+    way = 1 - 2 * core
+
+    def rows(up, start):
+        return out_ref.at[pl.ds(((chip + up) & (CHIPS - 1)) * QUAD + start * CAP, CAP)]
+
+    copies = [
+        (own_ref.at[pl.ds(HOME, CAP)], rows(0, core)),
+        (got_ref.at[pl.ds(GIVEN, CAP)], rows(0, 1 - core)),
+        (two_ref.at[pl.ds(4 * QUAD, CAP)], rows(FAR, core)),
+        (taken_ref.at[pl.ds(GIVEN, CAP)], rows(FAR, 1 - core)),
+    ]
+    for distance, ref, same, other in arrived(three_ref, six_ref, one_ref, two_ref):
+        for quad, start in ((same, core), (other, 1 - core)):
+            copies.append((ref.at[pl.ds(quad * QUAD, CAP)], rows(-way * distance, start)))
+        to = out_ref.at[pl.ds(((chip + way * distance) & (CHIPS - 1)) * QUAD, QUAD)]
+        copies.append((quads(taken_ref, distance - 1), to))
+    copy_all(copies, sems)
 
 
 def combined(parts):
@@ -114,12 +218,14 @@
     return shift, jnp.sum(sums * factor, axis=0), jnp.sum(values * factor, axis=0)
 
 
-def column_kernel(parts_ref, out_ref, ids_ref):
+def column_kernel(parts_any, after_ref, out_ref, ids_ref, parts_ref):
+    del after_ref
+    pltpu.sync_copy(parts_any, parts_ref)
     parts = parts_ref[...].astype(F32)
     shift, weight_sum, values = combined(parts)
     lane = iota((8, HD), 1)
     extra = jnp.where(lane == 0, shift, jnp.where(lane == 1, weight_sum, 0.0))
-    out_ref[...] = jnp.concatenate([values, extra], axis=0)
+    out_ref[...] = jnp.broadcast_to(jnp.concatenate([values, extra], axis=0)[None], out_ref.shape)
     n = parts.shape[0]
     source, place = iota((n, n * CAP), 0), iota((n, n * CAP), 1)
     ids = parts[:, 8, :]
@@ -127,21 +233,23 @@
     ids_ref[...] = jnp.sum(jnp.where(source == place // CAP, ids, 0.0), axis=0, keepdims=True).astype(jnp.int32)
 
 
-def project_kernel(parts_ref, weight_ref, out_ref):
+def project_kernel(parts_any, weight_ref, out_ref, parts_ref):
+    pltpu.sync_copy(parts_any, parts_ref)
     _, weight_sum, values = combined(parts_ref[...])
     attended = (values / weight_sum).astype(BF16)
-    total = jnp.zeros((8, weight_ref.shape[1]), F32)
     upper = jnp.dot(attended, weight_ref[:HD], preferred_element_type=F32)
     lower = jnp.dot(attended, weight_ref[HD:], preferred_element_type=F32)
-    out_ref[...] = (upper[:B] + lower[B:]).astype(out_ref.dtype)
-
-
-def add_kernel(parts_ref, out_ref):
+    partial = (upper[:B] + lower[B:]).astype(out_ref.dtype)
+    out_ref[...] = jnp.broadcast_to(partial[None], out_ref.shape)
+
+
+def add_kernel(parts_any, out_ref, parts_ref):
+    pltpu.sync_copy(parts_any, parts_ref)
     out_ref[...] = jnp.sum(parts_ref[...].astype(F32), axis=0).astype(out_ref.dtype)
 
 
 def local(queries, res_cache, res_count, move_cache, move_request, move_owner, out_weight):
-    kv_size = lax.axis_size("kv")
+    kv_size, tp_size = lax.axis_size("kv"), lax.axis_size("tp")
     owners = move_owner.reshape(-1)
     parts = pl.pallas_call(
         attend_kernel,
@@ -150,42 +258,80 @@
         out_specs=VMEM,
         name="attend",
     )(queries, res_cache, move_cache, res_count, move_request, owners[None, :], move_request[None, :])
-    outgoing = pl.pallas_call(
+    page = move_cache.shape[1:]
+
+    def pages(n):
+        return jax.ShapeDtypeStruct((n,) + page, BF16)
+
+    def shift(x, chips):
+        pairs = [(i, (i + 2 * chips * (1 - 2 * (i % 2))) % kv_size) for i in range(kv_size)]
+        return lax.ppermute(x, "kv", pairs)
+
+    def swap(x):
+        return lax.ppermute(x, "kv", [(i, i ^ 1) for i in range(kv_size)])
+
+    own, other = pl.pallas_call(
         pack_kernel,
-        out_shape=jax.ShapeDtypeStruct((kv_size * CAP,) + move_cache.shape[1:], BF16),
+        out_shape=(pages(HOME + CAP), pages(GIVEN + CAP)),
         in_specs=[VMEM, SMEM],
-        out_specs=VMEM,
+        out_specs=(VMEM, VMEM),
         scratch_shapes=[pltpu.SMEM((kv_size,), jnp.int32)],
         name="pack",
     )(move_cache, owners)
+    got = swap(other)
     parts = lax.all_to_all(parts, "kv", split_axis=0, concat_axis=0, tiled=True)
-    landed = lax.all_to_all(outgoing, "kv", split_axis=0, concat_axis=0, tiled=True)
+    def copies(kernel, name, out_pages, count, *args):
+        return pl.pallas_call(
+            kernel,
+            out_shape=tuple(pages(n) for n in out_pages),
+            in_specs=[ANY] * len(args),
+            out_specs=(ANY,) * len(out_pages),
+            scratch_shapes=[pltpu.SemaphoreType.DMA((count,))],
+            compiler_params=pltpu.CompilerParams(vmem_limit_bytes=SMALL),
+            cost_estimate=pl.CostEstimate(flops=0, bytes_accessed=1024, transcendentals=0),
+            name=name,
+        )(*args)
+
+    three, six = copies(merge_kernel, "merge", (6 * QUAD, 5 * QUAD), 4, own, got)
+    six_up, three_up = shift(six, 6), shift(three, 3)
     part, landed_ids = pl.pallas_call(
         column_kernel,
         out_shape=(
-            jax.ShapeDtypeStruct((16, HD), F32),
+            jax.ShapeDtypeStruct((tp_size, 16, HD), F32),
             jax.ShapeDtypeStruct((1, kv_size * CAP), jnp.int32),
         ),
-        in_specs=[VMEM],
+        in_specs=[ANY, ANY],
         out_specs=(VMEM, VMEM),
+        scratch_shapes=[pltpu.VMEM(parts.shape, BF16)],
+        compiler_params=pltpu.CompilerParams(vmem_limit_bytes=SMALL),
         name="column",
-    )(parts)
-    columns = lax.all_gather(part, "tp")
+    )(parts, three)
+    three, six = three_up, six_up
+    columns = lax.all_to_all(part, "tp", split_axis=0, concat_axis=0, tiled=True)
     partial_out = pl.pallas_call(
         project_kernel,
-        out_shape=jax.ShapeDtypeStruct((B, out_weight.shape[1]), BF16),
-        in_specs=[VMEM, VMEM],
+        out_shape=jax.ShapeDtypeStruct((kv_size, B, out_weight.shape[1]), BF16),
+        in_specs=[ANY, VMEM],
         out_specs=VMEM,
+        scratch_shapes=[pltpu.VMEM(columns.shape, F32)],
+        compiler_params=pltpu.CompilerParams(vmem_limit_bytes=SMALL),
         name="project",
     )(columns, out_weight)
-    partials = lax.all_gather(partial_out, "kv")
+    partials = lax.all_to_all(partial_out, "kv", split_axis=0, concat_axis=0, tiled=True)
     mixed = pl.pallas_call(
         add_kernel,
         out_shape=jax.ShapeDtypeStruct((B, out_weight.shape[1]), BF16),
-        in_specs=[VMEM],
+        in_specs=[ANY],
         out_specs=VMEM,
+        scratch_shapes=[pltpu.VMEM(partials.shape, BF16)],
+        compiler_params=pltpu.CompilerParams(vmem_limit_bytes=SMALL),
         name="add",
     )(partials)
+    one, two = copies(forward_kernel, "forward", (6 * QUAD, 5 * QUAD), 11, own, got, three, six, partial_out)
+    two, one = shift(two, 2), shift(one, 1)
+    (give,) = copies(give_kernel, "give", (GIVEN + CAP,), 15, three, six, one, two)
+    taken = swap(give)
+    (landed,) = copies(land_kernel, "land", (kv_size * CAP,), 25, own, got, three, six, one, two, taken)
     return (mixed, landed, landed_ids.reshape(-1))
 
 

time: 121 us -> 120 us (level)
  the two profiles are of different devices: /device:TPU:1 before, /device:TPU:23 now
where the time goes in v4:
time: 120 us; the launch traced here: 119 us
  starting transfers between devices  50.5 us (42%)
  waiting for transfers between devices  29.8 us (25%)
  Pallas kernels  28 us (23%)
  blocking collectives  9.92 us (8%)
    ppermute x4, waiting for transfers between devices, shift(): return lax.ppermute(x, 'kv', pairs)  28.4 us
    pallas_call x4, Pallas kernels, copies(): pl.pallas_call(kernel, out_shape=tuple((pages(n) for n in out_pages)), in...  19 us
    ppermute x4, starting transfers between devices, shift(): return lax.ppermute(x, 'kv', pairs)  18.2 us
    all_to_all x1, starting transfers between devices, local(): parts = lax.all_to_all(parts, 'kv', split_axis=0, concat_axis=0, tiled=True)  15.4 us
    ppermute x2, starting transfers between devices, swap(): return lax.ppermute(x, 'kv', [(i, i ^ 1) for i in range(kv_size)])  10.3 us
    all_to_all x1, blocking collectives, local(): lax.all_to_all(part, 'tp', split_axis=0, concat_axis=0, tiled=True)  9.92 us
    all_to_all x1, starting transfers between devices, local(): lax.all_to_all(partial_out, 'kv', split_axis=0, concat_axis=0, tiled=True)  6.67 us
    pallas_call x1, Pallas kernels, local(): pl.pallas_call(attend_kernel, out_shape=jax.ShapeDtypeStruct((kv_size, 16...  3.17 us
  transfers between devices with their start and end apart: 8, of which 4 were waited for; matrix products, arithmetic and copies ran while one was open for 0% of the time, Pallas kernels for 7%

profile of v4, /device:TPU:23, one launch (start us, length us, event | category | flops | bytes accessed | tf_op | source)
XLA Modules:
  0.0 119.0 jit_solution(4877661878225436577)
XLA Ops:
  0.6 3.1 %pack.1 = (bf16[34,2,8,512]{3,2,1,0:T(8,128)(2,1)}, bf16[30,2,8,512]{3,2,1,0:T(8,128)(2,1)}) custom-call(bf16[32,2,8,512]{3,2,1,0:T(8,128)(2,1)} %move_ref.3, s32[32]{0:T(128)} %bitcast.5), custom_call_target="tpu_custom_call" | custom-call | tf_op jit(solution)/shard_map/pack/pallas_call | solution.py:273
  3.7 2.6 %collective-permute-start = (bf16[30,2,8,512]{3,2,1,0:T(8,128)(2,1)}, bf16[30,2,8,512]{3,2,1,0:T(8,128)(2,1)S(1)}, u32[]{:S(2)}, u32[]{:S(2)}) collective-permute-start(bf16[30,2,8,512]{3,2,1,0:T(8,128)(2,1)} %get-tuple-element.12), channel_id=1, source_target_pairs={{0,16},{16,0},{32,48},{48,32},{64,80},{80,64},{96,112},{112,96},{1... | collective-permute-start | bytes 1474568 | tf_op jit(solution)/shard_map/ppermute | solution.py:271
  6.3 0.0 copy-start
  6.3 3.2 %attend.1 = bf16[32,16,128]{2,1,0:T(8,128)(2,1)} custom-call(bf16[4,8192]{1,0:T(4,128)(2,1)} %q_ref.1, bf16[32,2,8,512]{3,2,1,0:T(8,128)(2,1)} %res_ref.1, bf16[32,2,8,512]{3,2,1,0:T(8,128)(2,1)} %move_ref.3, s32[1,4]{1,0:T(1,128)} %count_ref.1, s32[32]{0:T(128)} %request_ref.1, s32[1,32]{1,0:T(1,128)} %bitcast.6, s32[1,32]{1,0:T(1,128)} %bitcast.4), custom_call_target="tpu_custom_call" | custom-call | tf_op jit(solution)/shard_map/attend/pallas_call | solution.py:254
  9.4 15.4 %all-to-all-start = ((bf16[32,16,128]{2,1,0:T(8,128)(2,1)}), bf16[32,16,128]{2,1,0:T(8,128)(2,1)S(1)}, u32[]{:S(2)}, u32[]{:S(2)}) async-start(bf16[32,16,128]{2,1,0:T(8,128)(2,1)} %attend.1), calls=%async_computation | async-start | bytes 262144 | tf_op jit(solution)/shard_map/all_to_all | solution.py:282
  24.8 0.0 collective-permute-done.got_ref
  24.8 0.0 copy-done
  24.8 1.0 merge.1
  25.8 0.0 copy-start.1
  25.8 6.5 %collective-permute-start.1 = (bf16[24,2,8,512]{3,2,1,0:T(8,128)(2,1)S(1)}, bf16[24,2,8,512]{3,2,1,0:T(8,128)(2,1)S(1)}, u32[]{:S(2)}, u32[]{:S(2)}) collective-permute-start(bf16[24,2,8,512]{3,2,1,0:T(8,128)(2,1)S(1)} %get-tuple-element.13.after_ref), channel_id=1, source_target_pairs={{0,96},{16,432},{32,128},{48,464},{64,160},{80,496},{96,192},{112,... | collective-permute-start | bytes 1179656 | tf_op jit(solution)/shard_map/ppermute | solution.py:268
  32.3 7.8 %collective-permute-start.2 = (bf16[20,2,8,512]{3,2,1,0:T(8,128)(2,1)S(1)}, bf16[20,2,8,512]{3,2,1,0:T(8,128)(2,1)S(1)}, u32[]{:S(2)}, u32[]{:S(2)}) collective-permute-start(bf16[20,2,8,512]{3,2,1,0:T(8,128)(2,1)S(1)} %get-tuple-element.15), channel_id=1, source_target_pairs={{0,192},{16,336},{32,224},{48,368},{64,256},{80,400},{96,288},{112... | collective-permute-start | bytes 983048 | tf_op jit(solution)/shard_map/ppermute | solution.py:268
  40.2 0.5 all-to-all-done.parts_any
  40.7 0.9 column.1
  41.5 9.9 %all_to_all.15.parts_any = f32[16,16,128]{2,1,0:T(8,128)S(1)} all-to-all(f32[16,16,128]{2,1,0:T(8,128)S(1)} %get-tuple-element.14), channel_id=1, replica_groups=mesh['kv'=32,'tp'=16] {'tp'}, dimensions={0} | all-to-all | bytes 262144 | tf_op jit(solution)/shard_map/all_to_all | solution.py:310
  51.4 0.0 copy-done.1
  51.4 1.2 %project.1.after_ref = bf16[32,4,1024]{2,1,0:T(4,128)(2,1)} custom-call(f32[16,16,128]{2,1,0:T(8,128)S(1)} %all_to_all.15.parts_any, bf16[256,1024]{1,0:T(8,128)(2,1)S(1)} %copy-done.1), custom_call_target="tpu_custom_call" | custom-call | tf_op jit(solution)/shard_map/project/pallas_call | solution.py:311
  52.7 6.7 %all-to-all-start.2 = ((bf16[32,4,1024]{2,1,0:T(4,128)(2,1)}), bf16[32,4,1024]{2,1,0:T(4,128)(2,1)S(1)}, u32[]{:S(2)}, u32[]{:S(2)}) async-start(bf16[32,4,1024]{2,1,0:T(4,128)(2,1)} %project.1.after_ref), calls=%async_computation.2 | async-start | bytes 524288 | tf_op jit(solution)/shard_map/all_to_all | solution.py:320
  59.3 17.2 %collective-permute-done.2.six_ref = bf16[20,2,8,512]{3,2,1,0:T(8,128)(2,1)S(1)} collective-permute-done((bf16[20,2,8,512]{3,2,1,0:T(8,128)(2,1)S(1)}, bf16[20,2,8,512]{3,2,1,0:T(8,128)(2,1)S(1)}, u32[]{:S(2)}, u32[]{:S(2)}) %collective-permute-start.2) | collective-permute-done | bytes 327712 | tf_op jit(solution)/shard_map/ppermute | solution.py:268
  76.5 0.0 collective-permute-done.1.three_ref
  76.5 1.0 forward.1
  77.6 1.9 %collective-permute-start.3 = (bf16[24,2,8,512]{3,2,1,0:T(8,128)(2,1)S(1)}, bf16[24,2,8,512]{3,2,1,0:T(8,128)(2,1)S(1)}, u32[]{:S(2)}, u32[]{:S(2)}) collective-permute-start(bf16[24,2,8,512]{3,2,1,0:T(8,128)(2,1)S(1)} %get-tuple-element.16), channel_id=1, source_target_pairs={{0,32},{16,496},{32,64},{48,16},{64,96},{80,48},{96,128},{112,80},... | collective-permute-start | bytes 1179656 | tf_op jit(solution)/shard_map/ppermute | solution.py:268
  79.5 1.9 %collective-permute-start.4 = (bf16[20,2,8,512]{3,2,1,0:T(8,128)(2,1)S(1)}, bf16[20,2,8,512]{3,2,1,0:T(8,128)(2,1)S(1)}, u32[]{:S(2)}, u32[]{:S(2)}) collective-permute-start(bf16[20,2,8,512]{3,2,1,0:T(8,128)(2,1)S(1)} %get-tuple-element.17), channel_id=1, source_target_pairs={{0,64},{16,464},{32,96},{48,496},{64,128},{80,16},{96,160},{112,48... | collective-permute-start | bytes 983048 | tf_op jit(solution)/shard_map/ppermute | solution.py:268
  81.4 11.2 %collective-permute-done.4.two_ref = bf16[20,2,8,512]{3,2,1,0:T(8,128)(2,1)S(1)} collective-permute-done((bf16[20,2,8,512]{3,2,1,0:T(8,128)(2,1)S(1)}, bf16[20,2,8,512]{3,2,1,0:T(8,128)(2,1)S(1)}, u32[]{:S(2)}, u32[]{:S(2)}) %collective-permute-start.4) | collective-permute-done | bytes 327712 | tf_op jit(solution)/shard_map/ppermute | solution.py:268
  92.7 0.0 collective-permute-done.3.one_ref
  92.7 0.8 give.1
  93.5 7.7 %collective-permute-start.5 = (bf16[30,2,8,512]{3,2,1,0:T(8,128)(2,1)S(1)}, bf16[30,2,8,512]{3,2,1,0:T(8,128)(2,1)}, u32[]{:S(2)}, u32[]{:S(2)}) collective-permute-start(bf16[30,2,8,512]{3,2,1,0:T(8,128)(2,1)S(1)} %give.1), channel_id=1, source_target_pairs={{0,16},{16,0},{32,48},{48,32},{64,80},{80,64},{96,112},{112,96},{1... | collective-permute-start | bytes 1474568 | tf_op jit(solution)/shard_map/ppermute | solution.py:271
  101.2 0.0 all-to-all-done.2.parts_any
  101.2 0.7 add.1
  101.9 0.9 collective-permute-done.5.taken_ref
  102.8 16.2 %land.1 = bf16[64,2,8,512]{3,2,1,0:T(8,128)(2,1)} custom-call(bf16[34,2,8,512]{3,2,1,0:T(8,128)(2,1)S(1)} %copy-done, bf16[30,2,8,512]{3,2,1,0:T(8,128)(2,1)S(1)} %collective-permute-done.got_ref, bf16[24,2,8,512]{3,2,1,0:T(8,128)(2,1)S(1)} %collective-permute-done.1.three_ref, bf16[20,2,8,512]{3,2,1,0:T(8,128)(2,1)S(1)} %collective-permute-done.2.six_ref, ...), custom_call_target="tpu_custom_call" | custom-call | bytes 1024 | tf_op jit(solution)/shard_map/land/pallas_call | solution.py:284
Async XLA Ops:
  3.7 21.1 %collective-permute-start = (bf16[30,2,8,512]{3,2,1,0:T(8,128)(2,1)}, bf16[30,2,8,512]{3,2,1,0:T(8,128)(2,1)S(1)}, u32[]{:S(2)}, u32[]{:S(2)}) collective-permute-start(bf16[30,2,8,512]{3,2,1,0:T(8,128)(2,1)} %get-tuple-element.12), channel_id=1, source_target_pairs={{0,16},{16,0},{32,48},{48,32},{64,80},{80,64},{96,112},{112,96},{1... | collective-permute-start | bytes 1474568 | tf_op jit(solution)/shard_map/ppermute | solution.py:271
  6.3 18.6 %copy-start = (bf16[34,2,8,512]{3,2,1,0:T(8,128)(2,1)S(1)}, bf16[34,2,8,512]{3,2,1,0:T(8,128)(2,1)}, u32[]{:S(2)}) copy-start(bf16[34,2,8,512]{3,2,1,0:T(8,128)(2,1)} %get-tuple-element.11.own_ref) | copy-start | bytes 1671172
  9.4 31.2 %all-to-all-start = ((bf16[32,16,128]{2,1,0:T(8,128)(2,1)}), bf16[32,16,128]{2,1,0:T(8,128)(2,1)S(1)}, u32[]{:S(2)}, u32[]{:S(2)}) async-start(bf16[32,16,128]{2,1,0:T(8,128)(2,1)} %attend.1), calls=%async_computation | async-start | bytes 262144 | tf_op jit(solution)/shard_map/all_to_all | solution.py:282
  25.8 25.6 %copy-start.1 = (bf16[256,1024]{1,0:T(8,128)(2,1)S(1)}, bf16[256,1024]{1,0:T(8,128)(2,1)}, u32[]{:S(2)}) copy-start(bf16[256,1024]{1,0:T(8,128)(2,1)} %weight_ref.1) | copy-start | bytes 1572868
  25.8 50.7 %collective-permute-start.1 = (bf16[24,2,8,512]{3,2,1,0:T(8,128)(2,1)S(1)}, bf16[24,2,8,512]{3,2,1,0:T(8,128)(2,1)S(1)}, u32[]{:S(2)}, u32[]{:S(2)}) collective-permute-start(bf16[24,2,8,512]{3,2,1,0:T(8,128)(2,1)S(1)} %get-tuple-element.13.after_ref), channel_id=1, source_target_pairs={{0,96},{16,432},{32,128},{48,464},{64,160},{80,496},{96,192},{112,... | collective-permute-start | bytes 1179656 | tf_op jit(solution)/shard_map/ppermute | solution.py:268
  32.3 44.2 %collective-permute-start.2 = (bf16[20,2,8,512]{3,2,1,0:T(8,128)(2,1)S(1)}, bf16[20,2,8,512]{3,2,1,0:T(8,128)(2,1)S(1)}, u32[]{:S(2)}, u32[]{:S(2)}) collective-permute-start(bf16[20,2,8,512]{3,2,1,0:T(8,128)(2,1)S(1)} %get-tuple-element.15), channel_id=1, source_target_pairs={{0,192},{16,336},{32,224},{48,368},{64,256},{80,400},{96,288},{112... | collective-permute-start | bytes 983048 | tf_op jit(solution)/shard_map/ppermute | solution.py:268
  52.7 48.5 %all-to-all-start.2 = ((bf16[32,4,1024]{2,1,0:T(4,128)(2,1)}), bf16[32,4,1024]{2,1,0:T(4,128)(2,1)S(1)}, u32[]{:S(2)}, u32[]{:S(2)}) async-start(bf16[32,4,1024]{2,1,0:T(4,128)(2,1)} %project.1.after_ref), calls=%async_computation.2 | async-start | bytes 524288 | tf_op jit(solution)/shard_map/all_to_all | solution.py:320
  77.6 15.1 %collective-permute-start.3 = (bf16[24,2,8,512]{3,2,1,0:T(8,128)(2,1)S(1)}, bf16[24,2,8,512]{3,2,1,0:T(8,128)(2,1)S(1)}, u32[]{:S(2)}, u32[]{:S(2)}) collective-permute-start(bf16[24,2,8,512]{3,2,1,0:T(8,128)(2,1)S(1)} %get-tuple-element.16), channel_id=1, source_target_pairs={{0,32},{16,496},{32,64},{48,16},{64,96},{80,48},{96,128},{112,80},... | collective-permute-start | bytes 1179656 | tf_op jit(solution)/shard_map/ppermute | solution.py:268
  79.5 13.2 %collective-permute-start.4 = (bf16[20,2,8,512]{3,2,1,0:T(8,128)(2,1)S(1)}, bf16[20,2,8,512]{3,2,1,0:T(8,128)(2,1)S(1)}, u32[]{:S(2)}, u32[]{:S(2)}) collective-permute-start(bf16[20,2,8,512]{3,2,1,0:T(8,128)(2,1)S(1)} %get-tuple-element.17), channel_id=1, source_target_pairs={{0,64},{16,464},{32,96},{48,496},{64,128},{80,16},{96,160},{112,48... | collective-permute-start | bytes 983048 | tf_op jit(solution)/shard_map/ppermute | solution.py:268
  93.5 9.3 %collective-permute-start.5 = (bf16[30,2,8,512]{3,2,1,0:T(8,128)(2,1)S(1)}, bf16[30,2,8,512]{3,2,1,0:T(8,128)(2,1)}, u32[]{:S(2)}, u32[]{:S(2)}) collective-permute-start(bf16[30,2,8,512]{3,2,1,0:T(8,128)(2,1)S(1)} %give.1), channel_id=1, source_target_pairs={{0,16},{16,0},{32,48},{48,32},{64,80},{80,64},{96,112},{112,96},{1... | collective-permute-start | bytes 1474568 | tf_op jit(solution)/shard_map/ppermute | solution.py:271

commit v5 on v4

--- a/solution.py
+++ b/solution.py
@@ -36,6 +36,11 @@
 def token_rows(ref, part):
     pages = ref[:, part].astype(F32)
     return pages.reshape(pages.shape[0] * PAGE, KVH * HD).astype(BF16)
+
+
+def side_lanes(lane, shift, weight_sum):
+    high = weight_sum.astype(BF16).astype(F32)
+    return jnp.where(lane == 0, shift, jnp.where(lane == 1, high, jnp.where(lane == 4, weight_sum - high, 0.0)))
 
 
 def attend_kernel(q_ref, res_ref, move_ref, count_ref, request_ref, owner_ref, request_row_ref, out_ref):
@@ -87,7 +92,7 @@
         weight_sum = jnp.sum(weights.astype(F32), axis=1, keepdims=True)
         summed = jnp.dot(weights, values[:, g * HD : (g + 1) * HD], preferred_element_type=F32)
         own = slice(g * rows, (g + 1) * rows)
-        extra = jnp.where(lane == 0, shift, jnp.where(lane == 1, weight_sum, 0.0))
+        extra = side_lanes(lane, shift, weight_sum)
         for r in range(CAP):
             extra = jnp.where(lane == 2 + r, slot_ids[r][own], extra)
         both = jnp.concatenate([summed.reshape(per, 8, HD), extra.reshape(per, 8, HD)], axis=1)
@@ -112,7 +117,8 @@
     return ref.at[pl.ds(first * QUAD, count * QUAD)]
 
 
-def pack_kernel(move_ref, owner_ref, own_ref, other_ref, used_ref):
+def pack_kernel(move_ref, owner_ref, after_ref, own_ref, other_ref, used_ref):
+    del after_ref
     own_ref[...] = jnp.zeros(own_ref.shape, own_ref.dtype)
     other_ref[...] = jnp.zeros(other_ref.shape, other_ref.dtype)
     for o in range(used_ref.shape[0]):
@@ -145,16 +151,15 @@
     lax.fori_loop(0, move_ref.shape[0], place, 0)
 
 
-def merge_kernel(own_ref, got_ref, three_ref, six_ref, sems):
-    copy_all(
-        [
-            (quads(own_ref, 5, 3), quads(six_ref, 0, 3)),
-            (quads(got_ref, 5, 2), quads(six_ref, 3, 2)),
-            (quads(own_ref, 2, 3), quads(three_ref, 0, 3)),
-            (quads(got_ref, 2, 3), quads(three_ref, 3, 3)),
-        ],
-        sems,
-    )
+def merge_six_kernel(own_ref, got_ref, out_ref, sems):
+    pairs = [(quads(own_ref, 5, 3), quads(out_ref, 0, 3)), (quads(got_ref, 5, 2), quads(out_ref, 3, 2))]
+    copy_all(pairs, sems)
+
+
+def merge_three_kernel(own_ref, got_ref, after_ref, out_ref, sems):
+    del after_ref
+    pairs = [(quads(own_ref, 2, 3), quads(out_ref, 0, 3)), (quads(got_ref, 2, 3), quads(out_ref, 3, 3))]
+    copy_all(pairs, sems)
 
 
 def forward_kernel(own_ref, got_ref, three_ref, six_ref, after_ref, one_ref, two_ref, sems):
@@ -179,7 +184,8 @@
     )
 
 
-def give_kernel(three_ref, six_ref, one_ref, two_ref, out_ref, sems):
+def give_kernel(three_ref, six_ref, one_ref, two_ref, after_ref, out_ref, sems):
+    del after_ref
     core = lax.axis_index("kv") % 2
     copies = [(two_ref.at[pl.ds(4 * QUAD + CAP, CAP)], out_ref.at[pl.ds(GIVEN, CAP)])]
     for distance, ref, same, other in arrived(three_ref, six_ref, one_ref, two_ref):
@@ -212,7 +218,8 @@
 
 
 def combined(parts):
-    shifts, sums, values = parts[:, 8:, 0:1], parts[:, 8:, 1:2], parts[:, :8, :]
+    shifts, values = parts[:, 8:, 0:1], parts[:, :8, :]
+    sums = parts[:, 8:, 1:2] + parts[:, 8:, 4:5]
     shift = jnp.max(shifts, axis=0)
     factor = jnp.exp(shifts - shift[None])
     return shift, jnp.sum(sums * factor, axis=0), jnp.sum(values * factor, axis=0)
@@ -224,8 +231,9 @@
     parts = parts_ref[...].astype(F32)
     shift, weight_sum, values = combined(parts)
     lane = iota((8, HD), 1)
-    extra = jnp.where(lane == 0, shift, jnp.where(lane == 1, weight_sum, 0.0))
-    out_ref[...] = jnp.broadcast_to(jnp.concatenate([values, extra], axis=0)[None], out_ref.shape)
+    extra = side_lanes(lane, shift, weight_sum)
+    out = jnp.concatenate([values, extra], axis=0).astype(out_ref.dtype)
+    out_ref[...] = jnp.broadcast_to(out[None], out_ref.shape)
     n = parts.shape[0]
     source, place = iota((n, n * CAP), 0), iota((n, n * CAP), 1)
     ids = parts[:, 8, :]
@@ -235,12 +243,15 @@
 
 def project_kernel(parts_any, weight_ref, out_ref, parts_ref):
     pltpu.sync_copy(parts_any, parts_ref)
-    _, weight_sum, values = combined(parts_ref[...])
+    _, weight_sum, values = combined(parts_ref[...].astype(F32))
     attended = (values / weight_sum).astype(BF16)
     upper = jnp.dot(attended, weight_ref[:HD], preferred_element_type=F32)
     lower = jnp.dot(attended, weight_ref[HD:], preferred_element_type=F32)
     partial = (upper[:B] + lower[B:]).astype(out_ref.dtype)
-    out_ref[...] = jnp.broadcast_to(partial[None], out_ref.shape)
+    half = partial.shape[1] // 2
+    for core in range(2):
+        part = partial[:, core * half : (core + 1) * half]
+        out_ref[:, core] = jnp.broadcast_to(part[None], (out_ref.shape[0],) + part.shape)
 
 
 def add_kernel(parts_any, out_ref, parts_ref):
@@ -273,31 +284,31 @@
     own, other = pl.pallas_call(
         pack_kernel,
         out_shape=(pages(HOME + CAP), pages(GIVEN + CAP)),
-        in_specs=[VMEM, SMEM],
+        in_specs=[VMEM, SMEM, ANY],
         out_specs=(VMEM, VMEM),
         scratch_shapes=[pltpu.SMEM((kv_size,), jnp.int32)],
         name="pack",
-    )(move_cache, owners)
+    )(move_cache, owners, parts)
     got = swap(other)
     parts = lax.all_to_all(parts, "kv", split_axis=0, concat_axis=0, tiled=True)
-    def copies(kernel, name, out_pages, count, *args):
+    def copies(kernel, name, out_pages, count, *args, out=ANY):
         return pl.pallas_call(
             kernel,
             out_shape=tuple(pages(n) for n in out_pages),
             in_specs=[ANY] * len(args),
-            out_specs=(ANY,) * len(out_pages),
+            out_specs=(out,) * len(out_pages),
             scratch_shapes=[pltpu.SemaphoreType.DMA((count,))],
             compiler_params=pltpu.CompilerParams(vmem_limit_bytes=SMALL),
             cost_estimate=pl.CostEstimate(flops=0, bytes_accessed=1024, transcendentals=0),
             name=name,
         )(*args)
 
-    three, six = copies(merge_kernel, "merge", (6 * QUAD, 5 * QUAD), 4, own, got)
-    six_up, three_up = shift(six, 6), shift(three, 3)
+    (six,) = copies(merge_six_kernel, "merge_six", (5 * QUAD,), 2, own, got)
+    (three,) = copies(merge_three_kernel, "merge_three", (6 * QUAD,), 2, own, got, six)
     part, landed_ids = pl.pallas_call(
         column_kernel,
         out_shape=(
-            jax.ShapeDtypeStruct((tp_size, 16, HD), F32),
+            jax.ShapeDtypeStruct((tp_size, 16, HD), BF16),
             jax.ShapeDtypeStruct((1, kv_size * CAP), jnp.int32),
         ),
         in_specs=[ANY, ANY],
@@ -305,33 +316,41 @@
         scratch_shapes=[pltpu.VMEM(parts.shape, BF16)],
         compiler_params=pltpu.CompilerParams(vmem_limit_bytes=SMALL),
         name="column",
+        cost_estimate=pl.CostEstimate(flops=0, bytes_accessed=1024, transcendentals=0),
     )(parts, three)
-    three, six = three_up, six_up
+    six, three = shift(six, 6), shift(three, 3)
     columns = lax.all_to_all(part, "tp", split_axis=0, concat_axis=0, tiled=True)
+    half = out_weight.shape[1] // 2
     partial_out = pl.pallas_call(
         project_kernel,
-        out_shape=jax.ShapeDtypeStruct((kv_size, B, out_weight.shape[1]), BF16),
+        out_shape=jax.ShapeDtypeStruct((CHIPS, 2, B, half), BF16),
         in_specs=[ANY, VMEM],
         out_specs=VMEM,
-        scratch_shapes=[pltpu.VMEM(columns.shape, F32)],
+        scratch_shapes=[pltpu.VMEM(columns.shape, BF16)],
         compiler_params=pltpu.CompilerParams(vmem_limit_bytes=SMALL),
         name="project",
+        cost_estimate=pl.CostEstimate(flops=0, bytes_accessed=1024, transcendentals=0),
     )(columns, out_weight)
-    partials = lax.all_to_all(partial_out, "kv", split_axis=0, concat_axis=0, tiled=True)
-    mixed = pl.pallas_call(
+    partials = lax.all_to_all(
+        partial_out.reshape(kv_size, B, half), "kv", split_axis=0, concat_axis=0, tiled=True
+    )
+    mixed_half = pl.pallas_call(
         add_kernel,
-        out_shape=jax.ShapeDtypeStruct((B, out_weight.shape[1]), BF16),
+        out_shape=jax.ShapeDtypeStruct((B, half), BF16),
         in_specs=[ANY],
         out_specs=VMEM,
         scratch_shapes=[pltpu.VMEM(partials.shape, BF16)],
         compiler_params=pltpu.CompilerParams(vmem_limit_bytes=SMALL),
         name="add",
+        cost_estimate=pl.CostEstimate(flops=0, bytes_accessed=1024, transcendentals=0),
     )(partials)
+    both_cores = [[2 * z, 2 * z + 1] for z in range(CHIPS)]
+    mixed = lax.all_gather(mixed_half, "kv", axis=1, tiled=True, axis_index_groups=both_cores)
     one, two = copies(forward_kernel, "forward", (6 * QUAD, 5 * QUAD), 11, own, got, three, six, partial_out)
     two, one = shift(two, 2), shift(one, 1)
-    (give,) = copies(give_kernel, "give", (GIVEN + CAP,), 15, three, six, one, two)
+    (give,) = copies(give_kernel, "give", (GIVEN + CAP,), 15, three, six, one, two, mixed_half)
     taken = swap(give)
-    (landed,) = copies(land_kernel, "land", (kv_size * CAP,), 25, own, got, three, six, one, two, taken)
+    (landed,) = copies(land_kernel, "land", (kv_size * CAP,), 25, own, got, three, six, one, two, taken, out=VMEM)
     return (mixed, landed, landed_ids.reshape(-1))
 
 

time: 120 us -> 105 us (0.88)
  the two profiles are of different devices: /device:TPU:23 before, /device:TPU:21 now
where the time goes in v5:
time: 105 us; the launch traced here: 104 us
  starting transfers between devices  49.3 us (47%)
  waiting for transfers between devices  26.9 us (26%)
  Pallas kernels  13.8 us (13%)
  blocking collectives  11.6 us (11%)
  local copies, waits for them, and re-layouts  1.66 us (2%)
    ppermute x4, waiting for transfers between devices, shift(): return lax.ppermute(x, 'kv', pairs)  26.9 us
    ppermute x4, starting transfers between devices, shift(): return lax.ppermute(x, 'kv', pairs)  18.2 us
    all_to_all x1, starting transfers between devices, local(): parts = lax.all_to_all(parts, 'kv', split_axis=0, concat_axis=0, tiled=True)  15.4 us
    all_to_all x1, blocking collectives, local(): lax.all_to_all(part, 'tp', split_axis=0, concat_axis=0, tiled=True)  9.78 us
    ppermute x2, starting transfers between devices, swap(): return lax.ppermute(x, 'kv', [(i, i ^ 1) for i in range(kv_size)])  9.59 us
    all_to_all x1, starting transfers between devices, local(): lax.all_to_all(partial_out.reshape(kv_size, B, half), 'kv', split_axis=0,...  6.16 us
    pallas_call x5, Pallas kernels, copies(): pl.pallas_call(kernel, out_shape=tuple((pages(n) for n in out_pages)), in...  5.46 us
    pallas_call x1, Pallas kernels, local(): pl.pallas_call(attend_kernel, out_shape=jax.ShapeDtypeStruct((kv_size, 16...  3.1 us
  transfers between devices with their start and end apart: 8, of which 2 were waited for; matrix products, arithmetic and copies ran while one was open for 0% of the time, Pallas kernels for 4%

profile of v5, /device:TPU:21, one launch (start us, length us, event | category | flops | bytes accessed | tf_op | source)
XLA Modules:
  0.0 104.1 jit_solution(9263361817919393286)
XLA Ops:
  0.6 3.1 %attend.1.after_ref = bf16[32,16,128]{2,1,0:T(8,128)(2,1)} custom-call(bf16[4,8192]{1,0:T(4,128)(2,1)} %q_ref.1, bf16[32,2,8,512]{3,2,1,0:T(8,128)(2,1)} %res_ref.1, bf16[32,2,8,512]{3,2,1,0:T(8,128)(2,1)} %move_ref.3, s32[1,4]{1,0:T(1,128)} %count_ref.1, s32[32]{0:T(128)} %request_ref.1, s32[1,32]{1,0:T(1,128)} %bitcast.6, s32[1,32]{1,0:T(1,128)} %bitcast.5), custom_call_target="tpu_custom_call" | custom-call | tf_op jit(solution)/shard_map/attend/pallas_call | solution.py:265
  3.7 3.0 %pack.1 = (bf16[34,2,8,512]{3,2,1,0:T(8,128)(2,1)}, bf16[30,2,8,512]{3,2,1,0:T(8,128)(2,1)}) custom-call(bf16[32,2,8,512]{3,2,1,0:T(8,128)(2,1)} %move_ref.3, s32[32]{0:T(128)} %bitcast.7, bf16[32,16,128]{2,1,0:T(8,128)(2,1)} %attend.1.after_ref), custom_call_target="tpu_custom_call" | custom-call | tf_op jit(solution)/shard_map/pack/pallas_call | solution.py:284
  6.8 2.6 %collective-permute-start = (bf16[30,2,8,512]{3,2,1,0:T(8,128)(2,1)}, bf16[30,2,8,512]{3,2,1,0:T(8,128)(2,1)S(1)}, u32[]{:S(2)}, u32[]{:S(2)}) collective-permute-start(bf16[30,2,8,512]{3,2,1,0:T(8,128)(2,1)} %get-tuple-element.10), channel_id=1, source_target_pairs={{0,16},{16,0},{32,48},{48,32},{64,80},{80,64},{96,112},{112,96},{1... | collective-permute-start | bytes 1474568 | tf_op jit(solution)/shard_map/ppermute | solution.py:282
  9.4 15.4 %all-to-all-start = ((bf16[32,16,128]{2,1,0:T(8,128)(2,1)}), bf16[32,16,128]{2,1,0:T(8,128)(2,1)S(1)}, u32[]{:S(2)}, u32[]{:S(2)}) async-start(bf16[32,16,128]{2,1,0:T(8,128)(2,1)} %attend.1.after_ref), calls=%async_computation | async-start | bytes 262144 | tf_op jit(solution)/shard_map/all_to_all | solution.py:293
  24.7 0.0 collective-permute-done.got_ref
  24.8 0.0 copy-start
  24.8 1.0 %copy-done = bf16[34,2,8,512]{3,2,1,0:T(8,128)(2,1)S(1)} copy-done((bf16[34,2,8,512]{3,2,1,0:T(8,128)(2,1)S(1)}, bf16[34,2,8,512]{3,2,1,0:T(8,128)(2,1)}, u32[]{:S(2)}) %copy-start) | copy-done | bytes 557080
  25.8 0.4 merge_six.1.after_ref
  26.2 0.5 merge_three.1.after_ref
  26.8 0.0 copy-start.2
  26.8 6.5 %collective-permute-start.1 = (bf16[24,2,8,512]{3,2,1,0:T(8,128)(2,1)S(1)}, bf16[24,2,8,512]{3,2,1,0:T(8,128)(2,1)S(1)}, u32[]{:S(2)}, u32[]{:S(2)}) collective-permute-start(bf16[24,2,8,512]{3,2,1,0:T(8,128)(2,1)S(1)} %merge_three.1.after_ref), channel_id=1, source_target_pairs={{0,96},{16,432},{32,128},{48,464},{64,160},{80,496},{96,192},{112,... | collective-permute-start | bytes 1179656 | tf_op jit(solution)/shard_map/ppermute | solution.py:279
  33.3 7.8 %collective-permute-start.2 = (bf16[20,2,8,512]{3,2,1,0:T(8,128)(2,1)S(1)}, bf16[20,2,8,512]{3,2,1,0:T(8,128)(2,1)S(1)}, u32[]{:S(2)}, u32[]{:S(2)}) collective-permute-start(bf16[20,2,8,512]{3,2,1,0:T(8,128)(2,1)S(1)} %merge_six.1.after_ref), channel_id=1, source_target_pairs={{0,192},{16,336},{32,224},{48,368},{64,256},{80,400},{96,288},{112... | collective-permute-start | bytes 983048 | tf_op jit(solution)/shard_map/ppermute | solution.py:279
  41.1 0.0 all-to-all-done.parts_any
  41.1 0.9 column.1
  42.0 0.0 copy-start.1
  42.0 9.8 %all_to_all.15.parts_any = bf16[16,16,128]{2,1,0:T(8,128)(2,1)S(1)} all-to-all(bf16[16,16,128]{2,1,0:T(8,128)(2,1)S(1)} %get-tuple-element.11), channel_id=1, replica_groups=mesh['kv'=32,'tp'=16] {'tp'}, dimensions={0} | all-to-all | bytes 131072 | tf_op jit(solution)/shard_map/all_to_all | solution.py:322
  51.8 0.0 copy-done.2
  51.8 1.1 %project.1.after_ref = bf16[16,2,4,512]{3,2,1,0:T(4,128)(2,1)} custom-call(bf16[16,16,128]{2,1,0:T(8,128)(2,1)S(1)} %all_to_all.15.parts_any, bf16[256,1024]{1,0:T(8,128)(2,1)S(1)} %copy-done.2), custom_call_target="tpu_custom_call" | custom-call | bytes 1024 | tf_op jit(solution)/shard_map/project/pallas_call | solution.py:324
  52.9 6.2 %all-to-all-start.2 = ((bf16[32,4,512]{2,1,0:T(4,128)(2,1)}), bf16[32,4,512]{2,1,0:T(4,128)(2,1)S(1)}, u32[]{:S(2)}, u32[]{:S(2)}) async-start(bf16[32,4,512]{2,1,0:T(4,128)(2,1)} %bitcast.3), calls=%async_computation.2 | async-start | bytes 262144 | tf_op jit(solution)/shard_map/all_to_all | solution.py:334
  59.1 16.4 %collective-permute-done.2.six_ref = bf16[20,2,8,512]{3,2,1,0:T(8,128)(2,1)S(1)} collective-permute-done((bf16[20,2,8,512]{3,2,1,0:T(8,128)(2,1)S(1)}, bf16[20,2,8,512]{3,2,1,0:T(8,128)(2,1)S(1)}, u32[]{:S(2)}, u32[]{:S(2)}) %collective-permute-start.2) | collective-permute-done | bytes 327712 | tf_op jit(solution)/shard_map/ppermute | solution.py:279
  75.5 0.0 collective-permute-done.1.three_ref
  75.5 0.0 copy-done.1
  75.5 1.0 forward.1
  76.6 1.9 %collective-permute-start.3 = (bf16[24,2,8,512]{3,2,1,0:T(8,128)(2,1)S(1)}, bf16[24,2,8,512]{3,2,1,0:T(8,128)(2,1)S(1)}, u32[]{:S(2)}, u32[]{:S(2)}) collective-permute-start(bf16[24,2,8,512]{3,2,1,0:T(8,128)(2,1)S(1)} %get-tuple-element.12), channel_id=1, source_target_pairs={{0,32},{16,496},{32,64},{48,16},{64,96},{80,48},{96,128},{112,80},... | collective-permute-start | bytes 1179656 | tf_op jit(solution)/shard_map/ppermute | solution.py:279
  78.5 1.9 %collective-permute-start.4 = (bf16[20,2,8,512]{3,2,1,0:T(8,128)(2,1)S(1)}, bf16[20,2,8,512]{3,2,1,0:T(8,128)(2,1)S(1)}, u32[]{:S(2)}, u32[]{:S(2)}) collective-permute-start(bf16[20,2,8,512]{3,2,1,0:T(8,128)(2,1)S(1)} %get-tuple-element.13), channel_id=1, source_target_pairs={{0,64},{16,464},{32,96},{48,496},{64,128},{80,16},{96,160},{112,48... | collective-permute-start | bytes 983048 | tf_op jit(solution)/shard_map/ppermute | solution.py:279
  80.4 0.0 all-to-all-done.2.parts_any
  80.4 0.2 add.1.after_ref
  80.7 10.5 %collective-permute-done.4.two_ref = bf16[20,2,8,512]{3,2,1,0:T(8,128)(2,1)S(1)} collective-permute-done((bf16[20,2,8,512]{3,2,1,0:T(8,128)(2,1)S(1)}, bf16[20,2,8,512]{3,2,1,0:T(8,128)(2,1)S(1)}, u32[]{:S(2)}, u32[]{:S(2)}) %collective-permute-start.4) | collective-permute-done | bytes 327712 | tf_op jit(solution)/shard_map/ppermute | solution.py:279
  91.1 0.0 collective-permute-done.3.one_ref
  91.1 0.8 give.1
  91.9 7.0 %collective-permute-start.5 = (bf16[30,2,8,512]{3,2,1,0:T(8,128)(2,1)S(1)}, bf16[30,2,8,512]{3,2,1,0:T(8,128)(2,1)S(1)}, u32[]{:S(2)}, u32[]{:S(2)}) collective-permute-start(bf16[30,2,8,512]{3,2,1,0:T(8,128)(2,1)S(1)} %give.1), channel_id=1, source_target_pairs={{0,16},{16,0},{32,48},{48,32},{64,80},{80,64},{96,112},{112,96},{1... | collective-permute-start | bytes 1474568 | tf_op jit(solution)/shard_map/ppermute | solution.py:282
  99.0 1.8 %all_gather.3 = bf16[4,1024]{1,0:T(4,128)(2,1)S(1)} all-gather(bf16[4,512]{1,0:T(4,128)(2,1)S(1)} %add.1.after_ref), channel_id=1, replica_groups={{0,16},{32,48},{64,80},{96,112},{128,144},{160,176},{192,208},{224,240}..., dimensions={1}, use_global_device_ids=true | all-gather | bytes 12288 | tf_op jit(solution)/shard_map/all_gather | solution.py:348
  100.8 0.0 collective-permute-done.5.taken_ref
  100.8 2.7 %land.1 = bf16[64,2,8,512]{3,2,1,0:T(8,128)(2,1)} custom-call(bf16[34,2,8,512]{3,2,1,0:T(8,128)(2,1)S(1)} %copy-done.1, bf16[30,2,8,512]{3,2,1,0:T(8,128)(2,1)S(1)} %collective-permute-done.got_ref, bf16[24,2,8,512]{3,2,1,0:T(8,128)(2,1)S(1)} %collective-permute-done.1.three_ref, bf16[20,2,8,512]{3,2,1,0:T(8,128)(2,1)S(1)} %collective-permute-done.2.six_ref, ...), custom_call_target="tpu_custom_call" | custom-call | bytes 1024 | tf_op jit(solution)/shard_map/land/pallas_call | solution.py:295
  103.5 0.6 copy.11
Async XLA Ops:
  6.8 18.0 %collective-permute-start = (bf16[30,2,8,512]{3,2,1,0:T(8,128)(2,1)}, bf16[30,2,8,512]{3,2,1,0:T(8,128)(2,1)S(1)}, u32[]{:S(2)}, u32[]{:S(2)}) collective-permute-start(bf16[30,2,8,512]{3,2,1,0:T(8,128)(2,1)} %get-tuple-element.10), channel_id=1, source_target_pairs={{0,16},{16,0},{32,48},{48,32},{64,80},{80,64},{96,112},{112,96},{1... | collective-permute-start | bytes 1474568 | tf_op jit(solution)/shard_map/ppermute | solution.py:282
  9.4 31.8 %all-to-all-start = ((bf16[32,16,128]{2,1,0:T(8,128)(2,1)}), bf16[32,16,128]{2,1,0:T(8,128)(2,1)S(1)}, u32[]{:S(2)}, u32[]{:S(2)}) async-start(bf16[32,16,128]{2,1,0:T(8,128)(2,1)} %attend.1.after_ref), calls=%async_computation | async-start | bytes 262144 | tf_op jit(solution)/shard_map/all_to_all | solution.py:293
  24.8 1.1 %copy-start = (bf16[34,2,8,512]{3,2,1,0:T(8,128)(2,1)S(1)}, bf16[34,2,8,512]{3,2,1,0:T(8,128)(2,1)}, u32[]{:S(2)}) copy-start(bf16[34,2,8,512]{3,2,1,0:T(8,128)(2,1)} %get-tuple-element.9.own_ref) | copy-start | bytes 1671172
  26.8 25.1 %copy-start.2 = (bf16[256,1024]{1,0:T(8,128)(2,1)S(1)}, bf16[256,1024]{1,0:T(8,128)(2,1)}, u32[]{:S(2)}) copy-start(bf16[256,1024]{1,0:T(8,128)(2,1)} %weight_ref.1) | copy-start | bytes 1572868
  26.8 48.7 %collective-permute-start.1 = (bf16[24,2,8,512]{3,2,1,0:T(8,128)(2,1)S(1)}, bf16[24,2,8,512]{3,2,1,0:T(8,128)(2,1)S(1)}, u32[]{:S(2)}, u32[]{:S(2)}) collective-permute-start(bf16[24,2,8,512]{3,2,1,0:T(8,128)(2,1)S(1)} %merge_three.1.after_ref), channel_id=1, source_target_pairs={{0,96},{16,432},{32,128},{48,464},{64,160},{80,496},{96,192},{112,... | collective-permute-start | bytes 1179656 | tf_op jit(solution)/shard_map/ppermute | solution.py:279
  33.3 42.2 %collective-permute-start.2 = (bf16[20,2,8,512]{3,2,1,0:T(8,128)(2,1)S(1)}, bf16[20,2,8,512]{3,2,1,0:T(8,128)(2,1)S(1)}, u32[]{:S(2)}, u32[]{:S(2)}) collective-permute-start(bf16[20,2,8,512]{3,2,1,0:T(8,128)(2,1)S(1)} %merge_six.1.after_ref), channel_id=1, source_target_pairs={{0,192},{16,336},{32,224},{48,368},{64,256},{80,400},{96,288},{112... | collective-permute-start | bytes 983048 | tf_op jit(solution)/shard_map/ppermute | solution.py:279
  42.0 33.5 %copy-start.1 = (bf16[34,2,8,512]{3,2,1,0:T(8,128)(2,1)S(1)}, bf16[34,2,8,512]{3,2,1,0:T(8,128)(2,1)}, u32[]{:S(2)}) copy-start(bf16[34,2,8,512]{3,2,1,0:T(8,128)(2,1)} %get-tuple-element.9.own_ref) | copy-start | bytes 1671172
  52.9 27.5 %all-to-all-start.2 = ((bf16[32,4,512]{2,1,0:T(4,128)(2,1)}), bf16[32,4,512]{2,1,0:T(4,128)(2,1)S(1)}, u32[]{:S(2)}, u32[]{:S(2)}) async-start(bf16[32,4,512]{2,1,0:T(4,128)(2,1)} %bitcast.3), calls=%async_computation.2 | async-start | bytes 262144 | tf_op jit(solution)/shard_map/all_to_all | solution.py:334
  76.6 14.6 %collective-permute-start.3 = (bf16[24,2,8,512]{3,2,1,0:T(8,128)(2,1)S(1)}, bf16[24,2,8,512]{3,2,1,0:T(8,128)(2,1)S(1)}, u32[]{:S(2)}, u32[]{:S(2)}) collective-permute-start(bf16[24,2,8,512]{3,2,1,0:T(8,128)(2,1)S(1)} %get-tuple-element.12), channel_id=1, source_target_pairs={{0,32},{16,496},{32,64},{48,16},{64,96},{80,48},{96,128},{112,80},... | collective-permute-start | bytes 1179656 | tf_op jit(solution)/shard_map/ppermute | solution.py:279
  78.5 12.7 %collective-permute-start.4 = (bf16[20,2,8,512]{3,2,1,0:T(8,128)(2,1)S(1)}, bf16[20,2,8,512]{3,2,1,0:T(8,128)(2,1)S(1)}, u32[]{:S(2)}, u32[]{:S(2)}) collective-permute-start(bf16[20,2,8,512]{3,2,1,0:T(8,128)(2,1)S(1)} %get-tuple-element.13), channel_id=1, source_target_pairs={{0,64},{16,464},{32,96},{48,496},{64,128},{80,16},{96,160},{112,48... | collective-permute-start | bytes 983048 | tf_op jit(solution)/shard_map/ppermute | solution.py:279
  91.9 8.8 %collective-permute-start.5 = (bf16[30,2,8,512]{3,2,1,0:T(8,128)(2,1)S(1)}, bf16[30,2,8,512]{3,2,1,0:T(8,128)(2,1)S(1)}, u32[]{:S(2)}, u32[]{:S(2)}) collective-permute-start(bf16[30,2,8,512]{3,2,1,0:T(8,128)(2,1)S(1)} %give.1), channel_id=1, source_target_pairs={{0,16},{16,0},{32,48},{48,32},{64,80},{80,64},{96,112},{112,96},{1... | collective-permute-start | bytes 1474568 | tf_op jit(solution)/shard_map/ppermute | solution.py:282

commit v6 on v5

--- a/solution.py
+++ b/solution.py
@@ -43,7 +43,8 @@
     return jnp.where(lane == 0, shift, jnp.where(lane == 1, high, jnp.where(lane == 4, weight_sum - high, 0.0)))
 
 
-def attend_kernel(q_ref, res_ref, move_ref, count_ref, request_ref, owner_ref, request_row_ref, out_ref):
+def attend_kernel(q_ref, res_ref, move_ref, count_ref, request_ref, owner_ref, request_row_ref, after_ref, out_ref):
+    del after_ref
     rows = GROUP * B
     n_res, n_move = res_ref.shape[0], move_ref.shape[0]
     page = iota((8, n_res * PAGE), 1) // PAGE
@@ -117,8 +118,7 @@
     return ref.at[pl.ds(first * QUAD, count * QUAD)]
 
 
-def pack_kernel(move_ref, owner_ref, after_ref, own_ref, other_ref, used_ref):
-    del after_ref
+def pack_kernel(move_ref, owner_ref, own_ref, other_ref, used_ref):
     own_ref[...] = jnp.zeros(own_ref.shape, own_ref.dtype)
     other_ref[...] = jnp.zeros(other_ref.shape, other_ref.dtype)
     for o in range(used_ref.shape[0]):
@@ -225,8 +225,13 @@
     return shift, jnp.sum(sums * factor, axis=0), jnp.sum(values * factor, axis=0)
 
 
-def column_kernel(parts_any, after_ref, out_ref, ids_ref, parts_ref):
-    del after_ref
+def fill_kernel(after_ref, out_ref):
+    del after_ref
+    out_ref[...] = jnp.zeros(out_ref.shape, F32)
+
+
+def column_kernel(parts_any, after_ref, fill_ref, out_ref, ids_ref, parts_ref):
+    del after_ref, fill_ref
     pltpu.sync_copy(parts_any, parts_ref)
     parts = parts_ref[...].astype(F32)
     shift, weight_sum, values = combined(parts)
@@ -262,13 +267,6 @@
 def local(queries, res_cache, res_count, move_cache, move_request, move_owner, out_weight):
     kv_size, tp_size = lax.axis_size("kv"), lax.axis_size("tp")
     owners = move_owner.reshape(-1)
-    parts = pl.pallas_call(
-        attend_kernel,
-        out_shape=jax.ShapeDtypeStruct((kv_size, 16, HD), BF16),
-        in_specs=[VMEM, VMEM, VMEM, SMEM, SMEM, VMEM, VMEM],
-        out_specs=VMEM,
-        name="attend",
-    )(queries, res_cache, move_cache, res_count, move_request, owners[None, :], move_request[None, :])
     page = move_cache.shape[1:]
 
     def pages(n):
@@ -284,13 +282,12 @@
     own, other = pl.pallas_call(
         pack_kernel,
         out_shape=(pages(HOME + CAP), pages(GIVEN + CAP)),
-        in_specs=[VMEM, SMEM, ANY],
+        in_specs=[VMEM, SMEM],
         out_specs=(VMEM, VMEM),
         scratch_shapes=[pltpu.SMEM((kv_size,), jnp.int32)],
         name="pack",
-    )(move_cache, owners, parts)
+    )(move_cache, owners)
     got = swap(other)
-    parts = lax.all_to_all(parts, "kv", split_axis=0, concat_axis=0, tiled=True)
     def copies(kernel, name, out_pages, count, *args, out=ANY):
         return pl.pallas_call(
             kernel,
@@ -304,21 +301,39 @@
         )(*args)
 
     (six,) = copies(merge_six_kernel, "merge_six", (5 * QUAD,), 2, own, got)
-    (three,) = copies(merge_three_kernel, "merge_three", (6 * QUAD,), 2, own, got, six)
+    six_up = shift(six, 6)
+    parts = pl.pallas_call(
+        attend_kernel,
+        out_shape=jax.ShapeDtypeStruct((kv_size, 16, HD), BF16),
+        in_specs=[VMEM, VMEM, VMEM, SMEM, SMEM, VMEM, VMEM, ANY],
+        out_specs=VMEM,
+        name="attend",
+    )(queries, res_cache, move_cache, res_count, move_request, owners[None, :], move_request[None, :], six)
+    (three,) = copies(merge_three_kernel, "merge_three", (6 * QUAD,), 2, own, got, parts)
+    three_up = shift(three, 3)
+    parts = lax.all_to_all(parts, "kv", split_axis=0, concat_axis=0, tiled=True)
+    fill = pl.pallas_call(
+        fill_kernel,
+        out_shape=jax.ShapeDtypeStruct((8, 128), F32),
+        in_specs=[ANY],
+        out_specs=VMEM,
+        cost_estimate=pl.CostEstimate(flops=100000000000, bytes_accessed=1000000, transcendentals=0),
+        name="fill",
+    )(res_count)
     part, landed_ids = pl.pallas_call(
         column_kernel,
         out_shape=(
             jax.ShapeDtypeStruct((tp_size, 16, HD), BF16),
             jax.ShapeDtypeStruct((1, kv_size * CAP), jnp.int32),
         ),
-        in_specs=[ANY, ANY],
+        in_specs=[ANY, ANY, ANY],
         out_specs=(VMEM, VMEM),
         scratch_shapes=[pltpu.VMEM(parts.shape, BF16)],
         compiler_params=pltpu.CompilerParams(vmem_limit_bytes=SMALL),
         name="column",
         cost_estimate=pl.CostEstimate(flops=0, bytes_accessed=1024, transcendentals=0),
-    )(parts, three)
-    six, three = shift(six, 6), shift(three, 3)
+    )(parts, three, fill)
+    six, three = six_up, three_up
     columns = lax.all_to_all(part, "tp", split_axis=0, concat_axis=0, tiled=True)
     half = out_weight.shape[1] // 2
     partial_out = pl.pallas_call(

time: 105 us -> 116 us (1.10)
  the two profiles are of different devices: /device:TPU:21 before, /device:TPU:1 now
where the time goes in v6:
time: 116 us; the launch traced here: 115 us
  starting transfers between devices  54.5 us (47%)
  waiting for transfers between devices  26.3 us (23%)
  blocking collectives  16.9 us (15%)
  Pallas kernels  14.4 us (12%)
  local copies, waits for them, and re-layouts  2.36 us (2%)
    ppermute x4, starting transfers between devices, shift(): return lax.ppermute(x, 'kv', pairs)  24.1 us
    all_to_all x1, blocking collectives, local(): lax.all_to_all(part, 'tp', split_axis=0, concat_axis=0, tiled=True)  15.1 us
    all_to_all x1, waiting for transfers between devices, local(): parts = lax.all_to_all(parts, 'kv', split_axis=0, concat_axis=0, tiled=True)  13.6 us
    all_to_all x1, starting transfers between devices, local(): lax.all_to_all(partial_out.reshape(kv_size, B, half), 'kv', split_axis=0,...  13 us
    ppermute x2, starting transfers between devices, swap(): return lax.ppermute(x, 'kv', [(i, i ^ 1) for i in range(kv_size)])  11.1 us
    all_to_all x1, starting transfers between devices, local(): parts = lax.all_to_all(parts, 'kv', split_axis=0, concat_axis=0, tiled=True)  6.4 us
    all_to_all x1, waiting for transfers between devices, local(): lax.all_to_all(partial_out.reshape(kv_size, B, half), 'kv', split_axis=0,...  6.32 us
    pallas_call x5, Pallas kernels, copies(): pl.pallas_call(kernel, out_shape=tuple((pages(n) for n in out_pages)), in...  5.47 us
  transfers between devices with their start and end apart: 8, of which 4 were waited for; matrix products, arithmetic and copies ran while one was open for 0% of the time, Pallas kernels for 6%

profile of v6, /device:TPU:1, one launch (start us, length us, event | category | flops | bytes accessed | tf_op | source)
XLA Modules:
  0.0 115.3 jit_solution(5607440898508488910)
XLA Ops:
  0.6 3.1 %pack.1 = (bf16[34,2,8,512]{3,2,1,0:T(8,128)(2,1)}, bf16[30,2,8,512]{3,2,1,0:T(8,128)(2,1)}) custom-call(bf16[32,2,8,512]{3,2,1,0:T(8,128)(2,1)} %move_ref.3, s32[32]{0:T(128)} %bitcast.6), custom_call_target="tpu_custom_call" | custom-call | tf_op jit(solution)/shard_map/pack/pallas_call | solution.py:282
  3.7 8.8 %collective-permute-start = (bf16[30,2,8,512]{3,2,1,0:T(8,128)(2,1)}, bf16[30,2,8,512]{3,2,1,0:T(8,128)(2,1)S(1)}, u32[]{:S(2)}, u32[]{:S(2)}) collective-permute-start(bf16[30,2,8,512]{3,2,1,0:T(8,128)(2,1)} %get-tuple-element.10), channel_id=1, source_target_pairs={{0,16},{16,0},{32,48},{48,32},{64,80},{80,64},{96,112},{112,96},{1... | collective-permute-start | bytes 1474568 | tf_op jit(solution)/shard_map/ppermute | solution.py:280
  12.5 1.7 %collective-permute-done.got_ref = bf16[30,2,8,512]{3,2,1,0:T(8,128)(2,1)S(1)} collective-permute-done((bf16[30,2,8,512]{3,2,1,0:T(8,128)(2,1)}, bf16[30,2,8,512]{3,2,1,0:T(8,128)(2,1)S(1)}, u32[]{:S(2)}, u32[]{:S(2)}) %collective-permute-start) | collective-permute-done | bytes 491552 | tf_op jit(solution)/shard_map/ppermute | solution.py:280
  14.1 0.0 copy-start
  14.2 1.1 copy-done
  15.2 0.4 merge_six.1.after_ref
  15.6 0.0 copy-start.2
  15.6 9.2 %collective-permute-start.2 = (bf16[20,2,8,512]{3,2,1,0:T(8,128)(2,1)S(1)}, bf16[20,2,8,512]{3,2,1,0:T(8,128)(2,1)S(1)}, u32[]{:S(2)}, u32[]{:S(2)}) collective-permute-start(bf16[20,2,8,512]{3,2,1,0:T(8,128)(2,1)S(1)} %merge_six.1.after_ref), channel_id=1, source_target_pairs={{0,192},{16,336},{32,224},{48,368},{64,256},{80,400},{96,288},{112... | collective-permute-start | bytes 983048 | tf_op jit(solution)/shard_map/ppermute | solution.py:277
  24.8 0.0 copy-done.2
  24.8 0.0 copy-start.1
  24.8 3.2 %attend.1.after_ref = bf16[32,16,128]{2,1,0:T(8,128)(2,1)} custom-call(bf16[4,8192]{1,0:T(4,128)(2,1)} %q_ref.1, bf16[32,2,8,512]{3,2,1,0:T(8,128)(2,1)} %res_ref.1, bf16[32,2,8,512]{3,2,1,0:T(8,128)(2,1)} %move_ref.3, s32[1,4]{1,0:T(1,128)} %after_ref.1, s32[32]{0:T(128)} %request_ref.1, s32[1,32]{1,0:T(1,128)} %bitcast.7, s32[1,32]{1,0:T(1,128)} %bitcast.5, ...), custom_call_target="tpu_custom_call" | custom-call | tf_op jit(solution)/shard_map/attend/pallas_call | solution.py:305
  28.0 0.0 copy-start.3
  28.0 6.4 %all-to-all-start = ((bf16[32,16,128]{2,1,0:T(8,128)(2,1)}), bf16[32,16,128]{2,1,0:T(8,128)(2,1)S(1)}, u32[]{:S(2)}, u32[]{:S(2)}) async-start(bf16[32,16,128]{2,1,0:T(8,128)(2,1)} %attend.1.after_ref), calls=%async_computation | async-start | bytes 262144 | tf_op jit(solution)/shard_map/all_to_all | solution.py:314
  34.4 0.0 copy-done.1
  34.4 0.0 copy-done.3
  34.4 0.5 merge_three.1.after_ref
  35.0 6.4 %collective-permute-start.1 = (bf16[24,2,8,512]{3,2,1,0:T(8,128)(2,1)S(1)}, bf16[24,2,8,512]{3,2,1,0:T(8,128)(2,1)S(1)}, u32[]{:S(2)}, u32[]{:S(2)}) collective-permute-start(bf16[24,2,8,512]{3,2,1,0:T(8,128)(2,1)S(1)} %merge_three.1.after_ref), channel_id=1, source_target_pairs={{0,96},{16,432},{32,128},{48,464},{64,160},{80,496},{96,192},{112,... | collective-permute-start | bytes 1179656 | tf_op jit(solution)/shard_map/ppermute | solution.py:277
  41.3 0.6 fill.1.fill_ref
  41.9 0.0 copy-start.4
  41.9 13.6 %all-to-all-done.parts_any = bf16[32,16,128]{2,1,0:T(8,128)(2,1)S(1)} async-done(((bf16[32,16,128]{2,1,0:T(8,128)(2,1)}), bf16[32,16,128]{2,1,0:T(8,128)(2,1)S(1)}, u32[]{:S(2)}, u32[]{:S(2)}) %all-to-all-start) | async-done | bytes 131104 | tf_op jit(solution)/shard_map/all_to_all | solution.py:314
  55.5 0.0 copy-start.5
  55.5 0.7 copy-done.5
  56.2 0.9 column.1
  57.1 15.1 %all_to_all.15.parts_any = bf16[16,16,128]{2,1,0:T(8,128)(2,1)S(1)} all-to-all(bf16[16,16,128]{2,1,0:T(8,128)(2,1)S(1)} %get-tuple-element.11), channel_id=1, replica_groups=mesh['kv'=32,'tp'=16] {'tp'}, dimensions={0} | all-to-all | bytes 131072 | tf_op jit(solution)/shard_map/all_to_all | solution.py:337
  72.1 0.0 copy-done.4
  72.1 1.1 project.1.after_ref
  73.2 13.0 %all-to-all-start.2 = ((bf16[32,4,512]{2,1,0:T(4,128)(2,1)}), bf16[32,4,512]{2,1,0:T(4,128)(2,1)S(1)}, u32[]{:S(2)}, u32[]{:S(2)}) async-start(bf16[32,4,512]{2,1,0:T(4,128)(2,1)} %bitcast.3), calls=%async_computation.2 | async-start | bytes 262144 | tf_op jit(solution)/shard_map/all_to_all | solution.py:349
  86.2 0.0 collective-permute-done.2.six_ref
  86.2 0.0 collective-permute-done.1.three_ref
  86.2 1.1 forward.1
  87.3 4.6 %collective-permute-start.3 = (bf16[24,2,8,512]{3,2,1,0:T(8,128)(2,1)S(1)}, bf16[24,2,8,512]{3,2,1,0:T(8,128)(2,1)S(1)}, u32[]{:S(2)}, u32[]{:S(2)}) collective-permute-start(bf16[24,2,8,512]{3,2,1,0:T(8,128)(2,1)S(1)} %get-tuple-element.12), channel_id=1, source_target_pairs={{0,32},{16,496},{32,64},{48,16},{64,96},{80,48},{96,128},{112,80},... | collective-permute-start | bytes 1179656 | tf_op jit(solution)/shard_map/ppermute | solution.py:277
  91.9 4.0 %collective-permute-start.4 = (bf16[20,2,8,512]{3,2,1,0:T(8,128)(2,1)S(1)}, bf16[20,2,8,512]{3,2,1,0:T(8,128)(2,1)S(1)}, u32[]{:S(2)}, u32[]{:S(2)}) collective-permute-start(bf16[20,2,8,512]{3,2,1,0:T(8,128)(2,1)S(1)} %get-tuple-element.13), channel_id=1, source_target_pairs={{0,64},{16,464},{32,96},{48,496},{64,128},{80,16},{96,160},{112,48... | collective-permute-start | bytes 983048 | tf_op jit(solution)/shard_map/ppermute | solution.py:277
  95.8 6.3 %all-to-all-done.2.parts_any = bf16[32,4,512]{2,1,0:T(4,128)(2,1)S(1)} async-done(((bf16[32,4,512]{2,1,0:T(4,128)(2,1)}), bf16[32,4,512]{2,1,0:T(4,128)(2,1)S(1)}, u32[]{:S(2)}, u32[]{:S(2)}) %all-to-all-start.2) | async-done | bytes 131104 | tf_op jit(solution)/shard_map/all_to_all | solution.py:349
  102.2 0.2 add.1.after_ref
  102.4 4.7 %collective-permute-done.4.two_ref = bf16[20,2,8,512]{3,2,1,0:T(8,128)(2,1)S(1)} collective-permute-done((bf16[20,2,8,512]{3,2,1,0:T(8,128)(2,1)S(1)}, bf16[20,2,8,512]{3,2,1,0:T(8,128)(2,1)S(1)}, u32[]{:S(2)}, u32[]{:S(2)}) %collective-permute-start.4) | collective-permute-done | bytes 327712 | tf_op jit(solution)/shard_map/ppermute | solution.py:277
  107.1 0.0 collective-permute-done.3.one_ref
  107.1 0.8 give.1
  107.8 2.3 %collective-permute-start.5 = (bf16[30,2,8,512]{3,2,1,0:T(8,128)(2,1)S(1)}, bf16[30,2,8,512]{3,2,1,0:T(8,128)(2,1)S(1)}, u32[]{:S(2)}, u32[]{:S(2)}) collective-permute-start(bf16[30,2,8,512]{3,2,1,0:T(8,128)(2,1)S(1)} %give.1), channel_id=1, source_target_pairs={{0,16},{16,0},{32,48},{48,32},{64,80},{80,64},{96,112},{112,96},{1... | collective-permute-start | bytes 1474568 | tf_op jit(solution)/shard_map/ppermute | solution.py:280
  110.2 1.8 %all_gather.3 = bf16[4,1024]{1,0:T(4,128)(2,1)S(1)} all-gather(bf16[4,512]{1,0:T(4,128)(2,1)S(1)} %add.1.after_ref), channel_id=1, replica_groups={{0,16},{32,48},{64,80},{96,112},{128,144},{160,176},{192,208},{224,240}..., dimensions={1}, use_global_device_ids=true | all-gather | bytes 12288 | tf_op jit(solution)/shard_map/all_gather | solution.py:363
  112.0 0.0 collective-permute-done.5.taken_ref
  112.0 2.7 %land.1 = bf16[64,2,8,512]{3,2,1,0:T(8,128)(2,1)} custom-call(bf16[34,2,8,512]{3,2,1,0:T(8,128)(2,1)S(1)} %copy-done.1, bf16[30,2,8,512]{3,2,1,0:T(8,128)(2,1)S(1)} %collective-permute-done.got_ref, bf16[24,2,8,512]{3,2,1,0:T(8,128)(2,1)S(1)} %collective-permute-done.1.three_ref, bf16[20,2,8,512]{3,2,1,0:T(8,128)(2,1)S(1)} %collective-permute-done.2.six_ref, ...), custom_call_target="tpu_custom_call" | custom-call | bytes 1024 | tf_op jit(solution)/shard_map/land/pallas_call | solution.py:292
  114.7 0.6 copy.11
Async XLA Ops:
  3.7 10.5 %collective-permute-start = (bf16[30,2,8,512]{3,2,1,0:T(8,128)(2,1)}, bf16[30,2,8,512]{3,2,1,0:T(8,128)(2,1)S(1)}, u32[]{:S(2)}, u32[]{:S(2)}) collective-permute-start(bf16[30,2,8,512]{3,2,1,0:T(8,128)(2,1)} %get-tuple-element.10), channel_id=1, source_target_pairs={{0,16},{16,0},{32,48},{48,32},{64,80},{80,64},{96,112},{112,96},{1... | collective-permute-start | bytes 1474568 | tf_op jit(solution)/shard_map/ppermute | solution.py:280
  14.1 1.1 copy-start
  15.6 9.2 %copy-start.2 = (bf16[20,2,8,512]{3,2,1,0:T(8,128)(2,1)}, bf16[20,2,8,512]{3,2,1,0:T(8,128)(2,1)S(1)}, u32[]{:S(2)}) copy-start(bf16[20,2,8,512]{3,2,1,0:T(8,128)(2,1)S(1)} %merge_six.1.after_ref) | copy-start | bytes 983044
  15.6 70.6 %collective-permute-start.2 = (bf16[20,2,8,512]{3,2,1,0:T(8,128)(2,1)S(1)}, bf16[20,2,8,512]{3,2,1,0:T(8,128)(2,1)S(1)}, u32[]{:S(2)}, u32[]{:S(2)}) collective-permute-start(bf16[20,2,8,512]{3,2,1,0:T(8,128)(2,1)S(1)} %merge_six.1.after_ref), channel_id=1, source_target_pairs={{0,192},{16,336},{32,224},{48,368},{64,256},{80,400},{96,288},{112... | collective-permute-start | bytes 983048 | tf_op jit(solution)/shard_map/ppermute | solution.py:277
  24.8 9.6 %copy-start.1 = (bf16[34,2,8,512]{3,2,1,0:T(8,128)(2,1)S(1)}, bf16[34,2,8,512]{3,2,1,0:T(8,128)(2,1)}, u32[]{:S(2)}) copy-start(bf16[34,2,8,512]{3,2,1,0:T(8,128)(2,1)} %get-tuple-element.9.own_ref) | copy-start | bytes 1671172
  28.0 6.4 %copy-start.3 = (bf16[32,16,128]{2,1,0:T(8,128)(2,1)S(1)}, bf16[32,16,128]{2,1,0:T(8,128)(2,1)}, u32[]{:S(2)}) copy-start(bf16[32,16,128]{2,1,0:T(8,128)(2,1)} %attend.1.after_ref) | copy-start | bytes 393220
  28.0 27.5 %all-to-all-start = ((bf16[32,16,128]{2,1,0:T(8,128)(2,1)}), bf16[32,16,128]{2,1,0:T(8,128)(2,1)S(1)}, u32[]{:S(2)}, u32[]{:S(2)}) async-start(bf16[32,16,128]{2,1,0:T(8,128)(2,1)} %attend.1.after_ref), calls=%async_computation | async-start | bytes 262144 | tf_op jit(solution)/shard_map/all_to_all | solution.py:314
  35.0 51.2 %collective-permute-start.1 = (bf16[24,2,8,512]{3,2,1,0:T(8,128)(2,1)S(1)}, bf16[24,2,8,512]{3,2,1,0:T(8,128)(2,1)S(1)}, u32[]{:S(2)}, u32[]{:S(2)}) collective-permute-start(bf16[24,2,8,512]{3,2,1,0:T(8,128)(2,1)S(1)} %merge_three.1.after_ref), channel_id=1, source_target_pairs={{0,96},{16,432},{32,128},{48,464},{64,160},{80,496},{96,192},{112,... | collective-permute-start | bytes 1179656 | tf_op jit(solution)/shard_map/ppermute | solution.py:277
  41.9 30.2 %copy-start.4 = (bf16[256,1024]{1,0:T(8,128)(2,1)S(1)}, bf16[256,1024]{1,0:T(8,128)(2,1)}, u32[]{:S(2)}) copy-start(bf16[256,1024]{1,0:T(8,128)(2,1)} %weight_ref.1) | copy-start | bytes 1572868
  55.5 0.7 copy-start.5
  73.2 29.0 %all-to-all-start.2 = ((bf16[32,4,512]{2,1,0:T(4,128)(2,1)}), bf16[32,4,512]{2,1,0:T(4,128)(2,1)S(1)}, u32[]{:S(2)}, u32[]{:S(2)}) async-start(bf16[32,4,512]{2,1,0:T(4,128)(2,1)} %bitcast.3), calls=%async_computation.2 | async-start | bytes 262144 | tf_op jit(solution)/shard_map/all_to_all | solution.py:349
  87.3 19.8 %collective-permute-start.3 = (bf16[24,2,8,512]{3,2,1,0:T(8,128)(2,1)S(1)}, bf16[24,2,8,512]{3,2,1,0:T(8,128)(2,1)S(1)}, u32[]{:S(2)}, u32[]{:S(2)}) collective-permute-start(bf16[24,2,8,512]{3,2,1,0:T(8,128)(2,1)S(1)} %get-tuple-element.12), channel_id=1, source_target_pairs={{0,32},{16,496},{32,64},{48,16},{64,96},{80,48},{96,128},{112,80},... | collective-permute-start | bytes 1179656 | tf_op jit(solution)/shard_map/ppermute | solution.py:277
  91.9 15.2 %collective-permute-start.4 = (bf16[20,2,8,512]{3,2,1,0:T(8,128)(2,1)S(1)}, bf16[20,2,8,512]{3,2,1,0:T(8,128)(2,1)S(1)}, u32[]{:S(2)}, u32[]{:S(2)}) collective-permute-start(bf16[20,2,8,512]{3,2,1,0:T(8,128)(2,1)S(1)} %get-tuple-element.13), channel_id=1, source_target_pairs={{0,64},{16,464},{32,96},{48,496},{64,128},{80,16},{96,160},{112,48... | collective-permute-start | bytes 983048 | tf_op jit(solution)/shard_map/ppermute | solution.py:277
  107.8 4.1 %collective-permute-start.5 = (bf16[30,2,8,512]{3,2,1,0:T(8,128)(2,1)S(1)}, bf16[30,2,8,512]{3,2,1,0:T(8,128)(2,1)S(1)}, u32[]{:S(2)}, u32[]{:S(2)}) collective-permute-start(bf16[30,2,8,512]{3,2,1,0:T(8,128)(2,1)S(1)} %give.1), channel_id=1, source_target_pairs={{0,16},{16,0},{32,48},{48,32},{64,80},{80,64},{96,112},{112,96},{1... | collective-permute-start | bytes 1474568 | tf_op jit(solution)/shard_map/ppermute | solution.py:280

commit v7 on v6

--- a/solution.py
+++ b/solution.py
@@ -43,8 +43,7 @@
     return jnp.where(lane == 0, shift, jnp.where(lane == 1, high, jnp.where(lane == 4, weight_sum - high, 0.0)))
 
 
-def attend_kernel(q_ref, res_ref, move_ref, count_ref, request_ref, owner_ref, request_row_ref, after_ref, out_ref):
-    del after_ref
+def attend_kernel(q_ref, res_ref, move_ref, count_ref, request_ref, owner_ref, request_row_ref, out_ref):
     rows = GROUP * B
     n_res, n_move = res_ref.shape[0], move_ref.shape[0]
     page = iota((8, n_res * PAGE), 1) // PAGE
@@ -118,7 +117,7 @@
     return ref.at[pl.ds(first * QUAD, count * QUAD)]
 
 
-def pack_kernel(move_ref, owner_ref, own_ref, other_ref, used_ref):
+def pack_kernel(move_ref, owner_ref, own_out, other_out, own_ref, other_ref, used_ref, sems):
     own_ref[...] = jnp.zeros(own_ref.shape, own_ref.dtype)
     other_ref[...] = jnp.zeros(other_ref.shape, other_ref.dtype)
     for o in range(used_ref.shape[0]):
@@ -149,53 +148,54 @@
         return carry
 
     lax.fori_loop(0, move_ref.shape[0], place, 0)
-
-
-def merge_six_kernel(own_ref, got_ref, out_ref, sems):
-    pairs = [(quads(own_ref, 5, 3), quads(out_ref, 0, 3)), (quads(got_ref, 5, 2), quads(out_ref, 3, 2))]
-    copy_all(pairs, sems)
-
-
-def merge_three_kernel(own_ref, got_ref, after_ref, out_ref, sems):
-    del after_ref
-    pairs = [(quads(own_ref, 2, 3), quads(out_ref, 0, 3)), (quads(got_ref, 2, 3), quads(out_ref, 3, 3))]
-    copy_all(pairs, sems)
-
-
-def forward_kernel(own_ref, got_ref, three_ref, six_ref, after_ref, one_ref, two_ref, sems):
+    copy_all([(own_ref, own_out), (other_ref, other_out)], sems)
+
+
+def short_kernel(own_ref, got_ref, after_ref, one_ref, two_ref, sems):
     del after_ref
     copies = []
     for n, ref in enumerate((one_ref, two_ref)):
-        parts = [(own_ref, n), (got_ref, n), (three_ref, 1 + n), (three_ref, 4 + n), (six_ref, 1 + n)]
-        parts += [(six_ref, 4)] if n == 0 else []
-        copies += [(quads(source, first), quads(ref, to)) for to, (source, first) in enumerate(parts)]
+        for m in range(3):
+            copies.append((quads(own_ref, n + 3 * m), quads(ref, 2 * m)))
+            if n + 3 * m < FAR - 1:
+                copies.append((quads(got_ref, n + 3 * m), quads(ref, 2 * m + 1)))
     copy_all(copies, sems)
 
 
-def arrived(three_ref, six_ref, one_ref, two_ref):
+def long_kernel(own_ref, got_ref, one_ref, two_ref, three_ref, six_ref, sems):
+    copies = []
+    for n, ref in enumerate((three_ref, six_ref)):
+        own = 2 + 3 * n
+        copies += [(quads(own_ref, own), quads(ref, 0)), (quads(got_ref, own), quads(ref, 1))]
+        copies.append((quads(one_ref, 2 + 2 * n, 2), quads(ref, 2, 2)))
+        count = 2 - n
+        copies.append((quads(two_ref, 2 + 2 * n, count), quads(ref, 4, count)))
+    copy_all(copies, sems)
+
+
+def arrived(one_ref, two_ref, three_ref, six_ref):
     return (
-        (1, one_ref, 0, 1),
-        (2, two_ref, 0, 1),
-        (3, three_ref, 0, 3),
-        (4, one_ref, 2, 3),
-        (5, two_ref, 2, 3),
-        (6, six_ref, 0, 3),
-        (7, one_ref, 4, 5),
+        (1, one_ref, 0),
+        (2, two_ref, 0),
+        (3, three_ref, 0),
+        (4, three_ref, 2),
+        (5, three_ref, 4),
+        (6, six_ref, 0),
+        (7, six_ref, 2),
     )
 
 
-def give_kernel(three_ref, six_ref, one_ref, two_ref, after_ref, out_ref, sems):
-    del after_ref
+def give_kernel(one_ref, two_ref, three_ref, six_ref, out_ref, sems):
     core = lax.axis_index("kv") % 2
-    copies = [(two_ref.at[pl.ds(4 * QUAD + CAP, CAP)], out_ref.at[pl.ds(GIVEN, CAP)])]
-    for distance, ref, same, other in arrived(three_ref, six_ref, one_ref, two_ref):
-        for quad, start in ((same, core), (other, 1 - core)):
+    copies = [(six_ref.at[pl.ds(4 * QUAD + CAP, CAP)], out_ref.at[pl.ds(GIVEN, CAP)])]
+    for distance, ref, quad in arrived(one_ref, two_ref, three_ref, six_ref):
+        for quad, start in ((quad, core), (quad + 1, 1 - core)):
             to = out_ref.at[pl.ds((distance - 1) * QUAD + start * CAP, CAP)]
             copies.append((ref.at[pl.ds(quad * QUAD + CAP, CAP)], to))
     copy_all(copies, sems)
 
 
-def land_kernel(own_ref, got_ref, three_ref, six_ref, one_ref, two_ref, taken_ref, out_ref, sems):
+def land_kernel(own_ref, got_ref, one_ref, two_ref, three_ref, six_ref, taken_ref, out_ref, passed_ref, sems):
     me = lax.axis_index("kv")
     chip, core = me // 2, me % 2
     way = 1 - 2 * core
@@ -206,11 +206,11 @@
     copies = [
         (own_ref.at[pl.ds(HOME, CAP)], rows(0, core)),
         (got_ref.at[pl.ds(GIVEN, CAP)], rows(0, 1 - core)),
-        (two_ref.at[pl.ds(4 * QUAD, CAP)], rows(FAR, core)),
+        (six_ref.at[pl.ds(4 * QUAD, CAP)], rows(FAR, core)),
         (taken_ref.at[pl.ds(GIVEN, CAP)], rows(FAR, 1 - core)),
     ]
-    for distance, ref, same, other in arrived(three_ref, six_ref, one_ref, two_ref):
-        for quad, start in ((same, core), (other, 1 - core)):
+    for distance, ref, quad in arrived(one_ref, two_ref, three_ref, six_ref):
+        for quad, start in ((quad, core), (quad + 1, 1 - core)):
             copies.append((ref.at[pl.ds(quad * QUAD, CAP)], rows(-way * distance, start)))
         to = out_ref.at[pl.ds(((chip + way * distance) & (CHIPS - 1)) * QUAD, QUAD)]
         copies.append((quads(taken_ref, distance - 1), to))
@@ -225,13 +225,12 @@
     return shift, jnp.sum(sums * factor, axis=0), jnp.sum(values * factor, axis=0)
 
 
-def fill_kernel(after_ref, out_ref):
+def fill_kernel(*refs):
+    del refs
+
+
+def column_kernel(parts_any, after_ref, out_ref, ids_ref, parts_ref):
     del after_ref
-    out_ref[...] = jnp.zeros(out_ref.shape, F32)
-
-
-def column_kernel(parts_any, after_ref, fill_ref, out_ref, ids_ref, parts_ref):
-    del after_ref, fill_ref
     pltpu.sync_copy(parts_any, parts_ref)
     parts = parts_ref[...].astype(F32)
     shift, weight_sum, values = combined(parts)
@@ -259,7 +258,8 @@
         out_ref[:, core] = jnp.broadcast_to(part[None], (out_ref.shape[0],) + part.shape)
 
 
-def add_kernel(parts_any, out_ref, parts_ref):
+def add_kernel(parts_any, after_ref, out_ref, parts_ref):
+    del after_ref
     pltpu.sync_copy(parts_any, parts_ref)
     out_ref[...] = jnp.sum(parts_ref[...].astype(F32), axis=0).astype(out_ref.dtype)
 
@@ -283,56 +283,64 @@
         pack_kernel,
         out_shape=(pages(HOME + CAP), pages(GIVEN + CAP)),
         in_specs=[VMEM, SMEM],
-        out_specs=(VMEM, VMEM),
-        scratch_shapes=[pltpu.SMEM((kv_size,), jnp.int32)],
+        out_specs=(ANY, ANY),
+        scratch_shapes=[
+            pltpu.VMEM((HOME + CAP,) + page, BF16),
+            pltpu.VMEM((GIVEN + CAP,) + page, BF16),
+            pltpu.SMEM((kv_size,), jnp.int32),
+            pltpu.SemaphoreType.DMA((2,)),
+        ],
+        compiler_params=pltpu.CompilerParams(vmem_limit_bytes=SMALL),
         name="pack",
     )(move_cache, owners)
     got = swap(other)
-    def copies(kernel, name, out_pages, count, *args, out=ANY):
+    def copies(kernel, name, out_pages, count, *args):
         return pl.pallas_call(
             kernel,
             out_shape=tuple(pages(n) for n in out_pages),
             in_specs=[ANY] * len(args),
-            out_specs=(out,) * len(out_pages),
+            out_specs=(ANY,) * len(out_pages),
             scratch_shapes=[pltpu.SemaphoreType.DMA((count,))],
             compiler_params=pltpu.CompilerParams(vmem_limit_bytes=SMALL),
             cost_estimate=pl.CostEstimate(flops=0, bytes_accessed=1024, transcendentals=0),
             name=name,
         )(*args)
 
-    (six,) = copies(merge_six_kernel, "merge_six", (5 * QUAD,), 2, own, got)
-    six_up = shift(six, 6)
     parts = pl.pallas_call(
         attend_kernel,
         out_shape=jax.ShapeDtypeStruct((kv_size, 16, HD), BF16),
-        in_specs=[VMEM, VMEM, VMEM, SMEM, SMEM, VMEM, VMEM, ANY],
+        in_specs=[VMEM, VMEM, VMEM, SMEM, SMEM, VMEM, VMEM],
         out_specs=VMEM,
         name="attend",
-    )(queries, res_cache, move_cache, res_count, move_request, owners[None, :], move_request[None, :], six)
-    (three,) = copies(merge_three_kernel, "merge_three", (6 * QUAD,), 2, own, got, parts)
-    three_up = shift(three, 3)
+    )(queries, res_cache, move_cache, res_count, move_request, owners[None, :], move_request[None, :])
+    one, two = copies(short_kernel, "short", (6 * QUAD, 5 * QUAD), 11, own, got, parts)
+    one, two = shift(one, 1), shift(two, 2)
     parts = lax.all_to_all(parts, "kv", split_axis=0, concat_axis=0, tiled=True)
-    fill = pl.pallas_call(
+    three, six = copies(long_kernel, "long", (6 * QUAD, 5 * QUAD), 8, own, got, one, two)
+    six_up, three_up = shift(six, 6), shift(three, 3)
+    own = pl.pallas_call(
         fill_kernel,
-        out_shape=jax.ShapeDtypeStruct((8, 128), F32),
+        out_shape=pages(HOME + CAP),
         in_specs=[ANY],
-        out_specs=VMEM,
-        cost_estimate=pl.CostEstimate(flops=100000000000, bytes_accessed=1000000, transcendentals=0),
+        out_specs=ANY,
+        input_output_aliases={0: 0},
+        compiler_params=pltpu.CompilerParams(vmem_limit_bytes=SMALL),
+        cost_estimate=pl.CostEstimate(flops=10**11, bytes_accessed=1024, transcendentals=0),
         name="fill",
-    )(res_count)
+    )(own)
     part, landed_ids = pl.pallas_call(
         column_kernel,
         out_shape=(
             jax.ShapeDtypeStruct((tp_size, 16, HD), BF16),
             jax.ShapeDtypeStruct((1, kv_size * CAP), jnp.int32),
         ),
-        in_specs=[ANY, ANY, ANY],
+        in_specs=[ANY, ANY],
         out_specs=(VMEM, VMEM),
         scratch_shapes=[pltpu.VMEM(parts.shape, BF16)],
         compiler_params=pltpu.CompilerParams(vmem_limit_bytes=SMALL),
         name="column",
         cost_estimate=pl.CostEstimate(flops=0, bytes_accessed=1024, transcendentals=0),
-    )(parts, three, fill)
+    )(parts, own)
     six, three = six_up, three_up
     columns = lax.all_to_all(part, "tp", split_axis=0, concat_axis=0, tiled=True)
     half = out_weight.shape[1] // 2
@@ -349,23 +357,31 @@
     partials = lax.all_to_all(
         partial_out.reshape(kv_size, B, half), "kv", split_axis=0, concat_axis=0, tiled=True
     )
+    (give,) = copies(give_kernel, "give", (GIVEN + CAP,), 15, one, two, three, six)
+    taken = swap(give)
+    landed, own = pl.pallas_call(
+        land_kernel,
+        out_shape=(pages(kv_size * CAP), pages(HOME + CAP)),
+        in_specs=[ANY] * 7,
+        out_specs=(VMEM, ANY),
+        input_output_aliases={0: 1},
+        scratch_shapes=[pltpu.SemaphoreType.DMA((25,))],
+        compiler_params=pltpu.CompilerParams(vmem_limit_bytes=SMALL),
+        cost_estimate=pl.CostEstimate(flops=0, bytes_accessed=1024, transcendentals=0),
+        name="land",
+    )(own, got, one, two, three, six, taken)
     mixed_half = pl.pallas_call(
         add_kernel,
         out_shape=jax.ShapeDtypeStruct((B, half), BF16),
-        in_specs=[ANY],
+        in_specs=[ANY, ANY],
         out_specs=VMEM,
         scratch_shapes=[pltpu.VMEM(partials.shape, BF16)],
         compiler_params=pltpu.CompilerParams(vmem_limit_bytes=SMALL),
         name="add",
         cost_estimate=pl.CostEstimate(flops=0, bytes_accessed=1024, transcendentals=0),
-    )(partials)
+    )(partials, own)
     both_cores = [[2 * z, 2 * z + 1] for z in range(CHIPS)]
     mixed = lax.all_gather(mixed_half, "kv", axis=1, tiled=True, axis_index_groups=both_cores)
-    one, two = copies(forward_kernel, "forward", (6 * QUAD, 5 * QUAD), 11, own, got, three, six, partial_out)
-    two, one = shift(two, 2), shift(one, 1)
-    (give,) = copies(give_kernel, "give", (GIVEN + CAP,), 15, three, six, one, two, mixed_half)
-    taken = swap(give)
-    (landed,) = copies(land_kernel, "land", (kv_size * CAP,), 25, own, got, three, six, one, two, taken, out=VMEM)
     return (mixed, landed, landed_ids.reshape(-1))
 
 

time: 116 us -> 94.5 us (0.81)
  waiting for transfers between devices: 26.3 us -> 13.5 us
  starting transfers between devices: 54.5 us -> 49.2 us
  blocking collectives: 16.9 us -> 15.2 us
  Pallas kernels: 14.4 us -> 13 us
    all_to_all x1, waiting for transfers between devices: 13.6 us -> 0.32 us  [local(): parts = lax.all_to_all(parts, 'kv', split_axis=0, concat_axis=0, tiled=True)]
    ppermute x4, waiting for transfers between devices: 4.71 us -> 11.7 us  [shift(): return lax.ppermute(x, 'kv', pairs)]
    all_to_all x1, waiting for transfers between devices: 6.32 us -> 0.01 us  [local(): lax.all_to_all(partial_out.reshape(kv_size, B, half), 'kv', split_axis=0,...]
    all_to_all x1, starting transfers between devices: 13 us -> 6.72 us  [local(): lax.all_to_all(partial_out.reshape(kv_size, B, half), 'kv', split_axis=0,...]
    ppermute x4, starting transfers between devices: 24.1 us -> 21.7 us  [shift(): return lax.ppermute(x, 'kv', pairs)]
    pallas_call x5 -> x3, Pallas kernels: 5.47 us -> 3.09 us  [copies(): pl.pallas_call(kernel, out_shape=tuple((pages(n) for n in out_pages)), in...]
    ppermute x2, starting transfers between devices: 11.1 us -> 13.4 us  [swap(): return lax.ppermute(x, 'kv', [(i, i ^ 1) for i in range(kv_size)])]
    pallas_call x1 -> x2, Pallas kernels: 0.6 us -> 2.67 us  [the longest x1 2.67 us: local(): pl.pallas_call(land_kernel, out_shape=(pages(kv_size * CAP), pages(HOME +...]
  transfers between devices with their start and end apart: 8 -> 8, of which waited for: 4 -> 4; matrix products, arithmetic and copies ran while one was open for 0% -> 0% of each run, Pallas kernels for 6% -> 10%
where the time goes in v7:
time: 94.5 us; the launch traced here: 94 us
  starting transfers between devices  49.2 us (52%)
  blocking collectives  15.2 us (16%)
  waiting for transfers between devices  13.5 us (14%)
  Pallas kernels  13 us (14%)
  local copies, waits for them, and re-layouts  2.3 us (2%)
    ppermute x4, starting transfers between devices, shift(): return lax.ppermute(x, 'kv', pairs)  21.7 us
    ppermute x2, starting transfers between devices, swap(): return lax.ppermute(x, 'kv', [(i, i ^ 1) for i in range(kv_size)])  13.4 us
    all_to_all x1, blocking collectives, local(): lax.all_to_all(part, 'tp', split_axis=0, concat_axis=0, tiled=True)  13.3 us
    ppermute x4, waiting for transfers between devices, shift(): return lax.ppermute(x, 'kv', pairs)  11.7 us
    all_to_all x1, starting transfers between devices, local(): parts = lax.all_to_all(parts, 'kv', split_axis=0, concat_axis=0, tiled=True)  7.38 us
    all_to_all x1, starting transfers between devices, local(): lax.all_to_all(partial_out.reshape(kv_size, B, half), 'kv', split_axis=0,...  6.72 us
    pallas_call x1, Pallas kernels, local(): pl.pallas_call(attend_kernel, out_shape=jax.ShapeDtypeStruct((kv_size, 16...  3.12 us
    pallas_call x3, Pallas kernels, copies(): pl.pallas_call(kernel, out_shape=tuple((pages(n) for n in out_pages)), in...  3.09 us
  transfers between devices with their start and end apart: 8, of which 4 were waited for; matrix products, arithmetic and copies ran while one was open for 0% of the time, Pallas kernels for 10%

profile of v7, /device:TPU:1, one launch (start us, length us, event | category | flops | bytes accessed | tf_op | source)
XLA Modules:
  0.0 94.0 jit_solution(8906882562716462285)
XLA Ops:
  0.6 0.0 copy-start.2
  0.6 0.6 copy-done.2
  1.3 0.0 copy-start
  1.3 1.0 %copy-done = bf16[32,2,8,512]{3,2,1,0:T(8,128)(2,1)S(1)} copy-done((bf16[32,2,8,512]{3,2,1,0:T(8,128)(2,1)S(1)}, bf16[32,2,8,512]{3,2,1,0:T(8,128)(2,1)}, u32[]{:S(2)}) %copy-start) | copy-done | bytes 524312
  2.3 2.0 %pack.1 = (bf16[34,2,8,512]{3,2,1,0:T(8,128)(2,1)S(1)}, bf16[30,2,8,512]{3,2,1,0:T(8,128)(2,1)S(1)}) custom-call(bf16[32,2,8,512]{3,2,1,0:T(8,128)(2,1)S(1)} %copy-done, s32[32]{0:T(128)S(1)} %bitcast.6), custom_call_target="tpu_custom_call" | custom-call | tf_op jit(solution)/shard_map/pack/pallas_call | solution.py:282
  4.3 8.8 %collective-permute-start = (bf16[30,2,8,512]{3,2,1,0:T(8,128)(2,1)S(1)}, bf16[30,2,8,512]{3,2,1,0:T(8,128)(2,1)S(1)}, u32[]{:S(2)}, u32[]{:S(2)}) collective-permute-start(bf16[30,2,8,512]{3,2,1,0:T(8,128)(2,1)S(1)} %get-tuple-element.15), channel_id=1, source_target_pairs={{0,16},{16,0},{32,48},{48,32},{64,80},{80,64},{96,112},{112,96},{1... | collective-permute-start | bytes 1474568 | tf_op jit(solution)/shard_map/ppermute | solution.py:280
  13.1 3.1 %attend.1.after_ref = bf16[32,16,128]{2,1,0:T(8,128)(2,1)} custom-call(bf16[4,8192]{1,0:T(4,128)(2,1)} %q_ref.1, bf16[32,2,8,512]{3,2,1,0:T(8,128)(2,1)} %res_ref.1, bf16[32,2,8,512]{3,2,1,0:T(8,128)(2,1)} %move_ref.3, s32[1,4]{1,0:T(1,128)} %count_ref.1, s32[32]{0:T(128)} %request_ref.1, s32[1,32]{1,0:T(1,128)} %bitcast.5, s32[1,32]{1,0:T(1,128)} %bitcast.7), custom_call_target="tpu_custom_call" | custom-call | tf_op jit(solution)/shard_map/attend/pallas_call | solution.py:309
  16.2 0.0 collective-permute-done.got_ref
  16.2 1.0 %short.1 = (bf16[24,2,8,512]{3,2,1,0:T(8,128)(2,1)S(1)}, bf16[20,2,8,512]{3,2,1,0:T(8,128)(2,1)S(1)}) custom-call(bf16[34,2,8,512]{3,2,1,0:T(8,128)(2,1)S(1)} %get-tuple-element.13.refs_0_.own_ref, bf16[30,2,8,512]{3,2,1,0:T(8,128)(2,1)S(1)} %collective-permute-done.got_ref, bf16[32,16,128]{2,1,0:T(8,128)(2,1)} %attend.1.after_ref), custom_call_target="tpu_custom_call" | custom-call | bytes 1024 | tf_op jit(solution)/shard_map/short/pallas_call | solution.py:298
  17.3 5.7 %collective-permute-start.1 = (bf16[24,2,8,512]{3,2,1,0:T(8,128)(2,1)S(1)}, bf16[24,2,8,512]{3,2,1,0:T(8,128)(2,1)S(1)}, u32[]{:S(2)}, u32[]{:S(2)}) collective-permute-start(bf16[24,2,8,512]{3,2,1,0:T(8,128)(2,1)S(1)} %get-tuple-element.16), channel_id=1, source_target_pairs={{0,32},{16,496},{32,64},{48,16},{64,96},{80,48},{96,128},{112,80},... | collective-permute-start | bytes 1179656 | tf_op jit(solution)/shard_map/ppermute | solution.py:277
  23.0 3.1 %collective-permute-start.2 = (bf16[20,2,8,512]{3,2,1,0:T(8,128)(2,1)S(1)}, bf16[20,2,8,512]{3,2,1,0:T(8,128)(2,1)S(1)}, u32[]{:S(2)}, u32[]{:S(2)}) collective-permute-start(bf16[20,2,8,512]{3,2,1,0:T(8,128)(2,1)S(1)} %get-tuple-element.17), channel_id=1, source_target_pairs={{0,64},{16,464},{32,96},{48,496},{64,128},{80,16},{96,160},{112,48... | collective-permute-start | bytes 983048 | tf_op jit(solution)/shard_map/ppermute | solution.py:277
  26.1 7.4 %all-to-all-start = ((bf16[32,16,128]{2,1,0:T(8,128)(2,1)}), bf16[32,16,128]{2,1,0:T(8,128)(2,1)S(1)}, u32[]{:S(2)}, u32[]{:S(2)}) async-start(bf16[32,16,128]{2,1,0:T(8,128)(2,1)} %attend.1.after_ref), calls=%async_computation | async-start | bytes 262144 | tf_op jit(solution)/shard_map/all_to_all | solution.py:318
  33.5 1.4 %collective-permute-done.2.two_ref = bf16[20,2,8,512]{3,2,1,0:T(8,128)(2,1)S(1)} collective-permute-done((bf16[20,2,8,512]{3,2,1,0:T(8,128)(2,1)S(1)}, bf16[20,2,8,512]{3,2,1,0:T(8,128)(2,1)S(1)}, u32[]{:S(2)}, u32[]{:S(2)}) %collective-permute-start.2) | collective-permute-done | bytes 327712 | tf_op jit(solution)/shard_map/ppermute | solution.py:277
  34.9 0.0 collective-permute-done.1.one_ref
  34.9 1.3 %long.1 = (bf16[24,2,8,512]{3,2,1,0:T(8,128)(2,1)S(1)}, bf16[20,2,8,512]{3,2,1,0:T(8,128)(2,1)}) custom-call(bf16[34,2,8,512]{3,2,1,0:T(8,128)(2,1)S(1)} %get-tuple-element.13.refs_0_.own_ref, bf16[30,2,8,512]{3,2,1,0:T(8,128)(2,1)S(1)} %collective-permute-done.got_ref, bf16[24,2,8,512]{3,2,1,0:T(8,128)(2,1)S(1)} %collective-permute-done.1.one_ref, ...), custom_call_target="tpu_custom_call" | custom-call | bytes 1024 | tf_op jit(solution)/shard_map/long/pallas_call | solution.py:298
  36.2 5.0 %collective-permute-start.3 = (bf16[24,2,8,512]{3,2,1,0:T(8,128)(2,1)S(1)}, bf16[24,2,8,512]{3,2,1,0:T(8,128)(2,1)S(1)}, u32[]{:S(2)}, u32[]{:S(2)}) collective-permute-start(bf16[24,2,8,512]{3,2,1,0:T(8,128)(2,1)S(1)} %get-tuple-element.18), channel_id=1, source_target_pairs={{0,96},{16,432},{32,128},{48,464},{64,160},{80,496},{96,192},{112,... | collective-permute-start | bytes 1179656 | tf_op jit(solution)/shard_map/ppermute | solution.py:277
  41.2 7.8 %collective-permute-start.4 = (bf16[20,2,8,512]{3,2,1,0:T(8,128)(2,1)}, bf16[20,2,8,512]{3,2,1,0:T(8,128)(2,1)S(1)}, u32[]{:S(2)}, u32[]{:S(2)}) collective-permute-start(bf16[20,2,8,512]{3,2,1,0:T(8,128)(2,1)} %get-tuple-element.19), channel_id=1, source_target_pairs={{0,192},{16,336},{32,224},{48,368},{64,256},{80,400},{96,288},{112... | collective-permute-start | bytes 983048 | tf_op jit(solution)/shard_map/ppermute | solution.py:277
  49.1 0.0 copy-start.1
  49.1 0.3 all-to-all-done.parts_any
  49.4 0.9 column.1
  50.3 13.3 %all_to_all.15.parts_any = bf16[16,16,128]{2,1,0:T(8,128)(2,1)S(1)} all-to-all(bf16[16,16,128]{2,1,0:T(8,128)(2,1)S(1)} %get-tuple-element.14), channel_id=1, replica_groups=mesh['kv'=32,'tp'=16] {'tp'}, dimensions={0} | all-to-all | bytes 131072 | tf_op jit(solution)/shard_map/all_to_all | solution.py:345
  63.6 0.0 copy-done.1
  63.6 1.1 %project.1 = bf16[16,2,4,512]{3,2,1,0:T(4,128)(2,1)} custom-call(bf16[16,16,128]{2,1,0:T(8,128)(2,1)S(1)} %all_to_all.15.parts_any, bf16[256,1024]{1,0:T(8,128)(2,1)S(1)} %copy-done.1), custom_call_target="tpu_custom_call" | custom-call | bytes 1024 | tf_op jit(solution)/shard_map/project/pallas_call | solution.py:347
  64.7 6.7 %all-to-all-start.2 = ((bf16[32,4,512]{2,1,0:T(4,128)(2,1)}), bf16[32,4,512]{2,1,0:T(4,128)(2,1)S(1)}, u32[]{:S(2)}, u32[]{:S(2)}) async-start(bf16[32,4,512]{2,1,0:T(4,128)(2,1)} %bitcast.3), calls=%async_computation.2 | async-start | bytes 262144 | tf_op jit(solution)/shard_map/all_to_all | solution.py:357
  71.4 10.3 %collective-permute-done.4.six_ref = bf16[20,2,8,512]{3,2,1,0:T(8,128)(2,1)S(1)} collective-permute-done((bf16[20,2,8,512]{3,2,1,0:T(8,128)(2,1)}, bf16[20,2,8,512]{3,2,1,0:T(8,128)(2,1)S(1)}, u32[]{:S(2)}, u32[]{:S(2)}) %collective-permute-start.4) | collective-permute-done | bytes 327712 | tf_op jit(solution)/shard_map/ppermute | solution.py:277
  81.7 0.0 collective-permute-done.3.three_ref
  81.7 0.8 give.1
  82.5 4.6 %collective-permute-start.5 = (bf16[30,2,8,512]{3,2,1,0:T(8,128)(2,1)S(1)}, bf16[30,2,8,512]{3,2,1,0:T(8,128)(2,1)S(1)}, u32[]{:S(2)}, u32[]{:S(2)}) collective-permute-start(bf16[30,2,8,512]{3,2,1,0:T(8,128)(2,1)S(1)} %give.1), channel_id=1, source_target_pairs={{0,16},{16,0},{32,48},{48,32},{64,80},{80,64},{96,112},{112,96},{1... | collective-permute-start | bytes 1474568 | tf_op jit(solution)/shard_map/ppermute | solution.py:280
  87.1 1.5 %collective-permute-done.5.taken_ref = bf16[30,2,8,512]{3,2,1,0:T(8,128)(2,1)S(1)} collective-permute-done((bf16[30,2,8,512]{3,2,1,0:T(8,128)(2,1)S(1)}, bf16[30,2,8,512]{3,2,1,0:T(8,128)(2,1)S(1)}, u32[]{:S(2)}, u32[]{:S(2)}) %collective-permute-start.5) | collective-permute-done | bytes 491552 | tf_op jit(solution)/shard_map/ppermute | solution.py:280
  88.6 2.7 %land.1 = (bf16[64,2,8,512]{3,2,1,0:T(8,128)(2,1)}, bf16[34,2,8,512]{3,2,1,0:T(8,128)(2,1)S(1)}) custom-call(bf16[34,2,8,512]{3,2,1,0:T(8,128)(2,1)S(1)} %fill.1.after_ref.own_ref, bf16[30,2,8,512]{3,2,1,0:T(8,128)(2,1)S(1)} %collective-permute-done.got_ref, ...), custom_call_target="tpu_custom_call", output_to_operand_aliasing={{1}: (0, {})} | custom-call | bytes 1024 | tf_op jit(solution)/shard_map/land/pallas_call | solution.py:362
  91.2 0.0 all-to-all-done.2.parts_any
  91.3 0.2 add.1
  91.5 1.9 %all_gather.3 = bf16[4,1024]{1,0:T(4,128)(2,1)S(1)} all-gather(bf16[4,512]{1,0:T(4,128)(2,1)S(1)} %add.1), channel_id=1, replica_groups={{0,16},{32,48},{64,80},{96,112},{128,144},{160,176},{192,208},{224,240}..., dimensions={1}, use_global_device_ids=true | all-gather | bytes 12288 | tf_op jit(solution)/shard_map/all_gather | solution.py:384
  93.4 0.6 copy.15
  (1 shorter events, 0.0 us)
Async XLA Ops:
  0.6 0.7 copy-start.2
  1.3 1.0 %copy-start = (bf16[32,2,8,512]{3,2,1,0:T(8,128)(2,1)S(1)}, bf16[32,2,8,512]{3,2,1,0:T(8,128)(2,1)}, u32[]{:S(2)}) copy-start(bf16[32,2,8,512]{3,2,1,0:T(8,128)(2,1)} %move_ref.3) | copy-start | bytes 1572868
  4.3 11.9 %collective-permute-start = (bf16[30,2,8,512]{3,2,1,0:T(8,128)(2,1)S(1)}, bf16[30,2,8,512]{3,2,1,0:T(8,128)(2,1)S(1)}, u32[]{:S(2)}, u32[]{:S(2)}) collective-permute-start(bf16[30,2,8,512]{3,2,1,0:T(8,128)(2,1)S(1)} %get-tuple-element.15), channel_id=1, source_target_pairs={{0,16},{16,0},{32,48},{48,32},{64,80},{80,64},{96,112},{112,96},{1... | collective-permute-start | bytes 1474568 | tf_op jit(solution)/shard_map/ppermute | solution.py:280
  17.3 17.6 %collective-permute-start.1 = (bf16[24,2,8,512]{3,2,1,0:T(8,128)(2,1)S(1)}, bf16[24,2,8,512]{3,2,1,0:T(8,128)(2,1)S(1)}, u32[]{:S(2)}, u32[]{:S(2)}) collective-permute-start(bf16[24,2,8,512]{3,2,1,0:T(8,128)(2,1)S(1)} %get-tuple-element.16), channel_id=1, source_target_pairs={{0,32},{16,496},{32,64},{48,16},{64,96},{80,48},{96,128},{112,80},... | collective-permute-start | bytes 1179656 | tf_op jit(solution)/shard_map/ppermute | solution.py:277
  23.0 11.9 %collective-permute-start.2 = (bf16[20,2,8,512]{3,2,1,0:T(8,128)(2,1)S(1)}, bf16[20,2,8,512]{3,2,1,0:T(8,128)(2,1)S(1)}, u32[]{:S(2)}, u32[]{:S(2)}) collective-permute-start(bf16[20,2,8,512]{3,2,1,0:T(8,128)(2,1)S(1)} %get-tuple-element.17), channel_id=1, source_target_pairs={{0,64},{16,464},{32,96},{48,496},{64,128},{80,16},{96,160},{112,48... | collective-permute-start | bytes 983048 | tf_op jit(solution)/shard_map/ppermute | solution.py:277
  26.1 23.3 %all-to-all-start = ((bf16[32,16,128]{2,1,0:T(8,128)(2,1)}), bf16[32,16,128]{2,1,0:T(8,128)(2,1)S(1)}, u32[]{:S(2)}, u32[]{:S(2)}) async-start(bf16[32,16,128]{2,1,0:T(8,128)(2,1)} %attend.1.after_ref), calls=%async_computation | async-start | bytes 262144 | tf_op jit(solution)/shard_map/all_to_all | solution.py:318
  36.2 45.5 %collective-permute-start.3 = (bf16[24,2,8,512]{3,2,1,0:T(8,128)(2,1)S(1)}, bf16[24,2,8,512]{3,2,1,0:T(8,128)(2,1)S(1)}, u32[]{:S(2)}, u32[]{:S(2)}) collective-permute-start(bf16[24,2,8,512]{3,2,1,0:T(8,128)(2,1)S(1)} %get-tuple-element.18), channel_id=1, source_target_pairs={{0,96},{16,432},{32,128},{48,464},{64,160},{80,496},{96,192},{112,... | collective-permute-start | bytes 1179656 | tf_op jit(solution)/shard_map/ppermute | solution.py:277
  41.2 40.5 %collective-permute-start.4 = (bf16[20,2,8,512]{3,2,1,0:T(8,128)(2,1)}, bf16[20,2,8,512]{3,2,1,0:T(8,128)(2,1)S(1)}, u32[]{:S(2)}, u32[]{:S(2)}) collective-permute-start(bf16[20,2,8,512]{3,2,1,0:T(8,128)(2,1)} %get-tuple-element.19), channel_id=1, source_target_pairs={{0,192},{16,336},{32,224},{48,368},{64,256},{80,400},{96,288},{112... | collective-permute-start | bytes 983048 | tf_op jit(solution)/shard_map/ppermute | solution.py:277
  49.1 14.5 %copy-start.1 = (bf16[256,1024]{1,0:T(8,128)(2,1)S(1)}, bf16[256,1024]{1,0:T(8,128)(2,1)}, u32[]{:S(2)}) copy-start(bf16[256,1024]{1,0:T(8,128)(2,1)} %weight_ref.1) | copy-start | bytes 1572868
  64.7 26.6 %all-to-all-start.2 = ((bf16[32,4,512]{2,1,0:T(4,128)(2,1)}), bf16[32,4,512]{2,1,0:T(4,128)(2,1)S(1)}, u32[]{:S(2)}, u32[]{:S(2)}) async-start(bf16[32,4,512]{2,1,0:T(4,128)(2,1)} %bitcast.3), calls=%async_computation.2 | async-start | bytes 262144 | tf_op jit(solution)/shard_map/all_to_all | solution.py:357
  82.5 6.1 %collective-permute-start.5 = (bf16[30,2,8,512]{3,2,1,0:T(8,128)(2,1)S(1)}, bf16[30,2,8,512]{3,2,1,0:T(8,128)(2,1)S(1)}, u32[]{:S(2)}, u32[]{:S(2)}) collective-permute-start(bf16[30,2,8,512]{3,2,1,0:T(8,128)(2,1)S(1)} %give.1), channel_id=1, source_target_pairs={{0,16},{16,0},{32,48},{48,32},{64,80},{80,64},{96,112},{112,96},{1... | collective-permute-start | bytes 1474568 | tf_op jit(solution)/shard_map/ppermute | solution.py:280

commit v8 on v7

--- a/solution.py
+++ b/solution.py
@@ -17,6 +17,7 @@
 CHIPS = 16
 NEG = -1e30
 SMALL = 8 * 2**20
+LARGE = 56 * 2**20
 
 VMEM = pl.BlockSpec(memory_space=pltpu.VMEM)
 ANY = pl.BlockSpec(memory_space=pl.ANY)
@@ -290,7 +291,7 @@
             pltpu.SMEM((kv_size,), jnp.int32),
             pltpu.SemaphoreType.DMA((2,)),
         ],
-        compiler_params=pltpu.CompilerParams(vmem_limit_bytes=SMALL),
+        compiler_params=pltpu.CompilerParams(vmem_limit_bytes=LARGE),
         name="pack",
     )(move_cache, owners)
     got = swap(other)
@@ -363,7 +364,7 @@
         land_kernel,
         out_shape=(pages(kv_size * CAP), pages(HOME + CAP)),
         in_specs=[ANY] * 7,
-        out_specs=(VMEM, ANY),
+        out_specs=(ANY, ANY),
         input_output_aliases={0: 1},
         scratch_shapes=[pltpu.SemaphoreType.DMA((25,))],
         compiler_params=pltpu.CompilerParams(vmem_limit_bytes=SMALL),

time: 94.5 us -> 92.4 us (0.978)
  local copies, waits for them, and re-layouts: 2.3 us -> 0.61 us
    unnamed x7 -> x5, local copies, waits for them, and re-layouts: 2.3 us -> 0.61 us
    pallas_call x1, Pallas kernels: 2.67 us -> 1.17 us  [local(): pl.pallas_call(land_kernel, out_shape=(pages(kv_size * CAP), pages(HOME +...]
    pallas_call x1, Pallas kernels: 1.99 us -> 3.07 us  [local(): pl.pallas_call(pack_kernel, out_shape=(pages(HOME + CAP), pages(GIVEN + C...]
  transfers between devices with their start and end apart: 8 -> 8, of which waited for: 4 -> 4; matrix products, arithmetic and copies ran while one was open for 0% -> 0% of each run, Pallas kernels for 10% -> 9%
where the time goes in v8:
time: 92.4 us; the launch traced here: 91.9 us
  starting transfers between devices  49.2 us (53%)
  blocking collectives  15.2 us (16%)
  waiting for transfers between devices  13.5 us (15%)
  Pallas kernels  12.7 us (14%)
    ppermute x4, starting transfers between devices, shift(): return lax.ppermute(x, 'kv', pairs)  21.7 us
    ppermute x2, starting transfers between devices, swap(): return lax.ppermute(x, 'kv', [(i, i ^ 1) for i in range(kv_size)])  13.4 us
    all_to_all x1, blocking collectives, local(): lax.all_to_all(part, 'tp', split_axis=0, concat_axis=0, tiled=True)  13.3 us
    ppermute x4, waiting for transfers between devices, shift(): return lax.ppermute(x, 'kv', pairs)  11.7 us
    all_to_all x1, starting transfers between devices, local(): parts = lax.all_to_all(parts, 'kv', split_axis=0, concat_axis=0, tiled=True)  7.37 us
    all_to_all x1, starting transfers between devices, local(): lax.all_to_all(partial_out.reshape(kv_size, B, half), 'kv', split_axis=0,...  6.73 us
    pallas_call x1, Pallas kernels, local(): pl.pallas_call(attend_kernel, out_shape=jax.ShapeDtypeStruct((kv_size, 16...  3.17 us
    pallas_call x3, Pallas kernels, copies(): pl.pallas_call(kernel, out_shape=tuple((pages(n) for n in out_pages)), in...  3.1 us
  transfers between devices with their start and end apart: 8, of which 4 were waited for; matrix products, arithmetic and copies ran while one was open for 0% of the time, Pallas kernels for 9%

profile of v8, /device:TPU:1, one launch (start us, length us, event | category | flops | bytes accessed | tf_op | source)
XLA Modules:
  0.0 91.9 jit_solution(16710156297110441346)
XLA Ops:
  0.6 3.1 %pack.1 = (bf16[34,2,8,512]{3,2,1,0:T(8,128)(2,1)}, bf16[30,2,8,512]{3,2,1,0:T(8,128)(2,1)}) custom-call(bf16[32,2,8,512]{3,2,1,0:T(8,128)(2,1)} %move_ref.3, s32[32]{0:T(128)} %bitcast.6), custom_call_target="tpu_custom_call" | custom-call | tf_op jit(solution)/shard_map/pack/pallas_call | solution.py:283
  3.7 8.8 %collective-permute-start = (bf16[30,2,8,512]{3,2,1,0:T(8,128)(2,1)}, bf16[30,2,8,512]{3,2,1,0:T(8,128)(2,1)S(1)}, u32[]{:S(2)}, u32[]{:S(2)}) collective-permute-start(bf16[30,2,8,512]{3,2,1,0:T(8,128)(2,1)} %get-tuple-element.15), channel_id=1, source_target_pairs={{0,16},{16,0},{32,48},{48,32},{64,80},{80,64},{96,112},{112,96},{1... | collective-permute-start | bytes 1474568 | tf_op jit(solution)/shard_map/ppermute | solution.py:281
  12.5 0.0 copy-start
  12.5 3.2 %attend.1.after_ref = bf16[32,16,128]{2,1,0:T(8,128)(2,1)} custom-call(bf16[4,8192]{1,0:T(4,128)(2,1)} %q_ref.1, bf16[32,2,8,512]{3,2,1,0:T(8,128)(2,1)} %res_ref.1, bf16[32,2,8,512]{3,2,1,0:T(8,128)(2,1)} %move_ref.3, s32[1,4]{1,0:T(1,128)} %count_ref.1, s32[32]{0:T(128)} %request_ref.1, s32[1,32]{1,0:T(1,128)} %bitcast.7, s32[1,32]{1,0:T(1,128)} %bitcast.5), custom_call_target="tpu_custom_call" | custom-call | tf_op jit(solution)/shard_map/attend/pallas_call | solution.py:310
  15.7 0.0 collective-permute-done.got_ref
  15.7 0.0 copy-done
  15.7 1.0 %short.1 = (bf16[24,2,8,512]{3,2,1,0:T(8,128)(2,1)S(1)}, bf16[20,2,8,512]{3,2,1,0:T(8,128)(2,1)S(1)}) custom-call(bf16[34,2,8,512]{3,2,1,0:T(8,128)(2,1)S(1)} %copy-done, bf16[30,2,8,512]{3,2,1,0:T(8,128)(2,1)S(1)} %collective-permute-done.got_ref, bf16[32,16,128]{2,1,0:T(8,128)(2,1)} %attend.1.after_ref), custom_call_target="tpu_custom_call" | custom-call | bytes 1024 | tf_op jit(solution)/shard_map/short/pallas_call | solution.py:299
  16.7 5.8 %collective-permute-start.1 = (bf16[24,2,8,512]{3,2,1,0:T(8,128)(2,1)S(1)}, bf16[24,2,8,512]{3,2,1,0:T(8,128)(2,1)S(1)}, u32[]{:S(2)}, u32[]{:S(2)}) collective-permute-start(bf16[24,2,8,512]{3,2,1,0:T(8,128)(2,1)S(1)} %get-tuple-element.16), channel_id=1, source_target_pairs={{0,32},{16,496},{32,64},{48,16},{64,96},{80,48},{96,128},{112,80},... | collective-permute-start | bytes 1179656 | tf_op jit(solution)/shard_map/ppermute | solution.py:278
  22.5 3.1 %collective-permute-start.2 = (bf16[20,2,8,512]{3,2,1,0:T(8,128)(2,1)S(1)}, bf16[20,2,8,512]{3,2,1,0:T(8,128)(2,1)S(1)}, u32[]{:S(2)}, u32[]{:S(2)}) collective-permute-start(bf16[20,2,8,512]{3,2,1,0:T(8,128)(2,1)S(1)} %get-tuple-element.17), channel_id=1, source_target_pairs={{0,64},{16,464},{32,96},{48,496},{64,128},{80,16},{96,160},{112,48... | collective-permute-start | bytes 983048 | tf_op jit(solution)/shard_map/ppermute | solution.py:278
  25.6 7.4 %all-to-all-start = ((bf16[32,16,128]{2,1,0:T(8,128)(2,1)}), bf16[32,16,128]{2,1,0:T(8,128)(2,1)S(1)}, u32[]{:S(2)}, u32[]{:S(2)}) async-start(bf16[32,16,128]{2,1,0:T(8,128)(2,1)} %attend.1.after_ref), calls=%async_computation | async-start | bytes 262144 | tf_op jit(solution)/shard_map/all_to_all | solution.py:319
  33.0 1.4 %collective-permute-done.2.two_ref = bf16[20,2,8,512]{3,2,1,0:T(8,128)(2,1)S(1)} collective-permute-done((bf16[20,2,8,512]{3,2,1,0:T(8,128)(2,1)S(1)}, bf16[20,2,8,512]{3,2,1,0:T(8,128)(2,1)S(1)}, u32[]{:S(2)}, u32[]{:S(2)}) %collective-permute-start.2) | collective-permute-done | bytes 327712 | tf_op jit(solution)/shard_map/ppermute | solution.py:278
  34.4 0.0 collective-permute-done.1.one_ref
  34.4 1.3 %long.1 = (bf16[24,2,8,512]{3,2,1,0:T(8,128)(2,1)S(1)}, bf16[20,2,8,512]{3,2,1,0:T(8,128)(2,1)}) custom-call(bf16[34,2,8,512]{3,2,1,0:T(8,128)(2,1)S(1)} %copy-done, bf16[30,2,8,512]{3,2,1,0:T(8,128)(2,1)S(1)} %collective-permute-done.got_ref, bf16[24,2,8,512]{3,2,1,0:T(8,128)(2,1)S(1)} %collective-permute-done.1.one_ref, ...), custom_call_target="tpu_custom_call" | custom-call | bytes 1024 | tf_op jit(solution)/shard_map/long/pallas_call | solution.py:299
  35.7 5.0 %collective-permute-start.3 = (bf16[24,2,8,512]{3,2,1,0:T(8,128)(2,1)S(1)}, bf16[24,2,8,512]{3,2,1,0:T(8,128)(2,1)S(1)}, u32[]{:S(2)}, u32[]{:S(2)}) collective-permute-start(bf16[24,2,8,512]{3,2,1,0:T(8,128)(2,1)S(1)} %get-tuple-element.18), channel_id=1, source_target_pairs={{0,96},{16,432},{32,128},{48,464},{64,160},{80,496},{96,192},{112,... | collective-permute-start | bytes 1179656 | tf_op jit(solution)/shard_map/ppermute | solution.py:278
  40.7 7.8 %collective-permute-start.4 = (bf16[20,2,8,512]{3,2,1,0:T(8,128)(2,1)}, bf16[20,2,8,512]{3,2,1,0:T(8,128)(2,1)S(1)}, u32[]{:S(2)}, u32[]{:S(2)}) collective-permute-start(bf16[20,2,8,512]{3,2,1,0:T(8,128)(2,1)} %get-tuple-element.19), channel_id=1, source_target_pairs={{0,192},{16,336},{32,224},{48,368},{64,256},{80,400},{96,288},{112... | collective-permute-start | bytes 983048 | tf_op jit(solution)/shard_map/ppermute | solution.py:278
  48.5 0.0 copy-start.1
  48.5 0.3 all-to-all-done.parts_any
  48.9 0.9 column.1
  49.7 13.3 %all_to_all.15.parts_any = bf16[16,16,128]{2,1,0:T(8,128)(2,1)S(1)} all-to-all(bf16[16,16,128]{2,1,0:T(8,128)(2,1)S(1)} %get-tuple-element.14), channel_id=1, replica_groups=mesh['kv'=32,'tp'=16] {'tp'}, dimensions={0} | all-to-all | bytes 131072 | tf_op jit(solution)/shard_map/all_to_all | solution.py:346
  63.1 0.0 copy-done.1
  63.1 1.1 %project.1 = bf16[16,2,4,512]{3,2,1,0:T(4,128)(2,1)} custom-call(bf16[16,16,128]{2,1,0:T(8,128)(2,1)S(1)} %all_to_all.15.parts_any, bf16[256,1024]{1,0:T(8,128)(2,1)S(1)} %copy-done.1), custom_call_target="tpu_custom_call" | custom-call | bytes 1024 | tf_op jit(solution)/shard_map/project/pallas_call | solution.py:348
  64.1 6.7 %all-to-all-start.2 = ((bf16[32,4,512]{2,1,0:T(4,128)(2,1)}), bf16[32,4,512]{2,1,0:T(4,128)(2,1)S(1)}, u32[]{:S(2)}, u32[]{:S(2)}) async-start(bf16[32,4,512]{2,1,0:T(4,128)(2,1)} %bitcast.3), calls=%async_computation.2 | async-start | bytes 262144 | tf_op jit(solution)/shard_map/all_to_all | solution.py:358
  70.9 10.3 %collective-permute-done.4.six_ref = bf16[20,2,8,512]{3,2,1,0:T(8,128)(2,1)S(1)} collective-permute-done((bf16[20,2,8,512]{3,2,1,0:T(8,128)(2,1)}, bf16[20,2,8,512]{3,2,1,0:T(8,128)(2,1)S(1)}, u32[]{:S(2)}, u32[]{:S(2)}) %collective-permute-start.4) | collective-permute-done | bytes 327712 | tf_op jit(solution)/shard_map/ppermute | solution.py:278
  81.2 0.0 collective-permute-done.3.three_ref
  81.2 0.8 give.1
  81.9 4.6 %collective-permute-start.5 = (bf16[30,2,8,512]{3,2,1,0:T(8,128)(2,1)S(1)}, bf16[30,2,8,512]{3,2,1,0:T(8,128)(2,1)S(1)}, u32[]{:S(2)}, u32[]{:S(2)}) collective-permute-start(bf16[30,2,8,512]{3,2,1,0:T(8,128)(2,1)S(1)} %give.1), channel_id=1, source_target_pairs={{0,16},{16,0},{32,48},{48,32},{64,80},{80,64},{96,112},{112,96},{1... | collective-permute-start | bytes 1474568 | tf_op jit(solution)/shard_map/ppermute | solution.py:281
  86.6 1.5 %collective-permute-done.5.taken_ref = bf16[30,2,8,512]{3,2,1,0:T(8,128)(2,1)S(1)} collective-permute-done((bf16[30,2,8,512]{3,2,1,0:T(8,128)(2,1)S(1)}, bf16[30,2,8,512]{3,2,1,0:T(8,128)(2,1)S(1)}, u32[]{:S(2)}, u32[]{:S(2)}) %collective-permute-start.5) | collective-permute-done | bytes 491552 | tf_op jit(solution)/shard_map/ppermute | solution.py:281
  88.1 1.2 %land.1 = (bf16[64,2,8,512]{3,2,1,0:T(8,128)(2,1)}, bf16[34,2,8,512]{3,2,1,0:T(8,128)(2,1)S(1)}) custom-call(bf16[34,2,8,512]{3,2,1,0:T(8,128)(2,1)S(1)} %fill.1.after_ref.own_ref, bf16[30,2,8,512]{3,2,1,0:T(8,128)(2,1)S(1)} %collective-permute-done.got_ref, ...), custom_call_target="tpu_custom_call", output_to_operand_aliasing={{1}: (0, {})} | custom-call | bytes 1024 | tf_op jit(solution)/shard_map/land/pallas_call | solution.py:363
  89.2 0.0 all-to-all-done.2.parts_any
  89.2 0.2 add.1
  89.5 1.9 %all_gather.3 = bf16[4,1024]{1,0:T(4,128)(2,1)S(1)} all-gather(bf16[4,512]{1,0:T(4,128)(2,1)S(1)} %add.1), channel_id=1, replica_groups={{0,16},{32,48},{64,80},{96,112},{128,144},{160,176},{192,208},{224,240}..., dimensions={1}, use_global_device_ids=true | all-gather | bytes 12288 | tf_op jit(solution)/shard_map/all_gather | solution.py:385
  91.3 0.6 copy.15
  (1 shorter events, 0.0 us)
Async XLA Ops:
  3.7 12.0 %collective-permute-start = (bf16[30,2,8,512]{3,2,1,0:T(8,128)(2,1)}, bf16[30,2,8,512]{3,2,1,0:T(8,128)(2,1)S(1)}, u32[]{:S(2)}, u32[]{:S(2)}) collective-permute-start(bf16[30,2,8,512]{3,2,1,0:T(8,128)(2,1)} %get-tuple-element.15), channel_id=1, source_target_pairs={{0,16},{16,0},{32,48},{48,32},{64,80},{80,64},{96,112},{112,96},{1... | collective-permute-start | bytes 1474568 | tf_op jit(solution)/shard_map/ppermute | solution.py:281
  12.5 3.2 %copy-start = (bf16[34,2,8,512]{3,2,1,0:T(8,128)(2,1)S(1)}, bf16[34,2,8,512]{3,2,1,0:T(8,128)(2,1)}, u32[]{:S(2)}) copy-start(bf16[34,2,8,512]{3,2,1,0:T(8,128)(2,1)} %get-tuple-element.13.refs_0_.own_ref) | copy-start | bytes 1671172
  16.7 17.6 %collective-permute-start.1 = (bf16[24,2,8,512]{3,2,1,0:T(8,128)(2,1)S(1)}, bf16[24,2,8,512]{3,2,1,0:T(8,128)(2,1)S(1)}, u32[]{:S(2)}, u32[]{:S(2)}) collective-permute-start(bf16[24,2,8,512]{3,2,1,0:T(8,128)(2,1)S(1)} %get-tuple-element.16), channel_id=1, source_target_pairs={{0,32},{16,496},{32,64},{48,16},{64,96},{80,48},{96,128},{112,80},... | collective-permute-start | bytes 1179656 | tf_op jit(solution)/shard_map/ppermute | solution.py:278
  22.5 11.9 %collective-permute-start.2 = (bf16[20,2,8,512]{3,2,1,0:T(8,128)(2,1)S(1)}, bf16[20,2,8,512]{3,2,1,0:T(8,128)(2,1)S(1)}, u32[]{:S(2)}, u32[]{:S(2)}) collective-permute-start(bf16[20,2,8,512]{3,2,1,0:T(8,128)(2,1)S(1)} %get-tuple-element.17), channel_id=1, source_target_pairs={{0,64},{16,464},{32,96},{48,496},{64,128},{80,16},{96,160},{112,48... | collective-permute-start | bytes 983048 | tf_op jit(solution)/shard_map/ppermute | solution.py:278
  25.6 23.3 %all-to-all-start = ((bf16[32,16,128]{2,1,0:T(8,128)(2,1)}), bf16[32,16,128]{2,1,0:T(8,128)(2,1)S(1)}, u32[]{:S(2)}, u32[]{:S(2)}) async-start(bf16[32,16,128]{2,1,0:T(8,128)(2,1)} %attend.1.after_ref), calls=%async_computation | async-start | bytes 262144 | tf_op jit(solution)/shard_map/all_to_all | solution.py:319
  35.7 45.5 %collective-permute-start.3 = (bf16[24,2,8,512]{3,2,1,0:T(8,128)(2,1)S(1)}, bf16[24,2,8,512]{3,2,1,0:T(8,128)(2,1)S(1)}, u32[]{:S(2)}, u32[]{:S(2)}) collective-permute-start(bf16[24,2,8,512]{3,2,1,0:T(8,128)(2,1)S(1)} %get-tuple-element.18), channel_id=1, source_target_pairs={{0,96},{16,432},{32,128},{48,464},{64,160},{80,496},{96,192},{112,... | collective-permute-start | bytes 1179656 | tf_op jit(solution)/shard_map/ppermute | solution.py:278
  40.7 40.5 %collective-permute-start.4 = (bf16[20,2,8,512]{3,2,1,0:T(8,128)(2,1)}, bf16[20,2,8,512]{3,2,1,0:T(8,128)(2,1)S(1)}, u32[]{:S(2)}, u32[]{:S(2)}) collective-permute-start(bf16[20,2,8,512]{3,2,1,0:T(8,128)(2,1)} %get-tuple-element.19), channel_id=1, source_target_pairs={{0,192},{16,336},{32,224},{48,368},{64,256},{80,400},{96,288},{112... | collective-permute-start | bytes 983048 | tf_op jit(solution)/shard_map/ppermute | solution.py:278
  48.5 14.5 %copy-start.1 = (bf16[256,1024]{1,0:T(8,128)(2,1)S(1)}, bf16[256,1024]{1,0:T(8,128)(2,1)}, u32[]{:S(2)}) copy-start(bf16[256,1024]{1,0:T(8,128)(2,1)} %weight_ref.1) | copy-start | bytes 1572868
  64.1 25.1 %all-to-all-start.2 = ((bf16[32,4,512]{2,1,0:T(4,128)(2,1)}), bf16[32,4,512]{2,1,0:T(4,128)(2,1)S(1)}, u32[]{:S(2)}, u32[]{:S(2)}) async-start(bf16[32,4,512]{2,1,0:T(4,128)(2,1)} %bitcast.3), calls=%async_computation.2 | async-start | bytes 262144 | tf_op jit(solution)/shard_map/all_to_all | solution.py:358
  81.9 6.1 %collective-permute-start.5 = (bf16[30,2,8,512]{3,2,1,0:T(8,128)(2,1)S(1)}, bf16[30,2,8,512]{3,2,1,0:T(8,128)(2,1)S(1)}, u32[]{:S(2)}, u32[]{:S(2)}) collective-permute-start(bf16[30,2,8,512]{3,2,1,0:T(8,128)(2,1)S(1)} %give.1), channel_id=1, source_target_pairs={{0,16},{16,0},{32,48},{48,32},{64,80},{80,64},{96,112},{112,96},{1... | collective-permute-start | bytes 1474568 | tf_op jit(solution)/shard_map/ppermute | solution.py:281

commit v9 on v8

--- a/solution.py
+++ b/solution.py
@@ -118,9 +118,8 @@
     return ref.at[pl.ds(first * QUAD, count * QUAD)]
 
 
-def pack_kernel(move_ref, owner_ref, own_out, other_out, own_ref, other_ref, used_ref, sems):
-    own_ref[...] = jnp.zeros(own_ref.shape, own_ref.dtype)
-    other_ref[...] = jnp.zeros(other_ref.shape, other_ref.dtype)
+def pack_kernel(move_ref, owner_ref, own_out, other_out, slots_ref, used_ref, sems):
+    slots_ref[...] = jnp.zeros(slots_ref.shape, slots_ref.dtype)
     for o in range(used_ref.shape[0]):
         used_ref[o] = 0
     me = lax.axis_index("kv")
@@ -134,22 +133,14 @@
         lands = owner % 2
         carrier = jnp.where(up == 0, lands, jnp.where(up == FAR, core, (up > FAR).astype(jnp.int32)))
         distance = jnp.where(up > FAR, CHIPS - up, up)
-        slot = (distance - 1) * 4 + jnp.where(lands == carrier, 0, CAP) + rank
-        home = jnp.where(carrier == core, HOME, GIVEN) + rank
-        slot = jnp.where(up == 0, home, slot)
-
-        @pl.when(carrier == core)
-        def _():
-            own_ref[slot] = move_ref[p]
-
-        @pl.when(carrier != core)
-        def _():
-            other_ref[slot] = move_ref[p]
-
+        slot = (distance - 1) * 4 + jnp.where(lands == carrier, 0, CAP)
+        slot = jnp.where(up == 0, jnp.where(carrier == core, HOME, GIVEN), slot)
+        slots_ref[jnp.where(carrier == core, slot, HOME + CAP + slot) + rank] = move_ref[p]
         return carry
 
-    lax.fori_loop(0, move_ref.shape[0], place, 0)
-    copy_all([(own_ref, own_out), (other_ref, other_out)], sems)
+    lax.fori_loop(0, move_ref.shape[0], place, 0, unroll=8)
+    own, other = slots_ref.at[pl.ds(0, HOME + CAP)], slots_ref.at[pl.ds(HOME + CAP, GIVEN + CAP)]
+    copy_all([(other, other_out), (own, own_out)], sems)
 
 
 def short_kernel(own_ref, got_ref, after_ref, one_ref, two_ref, sems):
@@ -163,15 +154,24 @@
     copy_all(copies, sems)
 
 
-def long_kernel(own_ref, got_ref, one_ref, two_ref, three_ref, six_ref, sems):
-    copies = []
-    for n, ref in enumerate((three_ref, six_ref)):
-        own = 2 + 3 * n
-        copies += [(quads(own_ref, own), quads(ref, 0)), (quads(got_ref, own), quads(ref, 1))]
-        copies.append((quads(one_ref, 2 + 2 * n, 2), quads(ref, 2, 2)))
-        count = 2 - n
-        copies.append((quads(two_ref, 2 + 2 * n, count), quads(ref, 4, count)))
-    copy_all(copies, sems)
+def long_copies(first, own_ref, got_ref, one_ref, two_ref, out_ref):
+    n = first // 3 - 1
+    count = 2 - n
+    return [
+        (quads(own_ref, first - 1), quads(out_ref, 0)),
+        (quads(got_ref, first - 1), quads(out_ref, 1)),
+        (quads(one_ref, 2 + 2 * n, 2), quads(out_ref, 2, 2)),
+        (quads(two_ref, 2 + 2 * n, count), quads(out_ref, 4, count)),
+    ]
+
+
+def three_kernel(own_ref, got_ref, one_ref, two_ref, out_ref, sems):
+    copy_all(long_copies(3, own_ref, got_ref, one_ref, two_ref, out_ref), sems)
+
+
+def six_kernel(own_ref, got_ref, one_ref, two_ref, after_ref, out_ref, sems):
+    del after_ref
+    copy_all(long_copies(6, own_ref, got_ref, one_ref, two_ref, out_ref), sems)
 
 
 def arrived(one_ref, two_ref, three_ref, six_ref):
@@ -186,7 +186,8 @@
     )
 
 
-def give_kernel(one_ref, two_ref, three_ref, six_ref, out_ref, sems):
+def give_kernel(one_ref, two_ref, three_ref, six_ref, after_ref, out_ref, sems):
+    del after_ref
     core = lax.axis_index("kv") % 2
     copies = [(six_ref.at[pl.ds(4 * QUAD + CAP, CAP)], out_ref.at[pl.ds(GIVEN, CAP)])]
     for distance, ref, quad in arrived(one_ref, two_ref, three_ref, six_ref):
@@ -196,25 +197,33 @@
     copy_all(copies, sems)
 
 
-def land_kernel(own_ref, got_ref, one_ref, two_ref, three_ref, six_ref, taken_ref, out_ref, passed_ref, sems):
-    me = lax.axis_index("kv")
-    chip, core = me // 2, me % 2
+def rows(out_ref, up, start=0, count=CAP):
+    chip = lax.axis_index("kv") // 2
+    return out_ref.at[pl.ds(((chip + up) & (CHIPS - 1)) * QUAD + start * CAP, count)]
+
+
+def land_kernel(own_ref, got_ref, one_ref, two_ref, three_ref, six_ref, out_ref, sems):
+    core = lax.axis_index("kv") % 2
     way = 1 - 2 * core
-
-    def rows(up, start):
-        return out_ref.at[pl.ds(((chip + up) & (CHIPS - 1)) * QUAD + start * CAP, CAP)]
-
     copies = [
-        (own_ref.at[pl.ds(HOME, CAP)], rows(0, core)),
-        (got_ref.at[pl.ds(GIVEN, CAP)], rows(0, 1 - core)),
-        (six_ref.at[pl.ds(4 * QUAD, CAP)], rows(FAR, core)),
-        (taken_ref.at[pl.ds(GIVEN, CAP)], rows(FAR, 1 - core)),
+        (own_ref.at[pl.ds(HOME, CAP)], rows(out_ref, 0, core)),
+        (got_ref.at[pl.ds(GIVEN, CAP)], rows(out_ref, 0, 1 - core)),
+        (six_ref.at[pl.ds(4 * QUAD, CAP)], rows(out_ref, FAR, core)),
     ]
     for distance, ref, quad in arrived(one_ref, two_ref, three_ref, six_ref):
         for quad, start in ((quad, core), (quad + 1, 1 - core)):
-            copies.append((ref.at[pl.ds(quad * QUAD, CAP)], rows(-way * distance, start)))
-        to = out_ref.at[pl.ds(((chip + way * distance) & (CHIPS - 1)) * QUAD, QUAD)]
-        copies.append((quads(taken_ref, distance - 1), to))
+            copies.append((ref.at[pl.ds(quad * QUAD, CAP)], rows(out_ref, -way * distance, start)))
+    copy_all(copies, sems)
+
+
+def land_taken_kernel(taken_any, landed_ref, after_ref, out_ref, taken_ref, sems):
+    del landed_ref, after_ref
+    core = lax.axis_index("kv") % 2
+    way = 1 - 2 * core
+    pltpu.sync_copy(taken_any, taken_ref)
+    copies = [(taken_ref.at[pl.ds(GIVEN, CAP)], rows(out_ref, FAR, 1 - core))]
+    for distance in range(1, FAR):
+        copies.append((quads(taken_ref, distance - 1), rows(out_ref, way * distance, 0, QUAD)))
     copy_all(copies, sems)
 
 
@@ -252,15 +261,17 @@
     attended = (values / weight_sum).astype(BF16)
     upper = jnp.dot(attended, weight_ref[:HD], preferred_element_type=F32)
     lower = jnp.dot(attended, weight_ref[HD:], preferred_element_type=F32)
-    partial = (upper[:B] + lower[B:]).astype(out_ref.dtype)
-    half = partial.shape[1] // 2
-    for core in range(2):
-        part = partial[:, core * half : (core + 1) * half]
-        out_ref[:, core] = jnp.broadcast_to(part[None], (out_ref.shape[0],) + part.shape)
-
-
-def add_kernel(parts_any, after_ref, out_ref, parts_ref):
-    del after_ref
+    out_ref[...] = upper[:B] + lower[B:]
+
+
+def pair_kernel(parts_any, out_ref, parts_ref):
+    pltpu.sync_copy(parts_any, parts_ref)
+    both = (parts_ref[0] + parts_ref[1]).astype(out_ref.dtype)
+    out_ref[...] = jnp.broadcast_to(both[None], out_ref.shape)
+
+
+def add_kernel(parts_any, own_ref, out_ref, passed_ref, parts_ref):
+    del own_ref, passed_ref
     pltpu.sync_copy(parts_any, parts_ref)
     out_ref[...] = jnp.sum(parts_ref[...].astype(F32), axis=0).astype(out_ref.dtype)
 
@@ -286,8 +297,7 @@
         in_specs=[VMEM, SMEM],
         out_specs=(ANY, ANY),
         scratch_shapes=[
-            pltpu.VMEM((HOME + CAP,) + page, BF16),
-            pltpu.VMEM((GIVEN + CAP,) + page, BF16),
+            pltpu.VMEM((HOME + GIVEN + 2 * CAP,) + page, BF16),
             pltpu.SMEM((kv_size,), jnp.int32),
             pltpu.SemaphoreType.DMA((2,)),
         ],
@@ -317,7 +327,8 @@
     one, two = copies(short_kernel, "short", (6 * QUAD, 5 * QUAD), 11, own, got, parts)
     one, two = shift(one, 1), shift(two, 2)
     parts = lax.all_to_all(parts, "kv", split_axis=0, concat_axis=0, tiled=True)
-    three, six = copies(long_kernel, "long", (6 * QUAD, 5 * QUAD), 8, own, got, one, two)
+    (three,) = copies(three_kernel, "three", (6 * QUAD,), 4, own, got, one, two)
+    (six,) = copies(six_kernel, "six", (5 * QUAD,), 4, own, got, one, two, three)
     six_up, three_up = shift(six, 6), shift(three, 3)
     own = pl.pallas_call(
         fill_kernel,
@@ -344,45 +355,59 @@
     )(parts, own)
     six, three = six_up, three_up
     columns = lax.all_to_all(part, "tp", split_axis=0, concat_axis=0, tiled=True)
-    half = out_weight.shape[1] // 2
     partial_out = pl.pallas_call(
         project_kernel,
-        out_shape=jax.ShapeDtypeStruct((CHIPS, 2, B, half), BF16),
+        out_shape=jax.ShapeDtypeStruct((B, out_weight.shape[1]), F32),
         in_specs=[ANY, VMEM],
         out_specs=VMEM,
         scratch_shapes=[pltpu.VMEM(columns.shape, BF16)],
         compiler_params=pltpu.CompilerParams(vmem_limit_bytes=SMALL),
         name="project",
+    )(columns, out_weight)
+    pair = lax.all_gather(
+        partial_out, "kv", axis_index_groups=[[2 * z, 2 * z + 1] for z in range(CHIPS)]
+    )
+    chip_out = pl.pallas_call(
+        pair_kernel,
+        out_shape=jax.ShapeDtypeStruct((CHIPS, B, out_weight.shape[1]), BF16),
+        in_specs=[ANY],
+        out_specs=VMEM,
+        scratch_shapes=[pltpu.VMEM(pair.shape, F32)],
+        compiler_params=pltpu.CompilerParams(vmem_limit_bytes=SMALL),
+        name="pair",
+    )(pair)
+    partials = lax.all_to_all(
+        chip_out,
+        "kv",
+        split_axis=0,
+        concat_axis=0,
+        tiled=True,
+        axis_index_groups=[[2 * z + c for z in range(CHIPS)] for c in range(2)],
+    )
+    (give,) = copies(give_kernel, "give", (GIVEN + CAP,), 15, one, two, three, six, chip_out)
+    taken = swap(give)
+    (landed,) = copies(land_kernel, "land", (kv_size * CAP,), 17, own, got, one, two, three, six)
+    mixed, own = pl.pallas_call(
+        add_kernel,
+        out_shape=(jax.ShapeDtypeStruct((B, out_weight.shape[1]), BF16), pages(HOME + CAP)),
+        in_specs=[ANY, ANY],
+        out_specs=(VMEM, ANY),
+        input_output_aliases={1: 1},
+        scratch_shapes=[pltpu.VMEM(partials.shape, BF16)],
+        compiler_params=pltpu.CompilerParams(vmem_limit_bytes=SMALL),
+        name="add",
+    )(partials, own)
+    landed = pl.pallas_call(
+        land_taken_kernel,
+        out_shape=pages(kv_size * CAP),
+        in_specs=[ANY] * 3,
+        out_specs=ANY,
+        input_output_aliases={1: 0},
+        scratch_shapes=[pltpu.VMEM(taken.shape, BF16), pltpu.SemaphoreType.DMA((FAR,))],
+        compiler_params=pltpu.CompilerParams(vmem_limit_bytes=SMALL),
         cost_estimate=pl.CostEstimate(flops=0, bytes_accessed=1024, transcendentals=0),
-    )(columns, out_weight)
-    partials = lax.all_to_all(
-        partial_out.reshape(kv_size, B, half), "kv", split_axis=0, concat_axis=0, tiled=True
-    )
-    (give,) = copies(give_kernel, "give", (GIVEN + CAP,), 15, one, two, three, six)
-    taken = swap(give)
-    landed, own = pl.pallas_call(
-        land_kernel,
-        out_shape=(pages(kv_size * CAP), pages(HOME + CAP)),
-        in_specs=[ANY] * 7,
-        out_specs=(ANY, ANY),
-        input_output_aliases={0: 1},
-        scratch_shapes=[pltpu.SemaphoreType.DMA((25,))],
-        compiler_params=pltpu.CompilerParams(vmem_limit_bytes=SMALL),
-        cost_estimate=pl.CostEstimate(flops=0, bytes_accessed=1024, transcendentals=0),
-        name="land",
-    )(own, got, one, two, three, six, taken)
-    mixed_half = pl.pallas_call(
-        add_kernel,
-        out_shape=jax.ShapeDtypeStruct((B, half), BF16),
-        in_specs=[ANY, ANY],
-        out_specs=VMEM,
-        scratch_shapes=[pltpu.VMEM(partials.shape, BF16)],
-        compiler_params=pltpu.CompilerParams(vmem_limit_bytes=SMALL),
-        name="add",
-        cost_estimate=pl.CostEstimate(flops=0, bytes_accessed=1024, transcendentals=0),
-    )(partials, own)
-    both_cores = [[2 * z, 2 * z + 1] for z in range(CHIPS)]
-    mixed = lax.all_gather(mixed_half, "kv", axis=1, tiled=True, axis_index_groups=both_cores)
+        name="land_taken",
+    )(taken, landed, own)
     return (mixed, landed, landed_ids.reshape(-1))
 
 

time: 92.4 us -> 89.7 us (0.971)
  starting transfers between devices: 49.2 us -> 45.7 us
  waiting for transfers between devices: 13.5 us -> 10.6 us
  blocking collectives: 15.2 us -> 17.6 us
  Pallas kernels: 12.7 us -> 13.8 us
    all_to_all x1, starting transfers between devices: 6.73 us -> 3.68 us  [local(): lax.all_to_all(chip_out, 'kv', split_axis=0, concat_axis=0, tiled=True, a...]
    all_gather x1, blocking collectives: 1.87 us -> 4.26 us  [local(): lax.all_gather(partial_out, 'kv', axis_index_groups=[[2 * z, 2 * z + 1] f...]
    ppermute x4, waiting for transfers between devices: 11.7 us -> 9.57 us  [shift(): return lax.ppermute(x, 'kv', pairs)]
    ppermute x2, waiting for transfers between devices: 1.47 us -> 0.01 us  [swap(): return lax.ppermute(x, 'kv', [(i, i ^ 1) for i in range(kv_size)])]
    pallas_call x3 -> x5, Pallas kernels: 3.1 us -> 4.2 us  [copies(): pl.pallas_call(kernel, out_shape=tuple((pages(n) for n in out_pages)), in...]
    pallas_call x3 -> x4, Pallas kernels: 2.48 us -> 2.98 us  [the longest x1 1.15 us: local(): pl.pallas_call(land_taken_kernel, out_shape=pages(kv_size * CAP), in_spec...]
  transfers between devices with their start and end apart: 8 -> 8, of which waited for: 4 -> 4; matrix products, arithmetic and copies ran while one was open for 0% -> 0% of each run, Pallas kernels for 9% -> 10%
where the time goes in v9:
time: 89.7 us; the launch traced here: 88.5 us
  starting transfers between devices  45.7 us (51%)
  blocking collectives  17.6 us (20%)
  Pallas kernels  13.8 us (15%)
  waiting for transfers between devices  10.6 us (12%)
    ppermute x4, starting transfers between devices, shift(): return lax.ppermute(x, 'kv', pairs)  21.7 us
    all_to_all x1, blocking collectives, local(): lax.all_to_all(part, 'tp', split_axis=0, concat_axis=0, tiled=True)  13.3 us
    ppermute x2, starting transfers between devices, swap(): return lax.ppermute(x, 'kv', [(i, i ^ 1) for i in range(kv_size)])  13 us
    ppermute x4, waiting for transfers between devices, shift(): return lax.ppermute(x, 'kv', pairs)  9.57 us
    all_to_all x1, starting transfers between devices, local(): parts = lax.all_to_all(parts, 'kv', split_axis=0, concat_axis=0, tiled=True)  7.37 us
    all_gather x1, blocking collectives, local(): lax.all_gather(partial_out, 'kv', axis_index_groups=[[2 * z, 2 * z + 1] f...  4.26 us
    pallas_call x5, Pallas kernels, copies(): pl.pallas_call(kernel, out_shape=tuple((pages(n) for n in out_pages)), in...  4.2 us
    all_to_all x1, starting transfers between devices, local(): lax.all_to_all(chip_out, 'kv', split_axis=0, concat_axis=0, tiled=True, a...  3.68 us
  transfers between devices with their start and end apart: 8, of which 4 were waited for; matrix products, arithmetic and copies ran while one was open for 0% of the time, Pallas kernels for 10%

profile of v9, /device:TPU:1, one launch (start us, length us, event | category | flops | bytes accessed | tf_op | source)
XLA Modules:
  0.0 88.5 jit_solution(16531419950307389384)
XLA Ops:
  0.6 2.6 %pack.1 = (bf16[34,2,8,512]{3,2,1,0:T(8,128)(2,1)}, bf16[30,2,8,512]{3,2,1,0:T(8,128)(2,1)}) custom-call(bf16[32,2,8,512]{3,2,1,0:T(8,128)(2,1)} %move_ref.3, s32[32]{0:T(128)} %bitcast.7), custom_call_target="tpu_custom_call" | custom-call | tf_op jit(solution)/shard_map/pack/pallas_call | solution.py:294
  3.2 8.8 %collective-permute-start = (bf16[30,2,8,512]{3,2,1,0:T(8,128)(2,1)}, bf16[30,2,8,512]{3,2,1,0:T(8,128)(2,1)S(1)}, u32[]{:S(2)}, u32[]{:S(2)}) collective-permute-start(bf16[30,2,8,512]{3,2,1,0:T(8,128)(2,1)} %get-tuple-element.14), channel_id=1, source_target_pairs={{0,16},{16,0},{32,48},{48,32},{64,80},{80,64},{96,112},{112,96},{1... | collective-permute-start | bytes 1474568 | tf_op jit(solution)/shard_map/ppermute | solution.py:292
  12.0 0.0 copy-start
  12.0 3.2 %attend.1.after_ref = bf16[32,16,128]{2,1,0:T(8,128)(2,1)} custom-call(bf16[4,8192]{1,0:T(4,128)(2,1)} %q_ref.1, bf16[32,2,8,512]{3,2,1,0:T(8,128)(2,1)} %res_ref.1, bf16[32,2,8,512]{3,2,1,0:T(8,128)(2,1)} %move_ref.3, s32[1,4]{1,0:T(1,128)} %count_ref.1, s32[32]{0:T(128)} %request_ref.1, s32[1,32]{1,0:T(1,128)} %bitcast.8, s32[1,32]{1,0:T(1,128)} %bitcast.6), custom_call_target="tpu_custom_call" | custom-call | tf_op jit(solution)/shard_map/attend/pallas_call | solution.py:320
  15.2 0.0 collective-permute-done.got_ref
  15.2 0.0 copy-done
  15.2 1.0 %short.1 = (bf16[24,2,8,512]{3,2,1,0:T(8,128)(2,1)S(1)}, bf16[20,2,8,512]{3,2,1,0:T(8,128)(2,1)S(1)}) custom-call(bf16[34,2,8,512]{3,2,1,0:T(8,128)(2,1)S(1)} %copy-done, bf16[30,2,8,512]{3,2,1,0:T(8,128)(2,1)S(1)} %collective-permute-done.got_ref, bf16[32,16,128]{2,1,0:T(8,128)(2,1)} %attend.1.after_ref), custom_call_target="tpu_custom_call" | custom-call | bytes 1024 | tf_op jit(solution)/shard_map/short/pallas_call | solution.py:309
  16.2 5.8 %collective-permute-start.1 = (bf16[24,2,8,512]{3,2,1,0:T(8,128)(2,1)S(1)}, bf16[24,2,8,512]{3,2,1,0:T(8,128)(2,1)S(1)}, u32[]{:S(2)}, u32[]{:S(2)}) collective-permute-start(bf16[24,2,8,512]{3,2,1,0:T(8,128)(2,1)S(1)} %get-tuple-element.15), channel_id=1, source_target_pairs={{0,32},{16,496},{32,64},{48,16},{64,96},{80,48},{96,128},{112,80},... | collective-permute-start | bytes 1179656 | tf_op jit(solution)/shard_map/ppermute | solution.py:289
  22.0 3.1 %collective-permute-start.2 = (bf16[20,2,8,512]{3,2,1,0:T(8,128)(2,1)S(1)}, bf16[20,2,8,512]{3,2,1,0:T(8,128)(2,1)S(1)}, u32[]{:S(2)}, u32[]{:S(2)}) collective-permute-start(bf16[20,2,8,512]{3,2,1,0:T(8,128)(2,1)S(1)} %get-tuple-element.16), channel_id=1, source_target_pairs={{0,64},{16,464},{32,96},{48,496},{64,128},{80,16},{96,160},{112,48... | collective-permute-start | bytes 983048 | tf_op jit(solution)/shard_map/ppermute | solution.py:289
  25.1 7.4 %all-to-all-start = ((bf16[32,16,128]{2,1,0:T(8,128)(2,1)}), bf16[32,16,128]{2,1,0:T(8,128)(2,1)S(1)}, u32[]{:S(2)}, u32[]{:S(2)}) async-start(bf16[32,16,128]{2,1,0:T(8,128)(2,1)} %attend.1.after_ref), calls=%async_computation | async-start | bytes 262144 | tf_op jit(solution)/shard_map/all_to_all | solution.py:329
  32.5 1.4 %collective-permute-done.2.two_ref = bf16[20,2,8,512]{3,2,1,0:T(8,128)(2,1)S(1)} collective-permute-done((bf16[20,2,8,512]{3,2,1,0:T(8,128)(2,1)S(1)}, bf16[20,2,8,512]{3,2,1,0:T(8,128)(2,1)S(1)}, u32[]{:S(2)}, u32[]{:S(2)}) %collective-permute-start.2) | collective-permute-done | bytes 327712 | tf_op jit(solution)/shard_map/ppermute | solution.py:289
  33.9 0.0 collective-permute-done.1.one_ref
  33.9 0.5 three.1.after_ref
  34.4 5.0 %collective-permute-start.3 = (bf16[24,2,8,512]{3,2,1,0:T(8,128)(2,1)S(1)}, bf16[24,2,8,512]{3,2,1,0:T(8,128)(2,1)S(1)}, u32[]{:S(2)}, u32[]{:S(2)}) collective-permute-start(bf16[24,2,8,512]{3,2,1,0:T(8,128)(2,1)S(1)} %three.1.after_ref), channel_id=1, source_target_pairs={{0,96},{16,432},{32,128},{48,464},{64,160},{80,496},{96,192},{112,... | collective-permute-start | bytes 1179656 | tf_op jit(solution)/shard_map/ppermute | solution.py:289
  39.4 0.8 six.1
  40.2 7.8 %collective-permute-start.4 = (bf16[20,2,8,512]{3,2,1,0:T(8,128)(2,1)}, bf16[20,2,8,512]{3,2,1,0:T(8,128)(2,1)S(1)}, u32[]{:S(2)}, u32[]{:S(2)}) collective-permute-start(bf16[20,2,8,512]{3,2,1,0:T(8,128)(2,1)} %six.1), channel_id=1, source_target_pairs={{0,192},{16,336},{32,224},{48,368},{64,256},{80,400},{96,288},{112... | collective-permute-start | bytes 983048 | tf_op jit(solution)/shard_map/ppermute | solution.py:289
  48.0 0.0 copy-start.1
  48.1 0.3 all-to-all-done.parts_any
  48.4 0.9 column.1
  49.2 13.3 %all_to_all.15.parts_any = bf16[16,16,128]{2,1,0:T(8,128)(2,1)S(1)} all-to-all(bf16[16,16,128]{2,1,0:T(8,128)(2,1)S(1)} %get-tuple-element.12), channel_id=1, replica_groups=mesh['kv'=32,'tp'=16] {'tp'}, dimensions={0} | all-to-all | bytes 131072 | tf_op jit(solution)/shard_map/all_to_all | solution.py:357
  62.6 0.0 copy-done.1
  62.6 0.4 project.1
  62.9 4.3 %all-gather.1.parts_any = f32[2,4,1024]{2,1,0:T(4,128)S(1)} all-gather(f32[1,4,1024]{2,1,0:T(4,128)S(1)} %bitcast.5), channel_id=2, replica_groups={{0,16},{32,48},{64,80},{96,112},{128,144},{160,176},{192,208},{224,240}..., dimensions={0}, use_global_device_ids=true | all-gather | bytes 49152 | tf_op jit(solution)/shard_map/all_gather | solution.py:367
  67.2 0.7 pair.1.after_ref
  67.9 3.7 %all-to-all-start.2 = ((bf16[16,4,1024]{2,1,0:T(4,128)(2,1)}), bf16[16,4,1024]{2,1,0:T(4,128)(2,1)S(1)}, u32[]{:S(2)}, u32[]{:S(2)}) async-start(bf16[16,4,1024]{2,1,0:T(4,128)(2,1)} %pair.1.after_ref), calls=%async_computation.2 | async-start | bytes 262144 | tf_op jit(solution)/shard_map/all_to_all | solution.py:379
  71.6 8.2 %collective-permute-done.4.six_ref = bf16[20,2,8,512]{3,2,1,0:T(8,128)(2,1)S(1)} collective-permute-done((bf16[20,2,8,512]{3,2,1,0:T(8,128)(2,1)}, bf16[20,2,8,512]{3,2,1,0:T(8,128)(2,1)S(1)}, u32[]{:S(2)}, u32[]{:S(2)}) %collective-permute-start.4) | collective-permute-done | bytes 327712 | tf_op jit(solution)/shard_map/ppermute | solution.py:289
  79.7 0.0 collective-permute-done.3.three_ref
  79.7 0.9 %give.1 = bf16[30,2,8,512]{3,2,1,0:T(8,128)(2,1)} custom-call(bf16[24,2,8,512]{3,2,1,0:T(8,128)(2,1)S(1)} %collective-permute-done.1.one_ref, bf16[20,2,8,512]{3,2,1,0:T(8,128)(2,1)S(1)} %collective-permute-done.2.two_ref, bf16[24,2,8,512]{3,2,1,0:T(8,128)(2,1)S(1)} %collective-permute-done.3.three_ref, ...), custom_call_target="tpu_custom_call" | custom-call | bytes 1024 | tf_op jit(solution)/shard_map/give/pallas_call | solution.py:309
  80.6 4.2 %collective-permute-start.5 = (bf16[30,2,8,512]{3,2,1,0:T(8,128)(2,1)}, bf16[30,2,8,512]{3,2,1,0:T(8,128)(2,1)S(1)}, u32[]{:S(2)}, u32[]{:S(2)}) collective-permute-start(bf16[30,2,8,512]{3,2,1,0:T(8,128)(2,1)} %give.1), channel_id=1, source_target_pairs={{0,16},{16,0},{32,48},{48,32},{64,80},{80,64},{96,112},{112,96},{1... | collective-permute-start | bytes 1474568 | tf_op jit(solution)/shard_map/ppermute | solution.py:292
  84.9 1.0 %land.1.landed_ref = bf16[64,2,8,512]{3,2,1,0:T(8,128)(2,1)} custom-call(bf16[34,2,8,512]{3,2,1,0:T(8,128)(2,1)S(1)} %fill.1.after_ref.own_ref, bf16[30,2,8,512]{3,2,1,0:T(8,128)(2,1)S(1)} %collective-permute-done.got_ref, bf16[24,2,8,512]{3,2,1,0:T(8,128)(2,1)S(1)} %collective-permute-done.1.one_ref, ...), custom_call_target="tpu_custom_call" | custom-call | bytes 1024 | tf_op jit(solution)/shard_map/land/pallas_call | solution.py:309
  85.8 0.8 all-to-all-done.2.parts_any
  86.6 0.8 add.1
  87.4 0.0 collective-permute-done.5.taken_any
  87.4 1.2 %land_taken.1 = bf16[64,2,8,512]{3,2,1,0:T(8,128)(2,1)} custom-call(bf16[30,2,8,512]{3,2,1,0:T(8,128)(2,1)S(1)} %collective-permute-done.5.taken_any, bf16[64,2,8,512]{3,2,1,0:T(8,128)(2,1)} %land.1.landed_ref, bf16[34,2,8,512]{3,2,1,0:T(8,128)(2,1)S(1)} %get-tuple-element.17.after_ref), custom_call_target="tpu_custom_call", output_to_operand_aliasing={{}: (1, {})} | custom-call | bytes 1024 | tf_op jit(solution)/shard_map/land_taken/pallas_call | solution.py:400
  (1 shorter events, 0.0 us)
Async XLA Ops:
  3.2 12.0 %collective-permute-start = (bf16[30,2,8,512]{3,2,1,0:T(8,128)(2,1)}, bf16[30,2,8,512]{3,2,1,0:T(8,128)(2,1)S(1)}, u32[]{:S(2)}, u32[]{:S(2)}) collective-permute-start(bf16[30,2,8,512]{3,2,1,0:T(8,128)(2,1)} %get-tuple-element.14), channel_id=1, source_target_pairs={{0,16},{16,0},{32,48},{48,32},{64,80},{80,64},{96,112},{112,96},{1... | collective-permute-start | bytes 1474568 | tf_op jit(solution)/shard_map/ppermute | solution.py:292
  12.0 3.2 %copy-start = (bf16[34,2,8,512]{3,2,1,0:T(8,128)(2,1)S(1)}, bf16[34,2,8,512]{3,2,1,0:T(8,128)(2,1)}, u32[]{:S(2)}) copy-start(bf16[34,2,8,512]{3,2,1,0:T(8,128)(2,1)} %get-tuple-element.11.refs_0_.own_ref) | copy-start | bytes 1671172
  16.2 17.6 %collective-permute-start.1 = (bf16[24,2,8,512]{3,2,1,0:T(8,128)(2,1)S(1)}, bf16[24,2,8,512]{3,2,1,0:T(8,128)(2,1)S(1)}, u32[]{:S(2)}, u32[]{:S(2)}) collective-permute-start(bf16[24,2,8,512]{3,2,1,0:T(8,128)(2,1)S(1)} %get-tuple-element.15), channel_id=1, source_target_pairs={{0,32},{16,496},{32,64},{48,16},{64,96},{80,48},{96,128},{112,80},... | collective-permute-start | bytes 1179656 | tf_op jit(solution)/shard_map/ppermute | solution.py:289
  22.0 11.9 %collective-permute-start.2 = (bf16[20,2,8,512]{3,2,1,0:T(8,128)(2,1)S(1)}, bf16[20,2,8,512]{3,2,1,0:T(8,128)(2,1)S(1)}, u32[]{:S(2)}, u32[]{:S(2)}) collective-permute-start(bf16[20,2,8,512]{3,2,1,0:T(8,128)(2,1)S(1)} %get-tuple-element.16), channel_id=1, source_target_pairs={{0,64},{16,464},{32,96},{48,496},{64,128},{80,16},{96,160},{112,48... | collective-permute-start | bytes 983048 | tf_op jit(solution)/shard_map/ppermute | solution.py:289
  25.1 23.3 %all-to-all-start = ((bf16[32,16,128]{2,1,0:T(8,128)(2,1)}), bf16[32,16,128]{2,1,0:T(8,128)(2,1)S(1)}, u32[]{:S(2)}, u32[]{:S(2)}) async-start(bf16[32,16,128]{2,1,0:T(8,128)(2,1)} %attend.1.after_ref), calls=%async_computation | async-start | bytes 262144 | tf_op jit(solution)/shard_map/all_to_all | solution.py:329
  34.4 45.3 %collective-permute-start.3 = (bf16[24,2,8,512]{3,2,1,0:T(8,128)(2,1)S(1)}, bf16[24,2,8,512]{3,2,1,0:T(8,128)(2,1)S(1)}, u32[]{:S(2)}, u32[]{:S(2)}) collective-permute-start(bf16[24,2,8,512]{3,2,1,0:T(8,128)(2,1)S(1)} %three.1.after_ref), channel_id=1, source_target_pairs={{0,96},{16,432},{32,128},{48,464},{64,160},{80,496},{96,192},{112,... | collective-permute-start | bytes 1179656 | tf_op jit(solution)/shard_map/ppermute | solution.py:289
  40.2 39.5 %collective-permute-start.4 = (bf16[20,2,8,512]{3,2,1,0:T(8,128)(2,1)}, bf16[20,2,8,512]{3,2,1,0:T(8,128)(2,1)S(1)}, u32[]{:S(2)}, u32[]{:S(2)}) collective-permute-start(bf16[20,2,8,512]{3,2,1,0:T(8,128)(2,1)} %six.1), channel_id=1, source_target_pairs={{0,192},{16,336},{32,224},{48,368},{64,256},{80,400},{96,288},{112... | collective-permute-start | bytes 983048 | tf_op jit(solution)/shard_map/ppermute | solution.py:289
  48.0 14.5 %copy-start.1 = (bf16[256,1024]{1,0:T(8,128)(2,1)S(1)}, bf16[256,1024]{1,0:T(8,128)(2,1)}, u32[]{:S(2)}) copy-start(bf16[256,1024]{1,0:T(8,128)(2,1)} %weight_ref.1) | copy-start | bytes 1572868
  67.9 18.7 %all-to-all-start.2 = ((bf16[16,4,1024]{2,1,0:T(4,128)(2,1)}), bf16[16,4,1024]{2,1,0:T(4,128)(2,1)S(1)}, u32[]{:S(2)}, u32[]{:S(2)}) async-start(bf16[16,4,1024]{2,1,0:T(4,128)(2,1)} %pair.1.after_ref), calls=%async_computation.2 | async-start | bytes 262144 | tf_op jit(solution)/shard_map/all_to_all | solution.py:379
  80.6 6.7 %collective-permute-start.5 = (bf16[30,2,8,512]{3,2,1,0:T(8,128)(2,1)}, bf16[30,2,8,512]{3,2,1,0:T(8,128)(2,1)S(1)}, u32[]{:S(2)}, u32[]{:S(2)}) collective-permute-start(bf16[30,2,8,512]{3,2,1,0:T(8,128)(2,1)} %give.1), channel_id=1, source_target_pairs={{0,16},{16,0},{32,48},{48,32},{64,80},{80,64},{96,112},{112,96},{1... | collective-permute-start | bytes 1474568 | tf_op jit(solution)/shard_map/ppermute | solution.py:292

commit v10 on v9

--- a/solution.py
+++ b/solution.py
@@ -143,15 +143,23 @@
     copy_all([(other, other_out), (own, own_out)], sems)
 
 
-def short_kernel(own_ref, got_ref, after_ref, one_ref, two_ref, sems):
+def short_copies(n, own_ref, got_ref, out_ref):
+    copies = []
+    for m in range(3):
+        copies.append((quads(own_ref, n + 3 * m), quads(out_ref, 2 * m)))
+        if n + 3 * m < FAR - 1:
+            copies.append((quads(got_ref, n + 3 * m), quads(out_ref, 2 * m + 1)))
+    return copies
+
+
+def one_kernel(own_ref, got_ref, after_ref, out_ref, sems):
     del after_ref
-    copies = []
-    for n, ref in enumerate((one_ref, two_ref)):
-        for m in range(3):
-            copies.append((quads(own_ref, n + 3 * m), quads(ref, 2 * m)))
-            if n + 3 * m < FAR - 1:
-                copies.append((quads(got_ref, n + 3 * m), quads(ref, 2 * m + 1)))
-    copy_all(copies, sems)
+    copy_all(short_copies(0, own_ref, got_ref, out_ref), sems)
+
+
+def two_kernel(own_ref, got_ref, after_ref, out_ref, sems):
+    del after_ref
+    copy_all(short_copies(1, own_ref, got_ref, out_ref), sems)
 
 
 def long_copies(first, own_ref, got_ref, one_ref, two_ref, out_ref):
@@ -324,7 +332,8 @@
         out_specs=VMEM,
         name="attend",
     )(queries, res_cache, move_cache, res_count, move_request, owners[None, :], move_request[None, :])
-    one, two = copies(short_kernel, "short", (6 * QUAD, 5 * QUAD), 11, own, got, parts)
+    (one,) = copies(one_kernel, "one", (6 * QUAD,), 6, own, got, parts)
+    (two,) = copies(two_kernel, "two", (5 * QUAD,), 5, own, got, one)
     one, two = shift(one, 1), shift(two, 2)
     parts = lax.all_to_all(parts, "kv", split_axis=0, concat_axis=0, tiled=True)
     (three,) = copies(three_kernel, "three", (6 * QUAD,), 4, own, got, one, two)

time: 89.7 us -> 89.6 us (level)
  waiting for transfers between devices: 10.6 us -> 11.9 us
  starting transfers between devices: 45.7 us -> 44.5 us
    all_to_all x1, waiting for transfers between devices: 0.76 us -> 2.91 us  [local(): lax.all_to_all(chip_out, 'kv', split_axis=0, concat_axis=0, tiled=True, a...]
    ppermute x2, starting transfers between devices: 13 us -> 10.9 us  [swap(): return lax.ppermute(x, 'kv', [(i, i ^ 1) for i in range(kv_size)])]
    ppermute x4, waiting for transfers between devices: 9.57 us -> 8.58 us  [shift(): return lax.ppermute(x, 'kv', pairs)]
    pallas_call x5 -> x6, Pallas kernels: 4.2 us -> 4.21 us  [copies(): pl.pallas_call(kernel, out_shape=tuple((pages(n) for n in out_pages)), in...]
  transfers between devices with their start and end apart: 8 -> 8, of which waited for: 4 -> 4; matrix products, arithmetic and copies ran while one was open for 0% -> 0% of each run, Pallas kernels for 10% -> 11%
where the time goes in v10:
time: 89.6 us; the launch traced here: 88.5 us
  starting transfers between devices  44.5 us (50%)
  blocking collectives  17.5 us (20%)
  Pallas kernels  13.8 us (15%)
  waiting for transfers between devices  11.9 us (13%)
    ppermute x4, starting transfers between devices, shift(): return lax.ppermute(x, 'kv', pairs)  22.4 us
    all_to_all x1, blocking collectives, local(): lax.all_to_all(part, 'tp', split_axis=0, concat_axis=0, tiled=True)  13.3 us
    ppermute x2, starting transfers between devices, swap(): return lax.ppermute(x, 'kv', [(i, i ^ 1) for i in range(kv_size)])  10.9 us
    ppermute x4, waiting for transfers between devices, shift(): return lax.ppermute(x, 'kv', pairs)  8.58 us
    all_to_all x1, starting transfers between devices, local(): parts = lax.all_to_all(parts, 'kv', split_axis=0, concat_axis=0, tiled=True)  7.38 us
    pallas_call x6, Pallas kernels, copies(): pl.pallas_call(kernel, out_shape=tuple((pages(n) for n in out_pages)), in...  4.21 us
    all_gather x1, blocking collectives, local(): lax.all_gather(partial_out, 'kv', axis_index_groups=[[2 * z, 2 * z + 1] f...  4.16 us
    all_to_all x1, starting transfers between devices, local(): lax.all_to_all(chip_out, 'kv', split_axis=0, concat_axis=0, tiled=True, a...  3.83 us
  transfers between devices with their start and end apart: 8, of which 4 were waited for; matrix products, arithmetic and copies ran while one was open for 0% of the time, Pallas kernels for 11%

profile of v10, /device:TPU:1, one launch (start us, length us, event | category | flops | bytes accessed | tf_op | source)
XLA Modules:
  0.0 88.5 jit_solution(16953748145033778003)
XLA Ops:
  0.6 2.6 %pack.1 = (bf16[34,2,8,512]{3,2,1,0:T(8,128)(2,1)}, bf16[30,2,8,512]{3,2,1,0:T(8,128)(2,1)}) custom-call(bf16[32,2,8,512]{3,2,1,0:T(8,128)(2,1)} %move_ref.3, s32[32]{0:T(128)} %bitcast.7), custom_call_target="tpu_custom_call" | custom-call | tf_op jit(solution)/shard_map/pack/pallas_call | solution.py:302
  3.2 8.8 %collective-permute-start = (bf16[30,2,8,512]{3,2,1,0:T(8,128)(2,1)}, bf16[30,2,8,512]{3,2,1,0:T(8,128)(2,1)S(1)}, u32[]{:S(2)}, u32[]{:S(2)}) collective-permute-start(bf16[30,2,8,512]{3,2,1,0:T(8,128)(2,1)} %get-tuple-element.12), channel_id=1, source_target_pairs={{0,16},{16,0},{32,48},{48,32},{64,80},{80,64},{96,112},{112,96},{1... | collective-permute-start | bytes 1474568 | tf_op jit(solution)/shard_map/ppermute | solution.py:300
  12.0 0.0 copy-start
  12.0 3.2 %attend.1.after_ref = bf16[32,16,128]{2,1,0:T(8,128)(2,1)} custom-call(bf16[4,8192]{1,0:T(4,128)(2,1)} %q_ref.1, bf16[32,2,8,512]{3,2,1,0:T(8,128)(2,1)} %res_ref.1, bf16[32,2,8,512]{3,2,1,0:T(8,128)(2,1)} %move_ref.3, s32[1,4]{1,0:T(1,128)} %count_ref.1, s32[32]{0:T(128)} %request_ref.1, s32[1,32]{1,0:T(1,128)} %bitcast.8, s32[1,32]{1,0:T(1,128)} %bitcast.6), custom_call_target="tpu_custom_call" | custom-call | tf_op jit(solution)/shard_map/attend/pallas_call | solution.py:328
  15.2 0.0 collective-permute-done.got_ref
  15.2 0.0 copy-done
  15.2 0.6 one.1.after_ref
  15.8 5.8 %collective-permute-start.1 = (bf16[24,2,8,512]{3,2,1,0:T(8,128)(2,1)S(1)}, bf16[24,2,8,512]{3,2,1,0:T(8,128)(2,1)S(1)}, u32[]{:S(2)}, u32[]{:S(2)}) collective-permute-start(bf16[24,2,8,512]{3,2,1,0:T(8,128)(2,1)S(1)} %one.1.after_ref), channel_id=1, source_target_pairs={{0,32},{16,496},{32,64},{48,16},{64,96},{80,48},{96,128},{112,80},... | collective-permute-start | bytes 1179656 | tf_op jit(solution)/shard_map/ppermute | solution.py:297
  21.5 0.5 two.1
  22.0 3.1 %collective-permute-start.2 = (bf16[20,2,8,512]{3,2,1,0:T(8,128)(2,1)S(1)}, bf16[20,2,8,512]{3,2,1,0:T(8,128)(2,1)S(1)}, u32[]{:S(2)}, u32[]{:S(2)}) collective-permute-start(bf16[20,2,8,512]{3,2,1,0:T(8,128)(2,1)S(1)} %two.1), channel_id=1, source_target_pairs={{0,64},{16,464},{32,96},{48,496},{64,128},{80,16},{96,160},{112,48... | collective-permute-start | bytes 983048 | tf_op jit(solution)/shard_map/ppermute | solution.py:297
  25.1 7.4 %all-to-all-start = ((bf16[32,16,128]{2,1,0:T(8,128)(2,1)}), bf16[32,16,128]{2,1,0:T(8,128)(2,1)S(1)}, u32[]{:S(2)}, u32[]{:S(2)}) async-start(bf16[32,16,128]{2,1,0:T(8,128)(2,1)} %attend.1.after_ref), calls=%async_computation | async-start | bytes 262144 | tf_op jit(solution)/shard_map/all_to_all | solution.py:338
  32.5 0.7 collective-permute-done.2.two_ref
  33.2 0.0 collective-permute-done.1.one_ref
  33.2 0.5 three.1.after_ref
  33.7 5.7 %collective-permute-start.3 = (bf16[24,2,8,512]{3,2,1,0:T(8,128)(2,1)S(1)}, bf16[24,2,8,512]{3,2,1,0:T(8,128)(2,1)S(1)}, u32[]{:S(2)}, u32[]{:S(2)}) collective-permute-start(bf16[24,2,8,512]{3,2,1,0:T(8,128)(2,1)S(1)} %three.1.after_ref), channel_id=1, source_target_pairs={{0,96},{16,432},{32,128},{48,464},{64,160},{80,496},{96,192},{112,... | collective-permute-start | bytes 1179656 | tf_op jit(solution)/shard_map/ppermute | solution.py:297
  39.4 0.8 six.1
  40.2 7.8 %collective-permute-start.4 = (bf16[20,2,8,512]{3,2,1,0:T(8,128)(2,1)}, bf16[20,2,8,512]{3,2,1,0:T(8,128)(2,1)S(1)}, u32[]{:S(2)}, u32[]{:S(2)}) collective-permute-start(bf16[20,2,8,512]{3,2,1,0:T(8,128)(2,1)} %six.1), channel_id=1, source_target_pairs={{0,192},{16,336},{32,224},{48,368},{64,256},{80,400},{96,288},{112... | collective-permute-start | bytes 983048 | tf_op jit(solution)/shard_map/ppermute | solution.py:297
  48.1 0.0 copy-start.1
  48.1 0.4 all-to-all-done.parts_any
  48.5 0.9 column.1
  49.3 13.3 %all_to_all.15.parts_any = bf16[16,16,128]{2,1,0:T(8,128)(2,1)S(1)} all-to-all(bf16[16,16,128]{2,1,0:T(8,128)(2,1)S(1)} %get-tuple-element.10), channel_id=1, replica_groups=mesh['kv'=32,'tp'=16] {'tp'}, dimensions={0} | all-to-all | bytes 131072 | tf_op jit(solution)/shard_map/all_to_all | solution.py:366
  62.7 0.0 copy-done.1
  62.7 0.4 project.1
  63.1 4.2 %all-gather.1.parts_any = f32[2,4,1024]{2,1,0:T(4,128)S(1)} all-gather(f32[1,4,1024]{2,1,0:T(4,128)S(1)} %bitcast.5), channel_id=2, replica_groups={{0,16},{32,48},{64,80},{96,112},{128,144},{160,176},{192,208},{224,240}..., dimensions={0}, use_global_device_ids=true | all-gather | bytes 49152 | tf_op jit(solution)/shard_map/all_gather | solution.py:376
  67.2 0.7 pair.1.after_ref
  67.9 3.8 %all-to-all-start.2 = ((bf16[16,4,1024]{2,1,0:T(4,128)(2,1)}), bf16[16,4,1024]{2,1,0:T(4,128)(2,1)S(1)}, u32[]{:S(2)}, u32[]{:S(2)}) async-start(bf16[16,4,1024]{2,1,0:T(4,128)(2,1)} %pair.1.after_ref), calls=%async_computation.2 | async-start | bytes 262144 | tf_op jit(solution)/shard_map/all_to_all | solution.py:388
  71.7 7.9 %collective-permute-done.4.six_ref = bf16[20,2,8,512]{3,2,1,0:T(8,128)(2,1)S(1)} collective-permute-done((bf16[20,2,8,512]{3,2,1,0:T(8,128)(2,1)}, bf16[20,2,8,512]{3,2,1,0:T(8,128)(2,1)S(1)}, u32[]{:S(2)}, u32[]{:S(2)}) %collective-permute-start.4) | collective-permute-done | bytes 327712 | tf_op jit(solution)/shard_map/ppermute | solution.py:297
  79.6 0.0 collective-permute-done.3.three_ref
  79.6 0.9 %give.1 = bf16[30,2,8,512]{3,2,1,0:T(8,128)(2,1)} custom-call(bf16[24,2,8,512]{3,2,1,0:T(8,128)(2,1)S(1)} %collective-permute-done.1.one_ref, bf16[20,2,8,512]{3,2,1,0:T(8,128)(2,1)S(1)} %collective-permute-done.2.two_ref, bf16[24,2,8,512]{3,2,1,0:T(8,128)(2,1)S(1)} %collective-permute-done.3.three_ref, ...), custom_call_target="tpu_custom_call" | custom-call | bytes 1024 | tf_op jit(solution)/shard_map/give/pallas_call | solution.py:317
  80.5 2.1 %collective-permute-start.5 = (bf16[30,2,8,512]{3,2,1,0:T(8,128)(2,1)}, bf16[30,2,8,512]{3,2,1,0:T(8,128)(2,1)S(1)}, u32[]{:S(2)}, u32[]{:S(2)}) collective-permute-start(bf16[30,2,8,512]{3,2,1,0:T(8,128)(2,1)} %give.1), channel_id=1, source_target_pairs={{0,16},{16,0},{32,48},{48,32},{64,80},{80,64},{96,112},{112,96},{1... | collective-permute-start | bytes 1474568 | tf_op jit(solution)/shard_map/ppermute | solution.py:300
  82.7 1.0 %land.1.landed_ref = bf16[64,2,8,512]{3,2,1,0:T(8,128)(2,1)} custom-call(bf16[34,2,8,512]{3,2,1,0:T(8,128)(2,1)S(1)} %fill.1.after_ref.own_ref, bf16[30,2,8,512]{3,2,1,0:T(8,128)(2,1)S(1)} %collective-permute-done.got_ref, bf16[24,2,8,512]{3,2,1,0:T(8,128)(2,1)S(1)} %collective-permute-done.1.one_ref, ...), custom_call_target="tpu_custom_call" | custom-call | bytes 1024 | tf_op jit(solution)/shard_map/land/pallas_call | solution.py:317
  83.6 2.9 %all-to-all-done.2.parts_any = bf16[16,4,1024]{2,1,0:T(4,128)(2,1)S(1)} async-done(((bf16[16,4,1024]{2,1,0:T(4,128)(2,1)}), bf16[16,4,1024]{2,1,0:T(4,128)(2,1)S(1)}, u32[]{:S(2)}, u32[]{:S(2)}) %all-to-all-start.2) | async-done | bytes 131104 | tf_op jit(solution)/shard_map/all_to_all | solution.py:388
  86.5 0.8 add.1
  87.3 0.0 collective-permute-done.5.taken_any
  87.3 1.2 %land_taken.1 = bf16[64,2,8,512]{3,2,1,0:T(8,128)(2,1)} custom-call(bf16[30,2,8,512]{3,2,1,0:T(8,128)(2,1)S(1)} %collective-permute-done.5.taken_any, bf16[64,2,8,512]{3,2,1,0:T(8,128)(2,1)} %land.1.landed_ref, bf16[34,2,8,512]{3,2,1,0:T(8,128)(2,1)S(1)} %get-tuple-element.13.after_ref), custom_call_target="tpu_custom_call", output_to_operand_aliasing={{}: (1, {})} | custom-call | bytes 1024 | tf_op jit(solution)/shard_map/land_taken/pallas_call | solution.py:409
  (1 shorter events, 0.0 us)
Async XLA Ops:
  3.2 12.0 %collective-permute-start = (bf16[30,2,8,512]{3,2,1,0:T(8,128)(2,1)}, bf16[30,2,8,512]{3,2,1,0:T(8,128)(2,1)S(1)}, u32[]{:S(2)}, u32[]{:S(2)}) collective-permute-start(bf16[30,2,8,512]{3,2,1,0:T(8,128)(2,1)} %get-tuple-element.12), channel_id=1, source_target_pairs={{0,16},{16,0},{32,48},{48,32},{64,80},{80,64},{96,112},{112,96},{1... | collective-permute-start | bytes 1474568 | tf_op jit(solution)/shard_map/ppermute | solution.py:300
  12.0 3.2 %copy-start = (bf16[34,2,8,512]{3,2,1,0:T(8,128)(2,1)S(1)}, bf16[34,2,8,512]{3,2,1,0:T(8,128)(2,1)}, u32[]{:S(2)}) copy-start(bf16[34,2,8,512]{3,2,1,0:T(8,128)(2,1)} %get-tuple-element.9.refs_0_.own_ref) | copy-start | bytes 1671172
  15.8 17.4 %collective-permute-start.1 = (bf16[24,2,8,512]{3,2,1,0:T(8,128)(2,1)S(1)}, bf16[24,2,8,512]{3,2,1,0:T(8,128)(2,1)S(1)}, u32[]{:S(2)}, u32[]{:S(2)}) collective-permute-start(bf16[24,2,8,512]{3,2,1,0:T(8,128)(2,1)S(1)} %one.1.after_ref), channel_id=1, source_target_pairs={{0,32},{16,496},{32,64},{48,16},{64,96},{80,48},{96,128},{112,80},... | collective-permute-start | bytes 1179656 | tf_op jit(solution)/shard_map/ppermute | solution.py:297
  22.0 11.2 %collective-permute-start.2 = (bf16[20,2,8,512]{3,2,1,0:T(8,128)(2,1)S(1)}, bf16[20,2,8,512]{3,2,1,0:T(8,128)(2,1)S(1)}, u32[]{:S(2)}, u32[]{:S(2)}) collective-permute-start(bf16[20,2,8,512]{3,2,1,0:T(8,128)(2,1)S(1)} %two.1), channel_id=1, source_target_pairs={{0,64},{16,464},{32,96},{48,496},{64,128},{80,16},{96,160},{112,48... | collective-permute-start | bytes 983048 | tf_op jit(solution)/shard_map/ppermute | solution.py:297
  25.1 23.4 %all-to-all-start = ((bf16[32,16,128]{2,1,0:T(8,128)(2,1)}), bf16[32,16,128]{2,1,0:T(8,128)(2,1)S(1)}, u32[]{:S(2)}, u32[]{:S(2)}) async-start(bf16[32,16,128]{2,1,0:T(8,128)(2,1)} %attend.1.after_ref), calls=%async_computation | async-start | bytes 262144 | tf_op jit(solution)/shard_map/all_to_all | solution.py:338
  33.7 45.9 %collective-permute-start.3 = (bf16[24,2,8,512]{3,2,1,0:T(8,128)(2,1)S(1)}, bf16[24,2,8,512]{3,2,1,0:T(8,128)(2,1)S(1)}, u32[]{:S(2)}, u32[]{:S(2)}) collective-permute-start(bf16[24,2,8,512]{3,2,1,0:T(8,128)(2,1)S(1)} %three.1.after_ref), channel_id=1, source_target_pairs={{0,96},{16,432},{32,128},{48,464},{64,160},{80,496},{96,192},{112,... | collective-permute-start | bytes 1179656 | tf_op jit(solution)/shard_map/ppermute | solution.py:297
  40.2 39.4 %collective-permute-start.4 = (bf16[20,2,8,512]{3,2,1,0:T(8,128)(2,1)}, bf16[20,2,8,512]{3,2,1,0:T(8,128)(2,1)S(1)}, u32[]{:S(2)}, u32[]{:S(2)}) collective-permute-start(bf16[20,2,8,512]{3,2,1,0:T(8,128)(2,1)} %six.1), channel_id=1, source_target_pairs={{0,192},{16,336},{32,224},{48,368},{64,256},{80,400},{96,288},{112... | collective-permute-start | bytes 983048 | tf_op jit(solution)/shard_map/ppermute | solution.py:297
  48.1 14.6 %copy-start.1 = (bf16[256,1024]{1,0:T(8,128)(2,1)S(1)}, bf16[256,1024]{1,0:T(8,128)(2,1)}, u32[]{:S(2)}) copy-start(bf16[256,1024]{1,0:T(8,128)(2,1)} %weight_ref.1) | copy-start | bytes 1572868
  67.9 18.6 %all-to-all-start.2 = ((bf16[16,4,1024]{2,1,0:T(4,128)(2,1)}), bf16[16,4,1024]{2,1,0:T(4,128)(2,1)S(1)}, u32[]{:S(2)}, u32[]{:S(2)}) async-start(bf16[16,4,1024]{2,1,0:T(4,128)(2,1)} %pair.1.after_ref), calls=%async_computation.2 | async-start | bytes 262144 | tf_op jit(solution)/shard_map/all_to_all | solution.py:388
  80.5 6.8 %collective-permute-start.5 = (bf16[30,2,8,512]{3,2,1,0:T(8,128)(2,1)}, bf16[30,2,8,512]{3,2,1,0:T(8,128)(2,1)S(1)}, u32[]{:S(2)}, u32[]{:S(2)}) collective-permute-start(bf16[30,2,8,512]{3,2,1,0:T(8,128)(2,1)} %give.1), channel_id=1, source_target_pairs={{0,16},{16,0},{32,48},{48,32},{64,80},{80,64},{96,112},{112,96},{1... | collective-permute-start | bytes 1474568 | tf_op jit(solution)/shard_map/ppermute | solution.py:300

commit v11 on v10

--- a/solution.py
+++ b/solution.py
@@ -197,11 +197,15 @@
 def give_kernel(one_ref, two_ref, three_ref, six_ref, after_ref, out_ref, sems):
     del after_ref
     core = lax.axis_index("kv") % 2
+    page = out_ref.shape[1:]
     copies = [(six_ref.at[pl.ds(4 * QUAD + CAP, CAP)], out_ref.at[pl.ds(GIVEN, CAP)])]
-    for distance, ref, quad in arrived(one_ref, two_ref, three_ref, six_ref):
-        for quad, start in ((quad, core), (quad + 1, 1 - core)):
-            to = out_ref.at[pl.ds((distance - 1) * QUAD + start * CAP, CAP)]
-            copies.append((ref.at[pl.ds(quad * QUAD + CAP, CAP)], to))
+    to = out_ref.at[pl.ds(0, GIVEN)].reshape((FAR - 1, 2, CAP) + page)
+    for ref, distance, count in ((one_ref, 1, 1), (two_ref, 2, 1), (three_ref, 3, 3), (six_ref, 6, 2)):
+        chunks = ref.at[pl.ds(0, 2 * QUAD * count)].reshape((count, 2, QUAD) + page)
+        for other in range(2):
+            start = core + other * (1 - 2 * core)
+            source = chunks.at[:, other, pl.ds(CAP, CAP)]
+            copies.append((source, to.at[pl.ds(distance - 1, count), start]))
     copy_all(copies, sems)
 
 
@@ -393,7 +397,7 @@
         tiled=True,
         axis_index_groups=[[2 * z + c for z in range(CHIPS)] for c in range(2)],
     )
-    (give,) = copies(give_kernel, "give", (GIVEN + CAP,), 15, one, two, three, six, chip_out)
+    (give,) = copies(give_kernel, "give", (GIVEN + CAP,), 9, one, two, three, six, chip_out)
     taken = swap(give)
     (landed,) = copies(land_kernel, "land", (kv_size * CAP,), 17, own, got, one, two, three, six)
     mixed, own = pl.pallas_call(

time: 89.6 us -> 89.6 us (level)
  no operation moved by 1% of the time
where the time goes in v11:
time: 89.6 us; the launch traced here: 88.5 us
  starting transfers between devices  44.5 us (50%)
  blocking collectives  17.5 us (20%)
  Pallas kernels  13.8 us (15%)
  waiting for transfers between devices  12 us (13%)
    ppermute x4, starting transfers between devices, shift(): return lax.ppermute(x, 'kv', pairs)  22.4 us
    all_to_all x1, blocking collectives, local(): lax.all_to_all(part, 'tp', split_axis=0, concat_axis=0, tiled=True)  13.3 us
    ppermute x2, starting transfers between devices, swap(): return lax.ppermute(x, 'kv', [(i, i ^ 1) for i in range(kv_size)])  10.9 us
    ppermute x4, waiting for transfers between devices, shift(): return lax.ppermute(x, 'kv', pairs)  8.58 us
    all_to_all x1, starting transfers between devices, local(): parts = lax.all_to_all(parts, 'kv', split_axis=0, concat_axis=0, tiled=True)  7.38 us
    all_gather x1, blocking collectives, local(): lax.all_gather(partial_out, 'kv', axis_index_groups=[[2 * z, 2 * z + 1] f...  4.16 us
    pallas_call x6, Pallas kernels, copies(): pl.pallas_call(kernel, out_shape=tuple((pages(n) for n in out_pages)), in...  4.16 us
    all_to_all x1, starting transfers between devices, local(): lax.all_to_all(chip_out, 'kv', split_axis=0, concat_axis=0, tiled=True, a...  3.83 us
  transfers between devices with their start and end apart: 8, of which 4 were waited for; matrix products, arithmetic and copies ran while one was open for 0% of the time, Pallas kernels for 11%

profile of v11, /device:TPU:1, one launch (start us, length us, event | category | flops | bytes accessed | tf_op | source)
XLA Modules:
  0.0 88.5 jit_solution(2552873005169459321)
XLA Ops:
  0.6 2.6 %pack.1 = (bf16[34,2,8,512]{3,2,1,0:T(8,128)(2,1)}, bf16[30,2,8,512]{3,2,1,0:T(8,128)(2,1)}) custom-call(bf16[32,2,8,512]{3,2,1,0:T(8,128)(2,1)} %move_ref.3, s32[32]{0:T(128)} %bitcast.7), custom_call_target="tpu_custom_call" | custom-call | tf_op jit(solution)/shard_map/pack/pallas_call | solution.py:306
  3.2 8.8 %collective-permute-start = (bf16[30,2,8,512]{3,2,1,0:T(8,128)(2,1)}, bf16[30,2,8,512]{3,2,1,0:T(8,128)(2,1)S(1)}, u32[]{:S(2)}, u32[]{:S(2)}) collective-permute-start(bf16[30,2,8,512]{3,2,1,0:T(8,128)(2,1)} %get-tuple-element.12), channel_id=1, source_target_pairs={{0,16},{16,0},{32,48},{48,32},{64,80},{80,64},{96,112},{112,96},{1... | collective-permute-start | bytes 1474568 | tf_op jit(solution)/shard_map/ppermute | solution.py:304
  12.0 0.0 copy-start
  12.0 3.2 %attend.1.after_ref = bf16[32,16,128]{2,1,0:T(8,128)(2,1)} custom-call(bf16[4,8192]{1,0:T(4,128)(2,1)} %q_ref.1, bf16[32,2,8,512]{3,2,1,0:T(8,128)(2,1)} %res_ref.1, bf16[32,2,8,512]{3,2,1,0:T(8,128)(2,1)} %move_ref.3, s32[1,4]{1,0:T(1,128)} %count_ref.1, s32[32]{0:T(128)} %request_ref.1, s32[1,32]{1,0:T(1,128)} %bitcast.8, s32[1,32]{1,0:T(1,128)} %bitcast.6), custom_call_target="tpu_custom_call" | custom-call | tf_op jit(solution)/shard_map/attend/pallas_call | solution.py:332
  15.2 0.0 collective-permute-done.got_ref
  15.2 0.0 copy-done
  15.2 0.6 one.1.after_ref
  15.8 5.8 %collective-permute-start.1 = (bf16[24,2,8,512]{3,2,1,0:T(8,128)(2,1)S(1)}, bf16[24,2,8,512]{3,2,1,0:T(8,128)(2,1)S(1)}, u32[]{:S(2)}, u32[]{:S(2)}) collective-permute-start(bf16[24,2,8,512]{3,2,1,0:T(8,128)(2,1)S(1)} %one.1.after_ref), channel_id=1, source_target_pairs={{0,32},{16,496},{32,64},{48,16},{64,96},{80,48},{96,128},{112,80},... | collective-permute-start | bytes 1179656 | tf_op jit(solution)/shard_map/ppermute | solution.py:301
  21.5 0.5 two.1
  22.0 3.1 %collective-permute-start.2 = (bf16[20,2,8,512]{3,2,1,0:T(8,128)(2,1)S(1)}, bf16[20,2,8,512]{3,2,1,0:T(8,128)(2,1)S(1)}, u32[]{:S(2)}, u32[]{:S(2)}) collective-permute-start(bf16[20,2,8,512]{3,2,1,0:T(8,128)(2,1)S(1)} %two.1), channel_id=1, source_target_pairs={{0,64},{16,464},{32,96},{48,496},{64,128},{80,16},{96,160},{112,48... | collective-permute-start | bytes 983048 | tf_op jit(solution)/shard_map/ppermute | solution.py:301
  25.1 7.4 %all-to-all-start = ((bf16[32,16,128]{2,1,0:T(8,128)(2,1)}), bf16[32,16,128]{2,1,0:T(8,128)(2,1)S(1)}, u32[]{:S(2)}, u32[]{:S(2)}) async-start(bf16[32,16,128]{2,1,0:T(8,128)(2,1)} %attend.1.after_ref), calls=%async_computation | async-start | bytes 262144 | tf_op jit(solution)/shard_map/all_to_all | solution.py:342
  32.5 0.7 collective-permute-done.2.two_ref
  33.2 0.0 collective-permute-done.1.one_ref
  33.2 0.5 three.1.after_ref
  33.7 5.7 %collective-permute-start.3 = (bf16[24,2,8,512]{3,2,1,0:T(8,128)(2,1)S(1)}, bf16[24,2,8,512]{3,2,1,0:T(8,128)(2,1)S(1)}, u32[]{:S(2)}, u32[]{:S(2)}) collective-permute-start(bf16[24,2,8,512]{3,2,1,0:T(8,128)(2,1)S(1)} %three.1.after_ref), channel_id=1, source_target_pairs={{0,96},{16,432},{32,128},{48,464},{64,160},{80,496},{96,192},{112,... | collective-permute-start | bytes 1179656 | tf_op jit(solution)/shard_map/ppermute | solution.py:301
  39.4 0.8 six.1
  40.2 7.8 %collective-permute-start.4 = (bf16[20,2,8,512]{3,2,1,0:T(8,128)(2,1)}, bf16[20,2,8,512]{3,2,1,0:T(8,128)(2,1)S(1)}, u32[]{:S(2)}, u32[]{:S(2)}) collective-permute-start(bf16[20,2,8,512]{3,2,1,0:T(8,128)(2,1)} %six.1), channel_id=1, source_target_pairs={{0,192},{16,336},{32,224},{48,368},{64,256},{80,400},{96,288},{112... | collective-permute-start | bytes 983048 | tf_op jit(solution)/shard_map/ppermute | solution.py:301
  48.1 0.0 copy-start.1
  48.1 0.4 all-to-all-done.parts_any
  48.5 0.9 column.1
  49.3 13.3 %all_to_all.15.parts_any = bf16[16,16,128]{2,1,0:T(8,128)(2,1)S(1)} all-to-all(bf16[16,16,128]{2,1,0:T(8,128)(2,1)S(1)} %get-tuple-element.10), channel_id=1, replica_groups=mesh['kv'=32,'tp'=16] {'tp'}, dimensions={0} | all-to-all | bytes 131072 | tf_op jit(solution)/shard_map/all_to_all | solution.py:370
  62.7 0.0 copy-done.1
  62.7 0.4 project.1
  63.1 4.2 %all-gather.1.parts_any = f32[2,4,1024]{2,1,0:T(4,128)S(1)} all-gather(f32[1,4,1024]{2,1,0:T(4,128)S(1)} %bitcast.5), channel_id=2, replica_groups={{0,16},{32,48},{64,80},{96,112},{128,144},{160,176},{192,208},{224,240}..., dimensions={0}, use_global_device_ids=true | all-gather | bytes 49152 | tf_op jit(solution)/shard_map/all_gather | solution.py:380
  67.2 0.7 pair.1.after_ref
  67.9 3.8 %all-to-all-start.2 = ((bf16[16,4,1024]{2,1,0:T(4,128)(2,1)}), bf16[16,4,1024]{2,1,0:T(4,128)(2,1)S(1)}, u32[]{:S(2)}, u32[]{:S(2)}) async-start(bf16[16,4,1024]{2,1,0:T(4,128)(2,1)} %pair.1.after_ref), calls=%async_computation.2 | async-start | bytes 262144 | tf_op jit(solution)/shard_map/all_to_all | solution.py:392
  71.7 7.9 %collective-permute-done.4.six_ref = bf16[20,2,8,512]{3,2,1,0:T(8,128)(2,1)S(1)} collective-permute-done((bf16[20,2,8,512]{3,2,1,0:T(8,128)(2,1)}, bf16[20,2,8,512]{3,2,1,0:T(8,128)(2,1)S(1)}, u32[]{:S(2)}, u32[]{:S(2)}) %collective-permute-start.4) | collective-permute-done | bytes 327712 | tf_op jit(solution)/shard_map/ppermute | solution.py:301
  79.6 0.0 collective-permute-done.3.three_ref
  79.6 0.9 give.1
  80.5 2.1 %collective-permute-start.5 = (bf16[30,2,8,512]{3,2,1,0:T(8,128)(2,1)}, bf16[30,2,8,512]{3,2,1,0:T(8,128)(2,1)S(1)}, u32[]{:S(2)}, u32[]{:S(2)}) collective-permute-start(bf16[30,2,8,512]{3,2,1,0:T(8,128)(2,1)} %give.1), channel_id=1, source_target_pairs={{0,16},{16,0},{32,48},{48,32},{64,80},{80,64},{96,112},{112,96},{1... | collective-permute-start | bytes 1474568 | tf_op jit(solution)/shard_map/ppermute | solution.py:304
  82.6 1.0 %land.1.landed_ref = bf16[64,2,8,512]{3,2,1,0:T(8,128)(2,1)} custom-call(bf16[34,2,8,512]{3,2,1,0:T(8,128)(2,1)S(1)} %fill.1.after_ref.own_ref, bf16[30,2,8,512]{3,2,1,0:T(8,128)(2,1)S(1)} %collective-permute-done.got_ref, bf16[24,2,8,512]{3,2,1,0:T(8,128)(2,1)S(1)} %collective-permute-done.1.one_ref, ...), custom_call_target="tpu_custom_call" | custom-call | bytes 1024 | tf_op jit(solution)/shard_map/land/pallas_call | solution.py:321
  83.6 3.0 %all-to-all-done.2.parts_any = bf16[16,4,1024]{2,1,0:T(4,128)(2,1)S(1)} async-done(((bf16[16,4,1024]{2,1,0:T(4,128)(2,1)}), bf16[16,4,1024]{2,1,0:T(4,128)(2,1)S(1)}, u32[]{:S(2)}, u32[]{:S(2)}) %all-to-all-start.2) | async-done | bytes 131104 | tf_op jit(solution)/shard_map/all_to_all | solution.py:392
  86.5 0.8 add.1
  87.3 0.0 collective-permute-done.5.taken_any
  87.3 1.2 %land_taken.1 = bf16[64,2,8,512]{3,2,1,0:T(8,128)(2,1)} custom-call(bf16[30,2,8,512]{3,2,1,0:T(8,128)(2,1)S(1)} %collective-permute-done.5.taken_any, bf16[64,2,8,512]{3,2,1,0:T(8,128)(2,1)} %land.1.landed_ref, bf16[34,2,8,512]{3,2,1,0:T(8,128)(2,1)S(1)} %get-tuple-element.13.after_ref), custom_call_target="tpu_custom_call", output_to_operand_aliasing={{}: (1, {})} | custom-call | bytes 1024 | tf_op jit(solution)/shard_map/land_taken/pallas_call | solution.py:413
  (1 shorter events, 0.0 us)
Async XLA Ops:
  3.2 12.0 %collective-permute-start = (bf16[30,2,8,512]{3,2,1,0:T(8,128)(2,1)}, bf16[30,2,8,512]{3,2,1,0:T(8,128)(2,1)S(1)}, u32[]{:S(2)}, u32[]{:S(2)}) collective-permute-start(bf16[30,2,8,512]{3,2,1,0:T(8,128)(2,1)} %get-tuple-element.12), channel_id=1, source_target_pairs={{0,16},{16,0},{32,48},{48,32},{64,80},{80,64},{96,112},{112,96},{1... | collective-permute-start | bytes 1474568 | tf_op jit(solution)/shard_map/ppermute | solution.py:304
  12.0 3.2 %copy-start = (bf16[34,2,8,512]{3,2,1,0:T(8,128)(2,1)S(1)}, bf16[34,2,8,512]{3,2,1,0:T(8,128)(2,1)}, u32[]{:S(2)}) copy-start(bf16[34,2,8,512]{3,2,1,0:T(8,128)(2,1)} %get-tuple-element.9.refs_0_.own_ref) | copy-start | bytes 1671172
  15.8 17.4 %collective-permute-start.1 = (bf16[24,2,8,512]{3,2,1,0:T(8,128)(2,1)S(1)}, bf16[24,2,8,512]{3,2,1,0:T(8,128)(2,1)S(1)}, u32[]{:S(2)}, u32[]{:S(2)}) collective-permute-start(bf16[24,2,8,512]{3,2,1,0:T(8,128)(2,1)S(1)} %one.1.after_ref), channel_id=1, source_target_pairs={{0,32},{16,496},{32,64},{48,16},{64,96},{80,48},{96,128},{112,80},... | collective-permute-start | bytes 1179656 | tf_op jit(solution)/shard_map/ppermute | solution.py:301
  22.0 11.2 %collective-permute-start.2 = (bf16[20,2,8,512]{3,2,1,0:T(8,128)(2,1)S(1)}, bf16[20,2,8,512]{3,2,1,0:T(8,128)(2,1)S(1)}, u32[]{:S(2)}, u32[]{:S(2)}) collective-permute-start(bf16[20,2,8,512]{3,2,1,0:T(8,128)(2,1)S(1)} %two.1), channel_id=1, source_target_pairs={{0,64},{16,464},{32,96},{48,496},{64,128},{80,16},{96,160},{112,48... | collective-permute-start | bytes 983048 | tf_op jit(solution)/shard_map/ppermute | solution.py:301
  25.1 23.4 %all-to-all-start = ((bf16[32,16,128]{2,1,0:T(8,128)(2,1)}), bf16[32,16,128]{2,1,0:T(8,128)(2,1)S(1)}, u32[]{:S(2)}, u32[]{:S(2)}) async-start(bf16[32,16,128]{2,1,0:T(8,128)(2,1)} %attend.1.after_ref), calls=%async_computation | async-start | bytes 262144 | tf_op jit(solution)/shard_map/all_to_all | solution.py:342
  33.7 45.9 %collective-permute-start.3 = (bf16[24,2,8,512]{3,2,1,0:T(8,128)(2,1)S(1)}, bf16[24,2,8,512]{3,2,1,0:T(8,128)(2,1)S(1)}, u32[]{:S(2)}, u32[]{:S(2)}) collective-permute-start(bf16[24,2,8,512]{3,2,1,0:T(8,128)(2,1)S(1)} %three.1.after_ref), channel_id=1, source_target_pairs={{0,96},{16,432},{32,128},{48,464},{64,160},{80,496},{96,192},{112,... | collective-permute-start | bytes 1179656 | tf_op jit(solution)/shard_map/ppermute | solution.py:301
  40.2 39.4 %collective-permute-start.4 = (bf16[20,2,8,512]{3,2,1,0:T(8,128)(2,1)}, bf16[20,2,8,512]{3,2,1,0:T(8,128)(2,1)S(1)}, u32[]{:S(2)}, u32[]{:S(2)}) collective-permute-start(bf16[20,2,8,512]{3,2,1,0:T(8,128)(2,1)} %six.1), channel_id=1, source_target_pairs={{0,192},{16,336},{32,224},{48,368},{64,256},{80,400},{96,288},{112... | collective-permute-start | bytes 983048 | tf_op jit(solution)/shard_map/ppermute | solution.py:301
  48.1 14.6 %copy-start.1 = (bf16[256,1024]{1,0:T(8,128)(2,1)S(1)}, bf16[256,1024]{1,0:T(8,128)(2,1)}, u32[]{:S(2)}) copy-start(bf16[256,1024]{1,0:T(8,128)(2,1)} %weight_ref.1) | copy-start | bytes 1572868
  67.9 18.6 %all-to-all-start.2 = ((bf16[16,4,1024]{2,1,0:T(4,128)(2,1)}), bf16[16,4,1024]{2,1,0:T(4,128)(2,1)S(1)}, u32[]{:S(2)}, u32[]{:S(2)}) async-start(bf16[16,4,1024]{2,1,0:T(4,128)(2,1)} %pair.1.after_ref), calls=%async_computation.2 | async-start | bytes 262144 | tf_op jit(solution)/shard_map/all_to_all | solution.py:392
  80.5 6.8 %collective-permute-start.5 = (bf16[30,2,8,512]{3,2,1,0:T(8,128)(2,1)}, bf16[30,2,8,512]{3,2,1,0:T(8,128)(2,1)S(1)}, u32[]{:S(2)}, u32[]{:S(2)}) collective-permute-start(bf16[30,2,8,512]{3,2,1,0:T(8,128)(2,1)} %give.1), channel_id=1, source_target_pairs={{0,16},{16,0},{32,48},{48,32},{64,80},{80,64},{96,112},{112,96},{1... | collective-permute-start | bytes 1474568 | tf_op jit(solution)/shard_map/ppermute | solution.py:304
